TPU v7x, 32 devices: a whole 2x2x4 slice. The times are simulated.
32 devices in a mesh: dp: 16 (over z, y, x), mp: 2 (over core).
Axes of the slice: x: 2, y: 2, z: 4, core: 2. Of those that a mesh axis runs over, the one named last changes fastest.
Arguments:
- text_in: bfloat16 [16, 1024, 1024], P('dp'), may hold values from -6 to 6
- patch_in: bfloat16 [16, 256, 1024], P('dp'), may hold values from -6 to 6
- cot_text: bfloat16 [16, 1024, 1024], P('dp'), may hold values from -6 to 6
- cot_patch: bfloat16 [16, 256, 1024], P('dp'), may hold values from -6 to 6
- text_count: int32 [16], replicated, may hold values from 50 to 1024, as said below
- intersection: int32 [16, 4, 1024], P('dp'), may hold values from 0 to 196, as said below
- text_cell: int32 [16, 2, 1024], replicated, may hold values from 0 to 13
- wq: bfloat16 [1024, 1024], P('dp', 'mp'), may hold values from -0.1875 to 0.1875
- wk: bfloat16 [1024, 1024], P('dp', 'mp'), may hold values from -0.1875 to 0.1875
- wv: bfloat16 [1024, 1024], P('dp', 'mp'), may hold values from -0.1875 to 0.1875
- wo_t: bfloat16 [1024, 1024], P('dp', 'mp'), may hold values from -1.5 to 1.5
- gain_one: bfloat16 [1024], P('dp'), may hold values from 0.099609375 to 1.8984375
- w_gate: bfloat16 [1024, 2816], P('dp', 'mp'), may hold values from -0.1875 to 0.1875
- w_up: bfloat16 [1024, 2816], P('dp', 'mp'), may hold values from -0.1875 to 0.1875
- w_down_t: bfloat16 [1024, 2816], P('dp', 'mp'), may hold values from -0.21875 to 0.21875
- gain_two: bfloat16 [1024], P('dp'), may hold values from 0.099609375 to 1.8984375
- bias_table: bfloat16 [48, 16], P(None, 'mp'), may hold values from -4 to 4
Outputs:
- text_out: bfloat16 [16, 1024, 1024], P('dp')
- patch_out: bfloat16 [16, 256, 1024], P('dp')
- text_grad: bfloat16 [16, 1024, 1024], P('dp')
- patch_grad: bfloat16 [16, 256, 1024], P('dp')
- wq_grad: float32 [1024, 1024], P('dp', 'mp')
- wk_grad: float32 [1024, 1024], P('dp', 'mp')
- wv_grad: float32 [1024, 1024], P('dp', 'mp')
- wo_grad: float32 [1024, 1024], P('dp', 'mp')
- gain_one_grad: float32 [1024], P('dp')
- gate_grad: float32 [1024, 2816], P('dp', 'mp')
- up_grad: float32 [1024, 2816], P('dp', 'mp')
- down_grad: float32 [1024, 2816], P('dp', 'mp')
- gain_two_grad: float32 [1024], P('dp')
- table_grad: float32 [48, 16], P(None, 'mp')
Inputs may be any that keep to these rules, and one draw needn't show every extreme that they name: `text_count`: one page has exactly 1024 text tokens. `intersection`: patches in one grid row that a token's box covers, consecutive from the first entry; the first entry is always a patch, unused entries hold 196.
All inputs are finite; a program needn't handle non-finite values.
Results may differ from a plain program's by a relative error of at most 0.014.
Values may be sent and summed in bfloat16 or wider, within the bound.
No kernel may reach another device: no remote copies, remote signals or barrier semaphores. Data moves between devices by JAX's collectives and lax.ppermute only.
A program may use at most 256 MiB of HBM per device.

v0:
```python
import jax
import jax.numpy as jnp
from jax import lax
from jax.sharding import PartitionSpec as P

DH = 64
RB = 32
LQ = 4
GRID = 14
PSLOT = 256
TXT = 1024
QBLK = 512
PATCHES = 196
NB = 48


EPS = 1e-06
NEG_FILL = -1e30


def from_behind(block, axis, distance):
    devices = range(lax.axis_size(axis))
    route = [((i - distance) % len(devices), i) for i in devices]
    return lax.ppermute(block, axis, route)


def page_places(page_len, page_cells):
    text_ids = jnp.arange(TXT, dtype=jnp.int32)
    slot_ids = jnp.arange(PSLOT, dtype=jnp.int32)
    positions = jnp.concatenate([text_ids, page_len + slot_ids])
    row_coord = jnp.concatenate([page_cells[0], slot_ids // GRID])
    col_coord = jnp.concatenate([page_cells[1], slot_ids % GRID])
    live_keys = jnp.concatenate([text_ids < page_len, slot_ids < PATCHES])
    return (positions, row_coord, col_coord, live_keys)


def bucket_onehot(query_pos, query_row, query_col, key_places):
    rel_bucket = (
        jnp.clip(key_places[0][None, :] - query_pos[:, None], -(RB // 2), RB // 2 - 1) + RB // 2
    )
    row_gap = jnp.minimum(jnp.abs(key_places[1][None, :] - query_row[:, None]), LQ - 1)
    col_gap = jnp.minimum(jnp.abs(key_places[2][None, :] - query_col[:, None]), LQ - 1)
    lay_bucket = RB + row_gap * LQ + col_gap
    bucket_ids = jnp.arange(NB, dtype=jnp.int32)
    return ((rel_bucket[:, :, None] == bucket_ids) | (lay_bucket[:, :, None] == bucket_ids)).astype(
        jnp.bfloat16
    )


def block_scores(block_queries, query_pos, query_row, query_col, key_rows, key_places, table):
    onehot = bucket_onehot(query_pos, query_row, query_col, key_places)
    scores = jnp.einsum(
        "qhd,khd->hqk", block_queries, key_rows, preferred_element_type=jnp.float32
    ) * DH ** (-0.5)
    scores = scores + jnp.einsum("qkb,bh->hqk", onehot, table, preferred_element_type=jnp.float32)
    return (jnp.where(key_places[3][None, None, :], scores, NEG_FILL), onehot)


def split_blocks(queries, query_places, block_rows):
    block_count = queries.shape[0] // block_rows
    shaped = queries.reshape((block_count, block_rows) + queries.shape[1:])
    return (shaped, tuple((part.reshape(block_count, block_rows) for part in query_places)))


def attend(queries, query_places, key_rows, value_rows, key_places, table, block_rows):
    shaped, place_blocks = split_blocks(queries, query_places, block_rows)

    def one_block(inputs):
        block_queries, block_pos, block_row, block_col = inputs
        scores, onehot = block_scores(
            block_queries, block_pos, block_row, block_col, key_rows, key_places, table
        )
        row_max = jnp.max(scores, axis=-1, keepdims=True)
        exponent = jnp.exp(scores - row_max)
        row_total = jnp.sum(exponent, axis=-1, keepdims=True)
        weights_low = (exponent / row_total).astype(jnp.bfloat16)
        mixture = jnp.einsum(
            "hqk,khd->qhd", weights_low, value_rows, preferred_element_type=jnp.float32
        )
        return (mixture.astype(jnp.bfloat16), row_max + jnp.log(row_total))

    mixture, logsum = lax.map(one_block, (shaped,) + place_blocks)
    return (mixture.reshape(queries.shape), logsum)


def attend_back(
    queries, query_places, key_rows, value_rows, key_places, table, block_rows, logsum, grad_mixed
):
    shaped, place_blocks = split_blocks(queries, query_places, block_rows)
    grad_blocks = grad_mixed.reshape(shaped.shape)

    def one_step(carry, inputs):
        key_acc, value_acc, table_acc = carry
        block_queries, block_pos, block_row, block_col, block_logsum, block_grad = inputs
        scores, onehot = block_scores(
            block_queries, block_pos, block_row, block_col, key_rows, key_places, table
        )
        probs = jnp.exp(scores - block_logsum)
        grad_probs = jnp.einsum(
            "qhd,khd->hqk", block_grad, value_rows, preferred_element_type=jnp.float32
        )
        inner_sum = jnp.sum(probs * grad_probs, axis=-1, keepdims=True)
        grad_scores = (probs * (grad_probs - inner_sum)).astype(jnp.bfloat16)
        grad_query = jnp.einsum(
            "hqk,khd->qhd", grad_scores, key_rows, preferred_element_type=jnp.float32
        ) * DH ** (-0.5)
        key_acc = key_acc + jnp.einsum(
            "hqk,qhd->khd", grad_scores, block_queries, preferred_element_type=jnp.float32
        ) * DH ** (-0.5)
        value_acc = value_acc + jnp.einsum(
            "hqk,qhd->khd",
            probs.astype(jnp.bfloat16),
            block_grad,
            preferred_element_type=jnp.float32,
        )
        table_acc = table_acc + jnp.einsum(
            "hqk,qkb->bh", grad_scores, onehot, preferred_element_type=jnp.float32
        )
        return ((key_acc, value_acc, table_acc), grad_query)

    start_state = (
        jnp.zeros(key_rows.shape, jnp.float32),
        jnp.zeros(value_rows.shape, jnp.float32),
        jnp.zeros(table.shape, jnp.float32),
    )
    final_state, query_grad = lax.scan(
        one_step, start_state, (shaped,) + place_blocks + (logsum, grad_blocks)
    )
    return (query_grad.reshape(queries.shape), final_state[0], final_state[1], final_state[2])


def norm_rows(row_data):
    scale_inv = lax.rsqrt(jnp.mean(row_data * row_data, axis=-1, keepdims=True) + EPS)
    return (row_data * scale_inv, scale_inv)


def norm_back(grad_normed, unit_rows, scale_inv, gain):
    grad_unit = grad_normed * gain
    grad_gain = jnp.sum(grad_normed * unit_rows, axis=0)
    grad_rows = scale_inv * (
        grad_unit - unit_rows * jnp.mean(grad_unit * unit_rows, axis=-1, keepdims=True)
    )
    return (grad_rows, grad_gain)


def right_product(left, right):
    return lax.dot_general(
        left, right, (((1,), (1,)), ((), ())), preferred_element_type=jnp.float32
    )


def rows_product(left, right):
    return lax.dot_general(
        left, right, (((0,), (0,)), ((), ())), preferred_element_type=jnp.float32
    )


def body(
    text_in,
    patch_in,
    cot_text,
    cot_patch,
    text_count,
    intersection,
    text_cell,
    wq,
    wk,
    wv,
    wo_t,
    gain_one,
    w_gate,
    w_up,
    w_down_t,
    gain_two,
    bias_table,
):
    page_count = text_in.shape[0]
    model_width = text_in.shape[2]
    axis_span = lax.axis_size("dp")
    half_axis = axis_span // 2
    own_start = lax.axis_index("dp") * page_count
    own_counts = lax.dynamic_slice_in_dim(text_count, own_start, page_count, 0)
    own_cells = lax.dynamic_slice_in_dim(text_cell, own_start, page_count, 0)
    wq_full, wk_full, wv_full, wo_full, gate_full, up_full, down_full, gain_first, gain_second = (
        lax.all_gather(wq, "dp", axis=0, tiled=True),
        lax.all_gather(wk, "dp", axis=0, tiled=True),
        lax.all_gather(wv, "dp", axis=0, tiled=True),
        lax.all_gather(wo_t, "dp", axis=0, tiled=True),
        lax.all_gather(w_gate, "dp", axis=0, tiled=True),
        lax.all_gather(w_up, "dp", axis=0, tiled=True),
        lax.all_gather(w_down_t, "dp", axis=0, tiled=True),
        lax.all_gather(gain_one, "dp", axis=0, tiled=True),
        lax.all_gather(gain_two, "dp", axis=0, tiled=True),
    )
    gain_first = gain_first.astype(jnp.float32)
    gain_second = gain_second.astype(jnp.float32)
    local_heads = bias_table.shape[1]
    local_width = wq_full.shape[1]
    slot_ids = jnp.arange(PSLOT, dtype=jnp.int32)
    text_ids = jnp.arange(TXT, dtype=jnp.int32)
    covering = jnp.sum(
        (intersection[:, :, :, None] == slot_ids) & (slot_ids < PATCHES), axis=1
    ).astype(jnp.bfloat16)
    patch_rows, patch_cot = (patch_in, cot_patch)
    arriving = from_behind(patch_in, "dp", half_axis)
    embedded = text_in.astype(jnp.float32) + jnp.einsum(
        "gtp,gpd->gtd", covering, arriving, preferred_element_type=jnp.float32
    )
    text_total = page_count * TXT
    rows_all = jnp.concatenate(
        [
            embedded.reshape(text_total, model_width),
            patch_rows.reshape(-1, model_width).astype(jnp.float32),
        ],
        axis=0,
    )
    live_rows = jnp.concatenate(
        [
            (text_ids[None, :] < own_counts[:, None]).reshape(-1),
            jnp.tile(slot_ids < PATCHES, page_count),
        ]
    )
    unit_one, inv_one = norm_rows(rows_all)
    normed_one = (unit_one * gain_first).astype(jnp.bfloat16)
    query_all = jnp.dot(normed_one, wq_full, preferred_element_type=jnp.float32).astype(
        jnp.bfloat16
    )
    key_all = jnp.dot(normed_one, wk_full, preferred_element_type=jnp.float32).astype(jnp.bfloat16)
    value_all = jnp.dot(normed_one, wv_full, preferred_element_type=jnp.float32).astype(
        jnp.bfloat16
    )

    def text_part(array):
        return array[:text_total].reshape(page_count, TXT, local_heads, DH)

    def patch_part(array):
        return array[text_total:].reshape(page_count, PSLOT, local_heads, DH)

    query_text, key_text, value_text = (
        text_part(query_all),
        text_part(key_all),
        text_part(value_all),
    )
    query_patch, key_patch, value_patch = (
        patch_part(query_all),
        patch_part(key_all),
        patch_part(value_all),
    )
    key_for_patch, value_for_patch, key_for_text, value_for_text = from_behind(
        (key_text, value_text, key_patch, value_patch), "dp", half_axis
    )
    other_start = (lax.axis_index("dp") + half_axis) % axis_span * page_count
    patch_counts = lax.dynamic_slice_in_dim(text_count, other_start, page_count, 0)
    patch_cells = lax.dynamic_slice_in_dim(text_cell, other_start, page_count, 0)
    mix_text, mix_patch, lse_text, lse_patch = ([], [], [], [])
    page_index = 0
    text_places = page_places(own_counts[page_index], own_cells[page_index])
    patch_places = page_places(patch_counts[page_index], patch_cells[page_index])
    text_keys = jnp.concatenate([key_text[page_index], key_for_text[page_index]], axis=0)
    text_values = jnp.concatenate([value_text[page_index], value_for_text[page_index]], axis=0)
    patch_keys = jnp.concatenate([key_for_patch[page_index], key_patch[page_index]], axis=0)
    patch_values = jnp.concatenate([value_for_patch[page_index], value_patch[page_index]], axis=0)
    text_query_places = tuple((part[:TXT] for part in text_places[:3]))
    patch_query_places = tuple((part[TXT:] for part in patch_places[:3]))
    page_inputs = [
        (
            text_places,
            patch_places,
            text_keys,
            text_values,
            patch_keys,
            patch_values,
            text_query_places,
            patch_query_places,
        )
    ]
    mixed_one, logsum_one = attend(
        query_text[page_index],
        text_query_places,
        text_keys,
        text_values,
        text_places,
        bias_table,
        QBLK,
    )
    mixed_two, logsum_two = attend(
        query_patch[page_index],
        patch_query_places,
        patch_keys,
        patch_values,
        patch_places,
        bias_table,
        PSLOT,
    )
    mix_text.append(mixed_one)
    mix_patch.append(mixed_two)
    lse_text.append(logsum_one)
    lse_patch.append(logsum_two)
    mixture_all = jnp.concatenate(
        [
            jnp.stack(mix_text).reshape(text_total, local_width),
            jnp.stack(mix_patch).reshape(-1, local_width),
        ],
        axis=0,
    )
    attention = lax.psum(right_product(mixture_all, wo_full), "mp")
    hidden_rows = rows_all + attention
    unit_two, inv_two = norm_rows(hidden_rows)
    normed_two = (unit_two * gain_second).astype(jnp.bfloat16)
    gate_act = jnp.dot(normed_two, gate_full, preferred_element_type=jnp.float32).astype(
        jnp.bfloat16
    )
    up_act = jnp.dot(normed_two, up_full, preferred_element_type=jnp.float32).astype(jnp.bfloat16)
    up_value = up_act.astype(jnp.float32)
    gelu_value, gelu_pull = jax.vjp(
        lambda value_in: jax.nn.gelu(value_in, approximate=True), gate_act.astype(jnp.float32)
    )
    activated = (gelu_value * up_value).astype(jnp.bfloat16)
    ffn_sum = lax.psum(right_product(activated, down_full).astype(jnp.bfloat16), "mp").astype(
        jnp.float32
    )
    result = jnp.where(live_rows[:, None], hidden_rows + ffn_sum, 0.0).astype(jnp.bfloat16)
    cot_all = jnp.concatenate(
        [cot_text.reshape(text_total, model_width), patch_cot.reshape(-1, model_width)], axis=0
    )
    grad_out = jnp.where(live_rows[:, None], cot_all.astype(jnp.float32), 0.0)
    grad_ffn = grad_out.astype(jnp.bfloat16)
    grad_act = jnp.dot(grad_ffn, down_full, preferred_element_type=jnp.float32)
    down_grad = rows_product(grad_ffn, activated)
    grad_gate = gelu_pull(grad_act * up_value)[0].astype(jnp.bfloat16)
    grad_up = (grad_act * gelu_value).astype(jnp.bfloat16)
    gate_grad = rows_product(normed_two, grad_gate)
    up_grad = rows_product(normed_two, grad_up)
    normed_grad_two = lax.psum(
        right_product(grad_gate, gate_full) + right_product(grad_up, up_full), "mp"
    )
    hidden_norm_grad, gain_two_grad = norm_back(normed_grad_two, unit_two, inv_two, gain_second)
    hidden_grad = grad_out + hidden_norm_grad
    grad_attn = hidden_grad.astype(jnp.bfloat16)
    wo_grad = rows_product(grad_attn, mixture_all)
    grad_mix = jnp.dot(grad_attn, wo_full, preferred_element_type=jnp.float32).astype(jnp.bfloat16)
    grad_mix_text = text_part(grad_mix)
    grad_mix_patch = patch_part(grad_mix)
    query_grads_text, query_grads_patch = ([], [])
    key_tt, key_tp, key_pt, key_pp = ([], [], [], [])
    value_tt, value_tp, value_pt, value_pp = ([], [], [], [])
    page_index = 0
    (
        text_places,
        patch_places,
        text_keys,
        text_values,
        patch_keys,
        patch_values,
        text_query_places,
        patch_query_places,
    ) = page_inputs[page_index]
    grad_q_one, grad_k_one, grad_v_one, grad_t_one = attend_back(
        query_text[page_index],
        text_query_places,
        text_keys,
        text_values,
        text_places,
        bias_table,
        QBLK,
        lse_text[page_index],
        grad_mix_text[page_index],
    )
    grad_q_two, grad_k_two, grad_v_two, grad_t_two = attend_back(
        query_patch[page_index],
        patch_query_places,
        patch_keys,
        patch_values,
        patch_places,
        bias_table,
        PSLOT,
        lse_patch[page_index],
        grad_mix_patch[page_index],
    )
    query_grads_text.append(grad_q_one)
    query_grads_patch.append(grad_q_two)
    key_tt.append(grad_k_one[:TXT])
    key_tp.append(grad_k_one[TXT:])
    key_pt.append(grad_k_two[:TXT])
    key_pp.append(grad_k_two[TXT:])
    value_tt.append(grad_v_one[:TXT])
    value_tp.append(grad_v_one[TXT:])
    value_pt.append(grad_v_two[:TXT])
    value_pp.append(grad_v_two[TXT:])
    table_grad = grad_t_one + grad_t_two
    back_key_text, back_value_text, back_key_patch, back_value_patch = from_behind(
        (jnp.stack(key_pt), jnp.stack(value_pt), jnp.stack(key_tp), jnp.stack(value_tp)),
        "dp",
        half_axis,
    )
    key_text_grad = jnp.stack(key_tt) + back_key_text
    value_text_grad = jnp.stack(value_tt) + back_value_text
    key_patch_grad = jnp.stack(key_pp) + back_key_patch
    value_patch_grad = jnp.stack(value_pp) + back_value_patch

    def join_rows(text_side, patch_side):
        return jnp.concatenate(
            [text_side.reshape(text_total, local_width), patch_side.reshape(-1, local_width)],
            axis=0,
        ).astype(jnp.bfloat16)

    grad_query = join_rows(jnp.stack(query_grads_text), jnp.stack(query_grads_patch))
    grad_key = join_rows(key_text_grad, key_patch_grad)
    grad_value = join_rows(value_text_grad, value_patch_grad)
    wq_grad = rows_product(normed_one, grad_query)
    wk_grad = rows_product(normed_one, grad_key)
    wv_grad = rows_product(normed_one, grad_value)
    normed_grad_part = (
        right_product(grad_query, wq_full)
        + right_product(grad_key, wk_full)
        + right_product(grad_value, wv_full)
    )
    normed_grad_one = lax.psum(normed_grad_part, "mp")
    rows_norm_grad, gain_one_grad = norm_back(normed_grad_one, unit_one, inv_one, gain_first)
    rows_grad = hidden_grad + rows_norm_grad
    text_rows_grad = rows_grad[:text_total].reshape(page_count, TXT, model_width)
    patch_side_grad = rows_grad[text_total:].reshape(page_count, PSLOT, model_width)
    intersection_grad = jnp.einsum(
        "gtp,gtd->gpd",
        covering.astype(jnp.float32),
        text_rows_grad,
        precision=lax.Precision.HIGHEST,
        preferred_element_type=jnp.float32,
    )
    patch_result = result[text_total:].reshape(page_count, PSLOT, model_width)
    incoming = from_behind(intersection_grad, "dp", half_axis)
    patch_grad = (patch_side_grad + incoming).astype(jnp.bfloat16)
    wq_sum, wk_sum, wv_sum, wo_sum, gate_sum, up_sum, down_sum, gain_one_sum, gain_two_sum = (
        lax.psum_scatter(wq_grad, "dp", scatter_dimension=0, tiled=True),
        lax.psum_scatter(wk_grad, "dp", scatter_dimension=0, tiled=True),
        lax.psum_scatter(wv_grad, "dp", scatter_dimension=0, tiled=True),
        lax.psum_scatter(wo_grad, "dp", scatter_dimension=0, tiled=True),
        lax.psum_scatter(gate_grad, "dp", scatter_dimension=0, tiled=True),
        lax.psum_scatter(up_grad, "dp", scatter_dimension=0, tiled=True),
        lax.psum_scatter(down_grad, "dp", scatter_dimension=0, tiled=True),
        lax.psum_scatter(gain_one_grad, "dp", scatter_dimension=0, tiled=True),
        lax.psum_scatter(gain_two_grad, "dp", scatter_dimension=0, tiled=True),
    )
    table_sum = lax.psum(table_grad, "dp")
    text_out = result[:text_total].reshape(page_count, TXT, model_width)
    return (
        text_out,
        patch_result,
        text_rows_grad.astype(jnp.bfloat16),
        patch_grad,
        wq_sum,
        wk_sum,
        wv_sum,
        wo_sum,
        gain_one_sum,
        gate_sum,
        up_sum,
        down_sum,
        gain_two_sum,
        table_sum,
    )


def solution(mesh):
    placed = (
        P("dp", None, None),
        P("dp", None, None),
        P("dp", None, None),
        P("dp", None, None),
        P(),
        P("dp", None, None),
        P(),
        P("dp", "mp"),
        P("dp", "mp"),
        P("dp", "mp"),
        P("dp", "mp"),
        P("dp"),
        P("dp", "mp"),
        P("dp", "mp"),
        P("dp", "mp"),
        P("dp"),
        P(None, "mp"),
    )
    return jax.shard_map(
        body,
        mesh=mesh,
        in_specs=placed,
        out_specs=(
            P("dp", None, None),
            P("dp", None, None),
            P("dp", None, None),
            P("dp", None, None),
            P("dp", "mp"),
            P("dp", "mp"),
            P("dp", "mp"),
            P("dp", "mp"),
            P("dp"),
            P("dp", "mp"),
            P("dp", "mp"),
            P("dp", "mp"),
            P("dp"),
            P(None, "mp"),
        ),
        check_vma=False,
    )
```

profile of v0, /device:TPU:0, one launch (start us, length us, event | category | flops | bytes accessed | tf_op | source)
XLA Modules:
  0.0 2059.4 jit_solution(498228249935219588)
XLA Ops:
  23.3 40.8 %all-reduce.5 = (bf16[1024]{0:T(1024)(128)(2,1)S(1)}, bf16[1024]{0:T(1024)(128)(2,1)}) all-reduce(bf16[1024]{0:T(1024)(128)(2,1)S(1)} %dynamic-update-slice, bf16[1024]{0:T(1024)(128)(2,1)S(1)} %dynamic-update-slice.1), channel_id=1, replica_groups=mesh['dp'=16,'mp'=2] {'dp'}, use_global_device_ids=true, to_apply=%add | all-reduce | flops 2048 | bytes 8192
  103.6 29.5 %all-gather.12.cloned.1.call-done = bf16[1024,512]{1,0:T(8,128)(2,1)} async-done(((bf16[64,512]{1,0:T(8,128)(2,1)}), bf16[1024,512]{1,0:T(8,128)(2,1)}) %all-gather.12.cloned.1.call-update) | async-done | bytes 1048592 | tf_op jit(solution)/shard_map/all_gather | solution.py:187
  137.9 53.9 %all-gather.8.cloned.1.call-done = bf16[1024,512]{1,0:T(8,128)(2,1)} async-done(((bf16[64,512]{1,0:T(8,128)(2,1)}), bf16[1024,512]{1,0:T(8,128)(2,1)}) %all-gather.8.cloned.1.call-update) | async-done | bytes 1048592 | tf_op jit(solution)/shard_map/all_gather | solution.py:185
  202.4 52.7 %collective-permute-done.2 = bf16[1,256,8,64]{1,3,2,0:T(8,128)(2,1)S(1)} collective-permute-done((bf16[1,256,8,64]{1,3,2,0:T(8,128)(2,1)S(1)}, bf16[1,256,8,64]{1,3,2,0:T(8,128)(2,1)S(1)}, u32[]{:S(2)}, u32[]{:S(2)}) %collective-permute-start.2) | collective-permute-done | bytes 262176 | tf_op jit(solution)/shard_map/ppermute | solution.py:24
  257.3 135.7 %while.5 = (s32[]{:T(128)}, bf16[2,512,8,64]{1,3,2,0:T(8,128)(2,1)}, f32[2,8,512,1]{2,1,3,0:T(8,128)S(1)}, pred[1280]{0:T(1024)(128)(4,1)S(1)}, bf16[2,512,8,64]...) while((s32[]{:T(128)}, ...), condition=%wide.region_5.6_spmd, body=%wide.region_2.5_spmd.sunk | while | flops 1995173888 | bytes 123376064 | solution.py:82
  259.4 24.9 %fusion.234 = f32[512,1280,8]{1,2,0:T(8,128)} fusion(s32[512,1280]{1,0:T(8,128)S(1)} %get-tuple-element.770, s32[512,1280]{1,0:T(8,128)S(1)} %get-tuple-element.771, bf16[48,8]{0,1:T(8,128)(2,1)S(1)} %get-tuple-element.838), kind=kOutput, calls=%fused_computation.3.clone.1 | convolution fusion | flops 597688320 | bytes 26215168 | tf_op jit(solution)/shard_map/while/body/eval_jaxpr/qkb,bh->hqk/dot_general | solution.py:55
  327.1 24.9 %fusion.234 = f32[512,1280,8]{1,2,0:T(8,128)} fusion(s32[512,1280]{1,0:T(8,128)S(1)} %get-tuple-element.770, s32[512,1280]{1,0:T(8,128)S(1)} %get-tuple-element.771, bf16[48,8]{0,1:T(8,128)(2,1)S(1)} %get-tuple-element.838), kind=kOutput, calls=%fused_computation.3.clone.1 | convolution fusion | flops 597688320 | bytes 26215168 | tf_op jit(solution)/shard_map/while/body/eval_jaxpr/qkb,bh->hqk/dot_general | solution.py:55
  418.3 26.9 %all-reduce.11.cloned.1.call-done = f32[1280,1024]{1,0:T(8,128)} async-done(((f32[1280,1024]{1,0:T(8,128)}), f32[1280,1024]{1,0:T(8,128)}) %all-reduce.11.cloned.1.call-update) | async-done | bytes 5242896 | tf_op jit(solution)/shard_map/psum | solution.py:306
  454.2 61.1 %all-gather.18.cloned.1.call-done = bf16[1024,1408]{1,0:T(8,128)(2,1)} async-done(((bf16[64,1408]{1,0:T(8,128)(2,1)}), bf16[1024,1408]{1,0:T(8,128)(2,1)}) %all-gather.18.cloned.1.call-update) | async-done | bytes 2883600 | tf_op jit(solution)/shard_map/all_gather | solution.py:190
  524.0 59.3 %all-gather.16.cloned.1.call-done = bf16[1024,1408]{1,0:T(8,128)(2,1)} async-done(((bf16[64,1408]{1,0:T(8,128)(2,1)}), bf16[1024,1408]{1,0:T(8,128)(2,1)}) %all-gather.16.cloned.1.call-update) | async-done | bytes 2883600 | tf_op jit(solution)/shard_map/all_gather | solution.py:189
  592.0 59.4 %all-gather.20.cloned.1.call-done = bf16[1024,1408]{1,0:T(8,128)(2,1)} async-done(((bf16[64,1408]{1,0:T(8,128)(2,1)}), bf16[1024,1408]{1,0:T(8,128)(2,1)}) %all-gather.20.cloned.1.call-update) | async-done | bytes 2883600 | tf_op jit(solution)/shard_map/all_gather | solution.py:191
  759.7 303.1 %while.6 = (s32[]{:T(128)}, f32[1280,8,64]{0,2,1:T(8,128)}, f32[1280,8,64]{0,2,1:T(8,128)}, f32[48,8]{0,1:T(8,128)S(1)}, bf16[2,512,8,64]{1,3,2,0:T(8,128)(2,1)}...) while((s32[]{:T(128)}, f32[1280,8,64]{0,2,1:T(8,128)}, ...), condition=%wide.region_15.16_spmd.clone, body=%wide.region_13.15_spmd.clone.sunk | while | flops 4614648832 | bytes 387844160 | solution.py:126
  763.7 24.8 %fusion.252 = f32[512,1280,8]{0,2,1:T(8,128)} fusion(s32[512,1280]{0,1:T(8,128)S(1)} %minimum_add_fusion.6, s32[512,1280]{0,1:T(8,128)S(1)} %clamp_add_fusion.4, bf16[48,8]{0,1:T(8,128)(2,1)S(1)} %get-tuple-element.895), kind=kOutput, calls=%fused_computation.29.clone.1 | convolution fusion | flops 597688320 | bytes 26215168 | tf_op jit(solution)/shard_map/while/body/eval_jaxpr/qkb,bh->hqk/dot_general | solution.py:55
  788.4 23.6 %copy.80 = f32[512,1280,8]{1,0,2:T(8,128)} copy(f32[512,1280,8]{0,2,1:T(8,128)} %fusion.252) | data formatting | bytes 41943040 | tf_op jit(solution)/shard_map/while/body/eval_jaxpr/qkb,bh->hqk/dot_general | solution.py:55
  863.8 26.5 %fusion.255 = f32[48,8]{0,1:T(8,128)S(1)} fusion(bf16[8,512,1280]{1,0,2:T(8,128)(2,1)} %copy.81, s32[512,1280]{0,1:T(8,128)} %copy-done.13, s32[512,1280]{0,1:T(8,128)} %copy-done.14, f32[48,8]{0,1:T(8,128)S(1)} %get-tuple-element.864, pred[]{:T(512)S(6)} %compare.4), kind=kOutput, calls=%fused_computation.53.clone.1 | convolution fusion | flops 597689088 | bytes 15731713 | tf_op jit(solution)/shard_map/while/body/eval_jaxpr/hqk,qkb->bh/dot_general | solution.py:116
  913.7 24.8 %fusion.252 = f32[512,1280,8]{0,2,1:T(8,128)} fusion(s32[512,1280]{0,1:T(8,128)S(1)} %minimum_add_fusion.6, s32[512,1280]{0,1:T(8,128)S(1)} %clamp_add_fusion.4, bf16[48,8]{0,1:T(8,128)(2,1)S(1)} %get-tuple-element.895), kind=kOutput, calls=%fused_computation.29.clone.1 | convolution fusion | flops 597688320 | bytes 26215168 | tf_op jit(solution)/shard_map/while/body/eval_jaxpr/qkb,bh->hqk/dot_general | solution.py:55
  1013.9 26.5 %fusion.255 = f32[48,8]{0,1:T(8,128)S(1)} fusion(bf16[8,512,1280]{1,0,2:T(8,128)(2,1)} %copy.81, s32[512,1280]{0,1:T(8,128)} %copy-done.13, s32[512,1280]{0,1:T(8,128)} %copy-done.14, f32[48,8]{0,1:T(8,128)S(1)} %get-tuple-element.864, pred[]{:T(512)S(6)} %compare.4), kind=kOutput, calls=%fused_computation.53.clone.1 | convolution fusion | flops 597689088 | bytes 15731713 | tf_op jit(solution)/shard_map/while/body/eval_jaxpr/hqk,qkb->bh/dot_general | solution.py:116
  1089.2 193.4 %collective-permute-done.8 = f32[1,256,8,64]{1,3,2,0:T(8,128)S(1)} collective-permute-done((f32[1,256,8,64]{1,3,2,0:T(8,128)S(1)}, f32[1,256,8,64]{1,3,2,0:T(8,128)S(1)}, u32[]{:S(2)}, u32[]{:S(2)}) %collective-permute-start.8) | collective-permute-done | bytes 524320 | tf_op jit(solution)/shard_map/ppermute | solution.py:24
  1390.6 95.5 %all-reduce.4 = (f32[1024]{0:T(1024)S(1)}, f32[1024]{0:T(1024)S(1)}, f32[48,8]{0,1:T(8,128)}) all-reduce(f32[1024]{0:T(1024)S(1)} %get-tuple-element.471, f32[1024]{0:T(1024)S(1)} %copy-done.56, f32[48,8]{0,1:T(8,128)S(1)} %add.298), channel_id=6, replica_groups=mesh['dp'=16,'mp'=2] {'dp'}, use_global_device_ids=true, to_apply=%region_24.25.clone | all-reduce | flops 2432 | bytes 19456
  1506.3 80.2 %reduce-scatter.12.cloned.1.call-done = f32[64,512]{1,0:T(8,128)} async-done(((f32[1024,512]{1,0:T(8,128)}), f32[64,512]{1,0:T(8,128)}) %reduce-scatter.12.cloned.1.call-update) | async-done | bytes 131088 | tf_op jit(solution)/shard_map/reduce_scatter | solution.py:436
  1586.5 80.6 %reduce-scatter.10.cloned.1.call-done = f32[64,512]{1,0:T(8,128)} async-done(((f32[1024,512]{1,0:T(8,128)}), f32[64,512]{1,0:T(8,128)}) %reduce-scatter.10.cloned.1.call-update) | async-done | bytes 131088 | tf_op jit(solution)/shard_map/reduce_scatter | solution.py:435
  1667.0 125.8 %reduce-scatter.16.cloned.1.call-done = f32[64,1408]{1,0:T(8,128)} async-done(((f32[1024,1408]{1,0:T(8,128)}), f32[64,1408]{1,0:T(8,128)}) %reduce-scatter.16.cloned.1.call-update) | async-done | bytes 360464 | tf_op jit(solution)/shard_map/reduce_scatter | solution.py:438
  1792.8 129.8 %reduce-scatter.18.cloned.1.call-done = f32[64,1408]{1,0:T(8,128)} async-done(((f32[1024,1408]{1,0:T(8,128)}), f32[64,1408]{1,0:T(8,128)}) %reduce-scatter.18.cloned.1.call-update) | async-done | bytes 360464 | tf_op jit(solution)/shard_map/reduce_scatter | solution.py:439
  1922.6 129.7 %reduce-scatter.20.cloned.1.call-done = f32[64,1408]{1,0:T(8,128)} async-done(((f32[1024,1408]{1,0:T(8,128)}), f32[64,1408]{1,0:T(8,128)}) %reduce-scatter.20.cloned.1.call-update) | async-done | bytes 360464 | tf_op jit(solution)/shard_map/reduce_scatter | solution.py:440
  (401 shorter events, 646.4 us)
Async XLA Ops:
  7.2 91.7 %all-gather.10.cloned.1.call-start = ((), (), s32[]{:S(2)}) async-start(), calls=%async_computation.8 | async-start | bytes 1114112 | tf_op jit(solution)/shard_map/all_gather | solution.py:186
  7.9 125.2 %all-gather.12.cloned.1.call-start = ((), (), s32[]{:S(2)}) async-start(), calls=%async_computation.9 | async-start | bytes 1114112 | tf_op jit(solution)/shard_map/all_gather | solution.py:187
  8.7 183.1 %all-gather.8.cloned.1.call-start = ((), (), s32[]{:S(2)}) async-start(), calls=%async_computation.7 | async-start | bytes 1114112 | tf_op jit(solution)/shard_map/all_gather | solution.py:185
  9.4 401.2 %all-gather.14.cloned.1.call-start = ((), (), s32[]{:S(2)}) async-start(), calls=%async_computation.10 | async-start | bytes 1114112 | tf_op jit(solution)/shard_map/all_gather | solution.py:188
  13.6 431.6 %all-reduce.11.cloned.1.call-start = ((), (), s32[]{:S(2)}) async-start(), calls=%async_computation.11 | async-start | bytes 10485760 | tf_op jit(solution)/shard_map/psum | solution.py:306
  198.2 198.5 %collective-permute-start.4 = (bf16[1,1024,8,64]{1,3,2,0:T(8,128)(2,1)}, bf16[1,1024,8,64]{1,3,2,0:T(8,128)(2,1)}, u32[]{:S(2)}, u32[]{:S(2)}) collective-permute-start(bf16[1,1024,8,64]{1,3,2,0:T(8,128)(2,1)} %bitcast.29), channel_id=1, source_target_pairs={{16,0},{18,2},{20,4},{22,6},{24,8},{26,10},{28,12},{30,14},{0,16},... | collective-permute-start | bytes 3145736 | tf_op jit(solution)/shard_map/ppermute | solution.py:24
  200.4 204.3 %collective-permute-start.3 = (bf16[1,1024,8,64]{1,3,2,0:T(8,128)(2,1)}, bf16[1,1024,8,64]{1,3,2,0:T(8,128)(2,1)}, u32[]{:S(2)}, u32[]{:S(2)}) collective-permute-start(bf16[1,1024,8,64]{1,3,2,0:T(8,128)(2,1)} %bitcast.24), channel_id=1, source_target_pairs={{16,0},{18,2},{20,4},{22,6},{24,8},{26,10},{28,12},{30,14},{0,16},... | collective-permute-start | bytes 3145736 | tf_op jit(solution)/shard_map/ppermute | solution.py:24
  416.1 99.1 %all-gather.18.cloned.1.call-start = ((), (), s32[]{:S(2)}) async-start(), calls=%async_computation.13 | async-start | bytes 3063808 | tf_op jit(solution)/shard_map/all_gather | solution.py:190
  416.7 166.6 %all-gather.16.cloned.1.call-start = ((), (), s32[]{:S(2)}) async-start(), calls=%async_computation.12 | async-start | bytes 3063808 | tf_op jit(solution)/shard_map/all_gather | solution.py:189
  417.5 234.0 %all-gather.20.cloned.1.call-start = ((), (), s32[]{:S(2)}) async-start(), calls=%async_computation.14 | async-start | bytes 3063808 | tf_op jit(solution)/shard_map/all_gather | solution.py:191
  418.2 286.5 %all-reduce.15.cloned.1.call-start = ((), (), s32[]{:S(2)}) async-start(), calls=%async_computation.16 | async-start | bytes 10485760 | tf_op jit(solution)/shard_map/psum | solution.py:334
  686.6 675.5 %all-reduce.17.cloned.1.call-start = ((), (), s32[]{:S(2)}) async-start(), calls=%async_computation.17 | async-start | bytes 10485760 | tf_op jit(solution)/shard_map/psum | solution.py:418
  1064.6 228.7 %collective-permute-start.7 = (f32[1,1024,8,64]{1,3,2,0:T(8,128)S(1)}, f32[1,1024,8,64]{1,3,2,0:T(8,128)S(1)}, u32[]{:S(2)}, u32[]{:S(2)}) collective-permute-start(f32[1,1024,8,64]{1,3,2,0:T(8,128)S(1)} %slice_bitcast_fusion), channel_id=1, source_target_pairs={{16,0},{18,2},{20,4},{22,6},{24,8},{26,10},{28,12},{30,14},{0,16},... | collective-permute-start | bytes 6291464 | tf_op jit(solution)/shard_map/ppermute | solution.py:24
  1076.8 216.9 %collective-permute-start.5 = (f32[1,1024,8,64]{1,3,2,0:T(8,128)S(1)}, f32[1,1024,8,64]{1,3,2,0:T(8,128)S(1)}, u32[]{:S(2)}, u32[]{:S(2)}) collective-permute-start(f32[1,1024,8,64]{1,3,2,0:T(8,128)S(1)} %slice_bitcast_fusion.1), channel_id=1, source_target_pairs={{16,0},{18,2},{20,4},{22,6},{24,8},{26,10},{28,12},{30,14},{0,16},... | collective-permute-start | bytes 6291464 | tf_op jit(solution)/shard_map/ppermute | solution.py:24
  1079.1 203.5 %collective-permute-start.8 = (f32[1,256,8,64]{1,3,2,0:T(8,128)S(1)}, f32[1,256,8,64]{1,3,2,0:T(8,128)S(1)}, u32[]{:S(2)}, u32[]{:S(2)}) collective-permute-start(f32[1,256,8,64]{1,3,2,0:T(8,128)S(1)} %slice_bitcast_fusion.7), channel_id=1, source_target_pairs={{16,0},{18,2},{20,4},{22,6},{24,8},{26,10},{28,12},{30,14},{0,16},... | collective-permute-start | bytes 1572872 | tf_op jit(solution)/shard_map/ppermute | solution.py:24
  1084.1 209.1 %collective-permute-start.6 = (f32[1,256,8,64]{1,3,2,0:T(8,128)S(1)}, f32[1,256,8,64]{1,3,2,0:T(8,128)S(1)}, u32[]{:S(2)}, u32[]{:S(2)}) collective-permute-start(f32[1,256,8,64]{1,3,2,0:T(8,128)S(1)} %slice_bitcast_fusion.8), channel_id=1, source_target_pairs={{16,0},{18,2},{20,4},{22,6},{24,8},{26,10},{28,12},{30,14},{0,16},... | collective-permute-start | bytes 1572872 | tf_op jit(solution)/shard_map/ppermute | solution.py:24
  1301.3 192.0 %reduce-scatter.14.cloned.1.call-start = ((), (), s32[]{:S(2)}) async-start(), calls=%async_computation.21 | async-start | bytes 2228224 | tf_op jit(solution)/shard_map/reduce_scatter | solution.py:437
  1308.0 198.3 %reduce-scatter.8.cloned.1.call-start = ((), (), s32[]{:S(2)}) async-start(), calls=%async_computation.18 | async-start | bytes 2228224 | tf_op jit(solution)/shard_map/reduce_scatter | solution.py:434
  1313.4 273.1 %reduce-scatter.12.cloned.1.call-start = ((), (), s32[]{:S(2)}) async-start(), calls=%async_computation.20 | async-start | bytes 2228224 | tf_op jit(solution)/shard_map/reduce_scatter | solution.py:436
  1318.3 348.8 %reduce-scatter.10.cloned.1.call-start = ((), (), s32[]{:S(2)}) async-start(), calls=%async_computation.19 | async-start | bytes 2228224 | tf_op jit(solution)/shard_map/reduce_scatter | solution.py:435
  1323.4 469.4 %reduce-scatter.16.cloned.1.call-start = ((), (), s32[]{:S(2)}) async-start(), calls=%async_computation.22 | async-start | bytes 6127616 | tf_op jit(solution)/shard_map/reduce_scatter | solution.py:438
  1332.2 590.4 %reduce-scatter.18.cloned.1.call-start = ((), (), s32[]{:S(2)}) async-start(), calls=%async_computation.23 | async-start | bytes 6127616 | tf_op jit(solution)/shard_map/reduce_scatter | solution.py:439
  1340.4 711.9 %reduce-scatter.20.cloned.1.call-start = ((), (), s32[]{:S(2)}) async-start(), calls=%async_computation.24 | async-start | bytes 6127616 | tf_op jit(solution)/shard_map/reduce_scatter | solution.py:440
  1374.9 116.3 %collective-permute-start.9 = (f32[1,256,1024]{2,1,0:T(8,128)S(1)}, f32[1,256,1024]{2,1,0:T(8,128)S(1)}, u32[]{:S(2)}, u32[]{:S(2)}) collective-permute-start(f32[1,256,1024]{2,1,0:T(8,128)S(1)} %fusion.97), channel_id=1, source_target_pairs={{16,0},{18,2},{20,4},{22,6},{24,8},{26,10},{28,12},{30,14},{0,16},... | collective-permute-start | bytes 3145736 | tf_op jit(solution)/shard_map/ppermute | solution.py:24
  (95 other events, 1447.4 us)
Sparse Core Ops, SparseCore 0:
  10.8 65.4 all-gather.9
  79.0 54.0 all-gather.11
  135.9 55.8 all-gather.7
  194.4 125.9 all-gather.13
  416.3 28.8 all-reduce.10
  448.1 67.0 all-gather.17
  518.4 64.9 all-gather.15
  586.5 64.9 all-gather.19
  675.5 29.1 all-reduce.14
  706.9 23.3 all-reduce.12
  1301.5 31.2 all-reduce.16
  1335.5 85.5 reduce-scatter.13
  1423.9 82.3 reduce-scatter.7
  1509.0 77.4 reduce-scatter.11
  1589.2 77.8 reduce-scatter.9
  1669.8 122.9 reduce-scatter.15
  1795.5 126.9 reduce-scatter.17
  1925.3 126.9 reduce-scatter.19
where the time goes:
time: 2070 us; the launch traced here: 2060 us
  waiting for transfers between devices  1150 us (56%)
  matrix products  477 us (23%)
  local copies, waits for them, and re-layouts  155 us (7%)
  blocking collectives  136 us (7%)
  other arithmetic  110 us (5%)
    ppermute x10, waiting for transfers between devices, from_behind(): return lax.ppermute(block, axis, route)  256 us
    unnamed x2, blocking collectives  136 us
    reduce_scatter x1, waiting for transfers between devices, body(): lax.psum_scatter(up_grad, 'dp', scatter_dimension=0, tiled=True)  130 us
    reduce_scatter x1, waiting for transfers between devices, body(): lax.psum_scatter(down_grad, 'dp', scatter_dimension=0, tiled=True)  130 us
    reduce_scatter x1, waiting for transfers between devices, body(): lax.psum_scatter(gate_grad, 'dp', scatter_dimension=0, tiled=True)  126 us
    dot_general x5, matrix products, block_scores(): jnp.einsum('qkb,bh->hqk', onehot, table, preferred_element_type=jnp.float32)  113 us
    dot_general x5, matrix products, block_scores(): jnp.einsum('qhd,khd->hqk', block_queries, key_rows, preferred_element_typ...  83.6 us
    reduce_scatter x1, waiting for transfers between devices, body(): lax.psum_scatter(wk_grad, 'dp', scatter_dimension=0, tiled=True)  80.6 us
  transfers between devices with their start and end apart: 28, of which 17 were waited for; matrix products, arithmetic and copies ran while one was open for 17% of the time, Pallas kernels for 0%

commit v1 on v0

v1 whole, which is shorter than its diff:
```python
import functools

import jax
import jax.numpy as jnp
from jax import lax
from jax.experimental import pallas as pl
from jax.experimental.pallas import tpu as pltpu
from jax.sharding import PartitionSpec as P

DH = 64
RB = 32
LQ = 4
GRID = 14
PATCHES = 196
EPS = 1e-06

BQ = 256
PAD = 128
WIN = BQ + 2 * PAD
CELLS = 256
TILE0 = PATCHES
DEAD = 206
QROW0 = PATCHES
FEAT_ROWS = 208
MASKED = -1e30
VMEM = 60 * 1024 * 1024
F32 = jnp.float32
BF16 = jnp.bfloat16


def nt(left, right):
    return lax.dot_general(left, right, (((1,), (1,)), ((), ())), preferred_element_type=F32)


def nn(left, right):
    return lax.dot_general(left, right, (((1,), (0,)), ((), ())), preferred_element_type=F32)


def tn(left, right):
    return lax.dot_general(left, right, (((0,), (0,)), ((), ())), preferred_element_type=F32)


def params(**more):
    return pltpu.CompilerParams(vmem_limit_bytes=VMEM, **more)


def grid_of(devices):
    side = max(1, round((devices / 4) ** 0.5))
    return (devices // (side * side), side, side)


class Chips:
    def __init__(self):
        self.count = lax.axis_size("dp")
        self.sizes = grid_of(self.count)
        self.strides = (self.sizes[1] * self.sizes[2], self.sizes[2], 1)
        me = lax.axis_index("dp")
        self.coords = tuple((me // s) % m for s, m in zip(self.strides, self.sizes))

    def send(self, block, axis, distance):
        size, stride = self.sizes[axis], self.strides[axis]
        route = []
        for i in range(self.count):
            c = (i // stride) % size
            route.append((i, i + ((c + distance) % size - c) * stride))
        return lax.ppermute(block, "dp", route)

    def scatter_axis(self, block, dim, axis):
        size, at = self.sizes[axis], self.coords[axis]
        total = lax.dynamic_index_in_dim(block, at, dim, keepdims=False).astype(F32)
        for k in range(1, size):
            part = lax.dynamic_index_in_dim(block, (at + k) % size, dim, keepdims=False)
            total = total + self.send(part, axis, k).astype(F32)
        return total

    def scatter_rows(self, block):
        rows, columns = block.shape
        z, y, x = self.sizes
        part = block.reshape(z, y, x, rows // self.count, columns)
        half = columns // 256 * 128
        one = self.scatter_axis(part[..., :half], 2, 2).astype(BF16)
        two = self.scatter_axis(part[..., half:], 1, 1).astype(BF16)
        one = self.scatter_axis(one, 1, 1).astype(BF16)
        two = self.scatter_axis(two, 1, 2).astype(BF16)
        return self.scatter_axis(jnp.concatenate([one, two], axis=-1), 0, 0)


def other_core(block):
    return lax.ppermute(block, "mp", [(0, 1), (1, 0)])


def half_way(block):
    count = lax.axis_size("dp")
    route = [(i, (i + count // 2) % count) for i in range(count)]
    rows = block.shape[0] // 2
    core = lax.axis_index("mp")
    mine = lax.ppermute(lax.dynamic_slice_in_dim(block, core * rows, rows, 0), "dp", route)
    theirs = other_core(mine)
    first = core == 0
    return jnp.concatenate([jnp.where(first, mine, theirs), jnp.where(first, theirs, mine)], axis=0)


def attend_kernel(table, q_ref, k_ref, v_ref, cell_ref, cells_ref, lay_ref, mix_ref, prob_ref, keys, layout, near, score):
    pair, block = pl.program_id(0), pl.program_id(1)
    start = block * BQ

    @pl.when(block == 0)
    def _():
        keys[:, :128] = k_ref[...]
        keys[:, 128:] = cells_ref[...]
        gap = lax.broadcasted_iota(jnp.int32, (8, 896), 1) - (BQ + PAD)
        gap = jnp.clip(gap, -(RB // 2), RB // 2 - 1) + RB // 2
        for h in range(2):
            head = pair * 2 + h
            lay = lay_ref[...]
            grid = jnp.zeros(lay.shape, F32)
            for b in range(LQ * LQ):
                grid = jnp.where(lay == b, table[RB + b, head], grid)
            layout[h] = grid.astype(BF16)
            line = jnp.zeros(gap.shape, F32)
            for b in range(RB):
                line = jnp.where(gap == b, table[b, head], line)
            spread = jnp.broadcast_to(line[:1], (BQ, 896))
            spread = pltpu.roll(spread, 0, 1, stride=1, stride_axis=0)
            near[h] = spread[:, BQ : BQ + WIN]

    lane = lax.broadcasted_iota(jnp.int32, (1, 128), 1)
    feature = lax.broadcasted_iota(jnp.int32, (1, CELLS), 1)
    tile = feature - TILE0
    is_tile = (tile >= 0) & (tile < 10)
    left = is_tile & ((tile + 2) * 128 <= start)
    right = is_tile & (tile * 128 >= start + BQ + PAD)
    queries = q_ref[...].astype(F32) * DH ** (-0.5)
    length = k_ref.shape[0]
    mixed = []
    for h in range(2):
        head = pair * 2 + h
        far = jnp.where(left, table[0, head], jnp.where(right, table[RB - 1, head], 0.0))
        far = jnp.where(feature == DEAD, MASKED, far)
        bias = (nn(cell_ref[...], layout[h]) + far).astype(BF16)
        mine = jnp.where((lane // DH) == h, queries, 0.0).astype(BF16)
        score[h, :, PAD : PAD + length] = nt(jnp.concatenate([mine, bias], axis=1), keys[...])
        window = pl.ds(pl.multiple_of(start, 128), WIN)
        score[h, :, window] += near[h]
        scores = score[h, :, PAD : PAD + length]
        top = jnp.max(scores, axis=1, keepdims=True)
        weight = jnp.exp(scores - top)
        total = jnp.sum(weight, axis=1, keepdims=True)
        prob = (weight * (1.0 / total)).astype(BF16)
        prob_ref[h] = prob
        mixed.append(nn(prob, v_ref[...]))
    mix_ref[...] = jnp.where(lane < DH, mixed[0], mixed[1]).astype(BF16)


def attend(table, queries, keys, values, cells, lay):
    rows, width = queries.shape
    pairs, blocks = width // 128, rows // BQ
    pair_spec = pl.BlockSpec((rows, 128), lambda p, b: (0, p))
    block_spec = pl.BlockSpec((BQ, 128), lambda p, b: (b, p))
    return pl.pallas_call(
        attend_kernel,
        grid=(pairs, blocks),
        in_specs=[
            pl.BlockSpec(memory_space=pltpu.SMEM),
            block_spec,
            pair_spec,
            pair_spec,
            pl.BlockSpec((BQ, CELLS), lambda p, b: (b, 0)),
            pl.BlockSpec((rows, CELLS), lambda p, b: (0, 0)),
            pl.BlockSpec((CELLS, CELLS), lambda p, b: (0, 0)),
        ],
        out_specs=[block_spec, pl.BlockSpec((2, BQ, rows), lambda p, b: (p, b, 0))],
        out_shape=[
            jax.ShapeDtypeStruct((rows, width), BF16),
            jax.ShapeDtypeStruct((2 * pairs, rows, rows), BF16),
        ],
        scratch_shapes=[
            pltpu.VMEM((rows, 128 + CELLS), BF16),
            pltpu.VMEM((2, CELLS, CELLS), BF16),
            pltpu.VMEM((2, BQ, WIN), F32),
            pltpu.VMEM((2, BQ, rows + 2 * PAD), F32),
        ],
        compiler_params=params(),
        cost_estimate=pl.CostEstimate(
            flops=2 * 2 * pairs * rows * rows * 512 * 3 // 2,
            bytes_accessed=2 * 2 * pairs * rows * rows,
            transcendentals=2 * pairs * rows * rows,
        ),
        name="attend",
    )(table, queries, keys, values, cells, cells, lay)


def attend_back_kernel(
    q_ref, k_ref, v_ref, gm_ref, mix_ref, prob_ref, cells_ref, cells_t_ref, lay_ref,
    gq_ref, gk_ref, gv_ref, lay_out, far_out, near_out,
    grads, key_acc, value_acc, near_acc,
):
    pair, block = pl.program_id(0), pl.program_id(1)
    start = block * BQ
    length = k_ref.shape[0]

    @pl.when((pair == 0) & (block == 0))
    def _():
        grads[...] = jnp.zeros(grads.shape, BF16)

    @pl.when(block == 0)
    def _():
        key_acc[...] = jnp.zeros(key_acc.shape, F32)
        value_acc[...] = jnp.zeros(value_acc.shape, F32)
        near_acc[...] = jnp.zeros(near_acc.shape, F32)

    lane = lax.broadcasted_iota(jnp.int32, (1, 128), 1)
    grad_mix = gm_ref[...].astype(F32)
    weighted = grad_mix * mix_ref[...].astype(F32)
    queries_t = q_ref[...].astype(F32).T.astype(BF16)
    grad_mix_t = grad_mix.T.astype(BF16)
    found = []
    for h in range(2):
        own = (lane // DH) == h
        mine = jnp.where(own, grad_mix, 0.0).astype(BF16)
        inner = jnp.sum(jnp.where(own, weighted, 0.0), axis=1, keepdims=True)
        grad_prob = nt(mine, v_ref[...])
        prob = prob_ref[h]
        grad_score = (prob.astype(F32) * (grad_prob - inner)).astype(BF16)
        grads[h, :, PAD : PAD + length] = grad_score
        found.append(nn(grad_score, k_ref[...]))
        left = jnp.concatenate([queries_t[h * DH : (h + 1) * DH], cells_t_ref[...]], axis=0)
        key_acc[h] += nn(left, grad_score)
        value_acc[h] += nn(grad_mix_t[h * DH : (h + 1) * DH], prob)
        window = pl.ds(pl.multiple_of(start, 128), WIN)
        near_acc[h] += grads[h, :, window].astype(F32)
    gq_ref[...] = (jnp.where(lane < DH, found[0], found[1]) * DH ** (-0.5)).astype(BF16)

    @pl.when(block == pl.num_programs(1) - 1)
    def _():
        both = jnp.concatenate([key_acc[0, :DH], key_acc[1, :DH]], axis=0)
        gk_ref[...] = (both.T * DH ** (-0.5)).astype(BF16)
        both = jnp.concatenate([value_acc[0], value_acc[1]], axis=0)
        gv_ref[...] = both.T.astype(BF16)
        for h in range(2):
            by_cell = key_acc[h, DH:]
            high = by_cell.astype(BF16)
            low = (by_cell - high.astype(F32)).astype(BF16)
            pairs = nn(high, cells_ref[...]) + nn(low, cells_ref[...])
            lay = lay_ref[:FEAT_ROWS]
            sums = [
                jnp.sum(jnp.where(lay == b, pairs, 0.0), axis=0, keepdims=True)
                for b in range(LQ * LQ)
            ]
            lay_out[h] = jnp.concatenate(sums, axis=0)
            far_out[h] = key_acc[h, DH + QROW0 - 4 :]
            near_out[h] = near_acc[h]


def attend_back(queries, keys, values, grad_mix, mixture, probs, cells, cells_t, lay):
    rows, width = queries.shape
    pairs, blocks = width // 128, rows // BQ
    pair_spec = pl.BlockSpec((rows, 128), lambda p, b: (0, p))
    block_spec = pl.BlockSpec((BQ, 128), lambda p, b: (b, p))
    small = lambda *shape: pl.BlockSpec((2,) + shape, lambda p, b: (p, 0, 0))
    wide = jax.ShapeDtypeStruct((rows, width), BF16)
    return pl.pallas_call(
        attend_back_kernel,
        grid=(pairs, blocks),
        in_specs=[
            block_spec,
            pair_spec,
            pair_spec,
            block_spec,
            block_spec,
            pl.BlockSpec((2, BQ, rows), lambda p, b: (p, b, 0)),
            pl.BlockSpec((rows, CELLS), lambda p, b: (0, 0)),
            pl.BlockSpec((FEAT_ROWS, BQ), lambda p, b: (0, b)),
            pl.BlockSpec((CELLS, CELLS), lambda p, b: (0, 0)),
        ],
        out_specs=[
            block_spec,
            pair_spec,
            pair_spec,
            small(LQ * LQ, CELLS),
            small(FEAT_ROWS - QROW0 + 4, rows),
            small(BQ, WIN),
        ],
        out_shape=[
            wide,
            wide,
            wide,
            jax.ShapeDtypeStruct((2 * pairs, LQ * LQ, CELLS), F32),
            jax.ShapeDtypeStruct((2 * pairs, FEAT_ROWS - QROW0 + 4, rows), F32),
            jax.ShapeDtypeStruct((2 * pairs, BQ, WIN), F32),
        ],
        scratch_shapes=[
            pltpu.VMEM((2, BQ, rows + 2 * PAD), BF16),
            pltpu.VMEM((2, DH + FEAT_ROWS, rows), F32),
            pltpu.VMEM((2, DH, rows), F32),
            pltpu.VMEM((2, BQ, WIN), F32),
        ],
        compiler_params=params(),
        cost_estimate=pl.CostEstimate(
            flops=2 * 2 * pairs * rows * rows * 256 * 4,
            bytes_accessed=2 * 2 * pairs * rows * rows,
            transcendentals=0,
        ),
        name="attend_back",
    )(queries, keys, values, grad_mix, mixture, probs, cells, cells_t, lay)


def table_sums(lay_sums, far_sums, near_sums, rows):
    heads = lay_sums.shape[0]
    lay_part = jnp.sum(lay_sums, axis=-1)
    blocks = rows // BQ
    far = far_sums[:, 4 : 4 + blocks]
    key = jnp.arange(rows)[None, :]
    first = (jnp.arange(blocks) * BQ)[:, None]
    far_left = jnp.sum(jnp.where(key < first - PAD, far, 0.0), axis=(1, 2))
    far_right = jnp.sum(jnp.where(key >= first + BQ + PAD, far, 0.0), axis=(1, 2))
    flat = jnp.pad(near_sums.reshape(heads, BQ * WIN), ((0, 0), (0, BQ)))
    skew = flat.reshape(heads, BQ, WIN + 1)
    middle = jnp.sum(skew[:, :, PAD - RB // 2 + 1 : PAD + RB // 2 - 1], axis=1)
    gap = jnp.arange(WIN)[None, :] - PAD - jnp.arange(BQ)[:, None]
    near_left = jnp.sum(jnp.where(gap <= -(RB // 2), near_sums, 0.0), axis=(1, 2))
    near_right = jnp.sum(jnp.where(gap >= RB // 2 - 1, near_sums, 0.0), axis=(1, 2))
    rel_part = jnp.concatenate(
        [(far_left + near_left)[:, None], middle, (far_right + near_right)[:, None]], axis=1
    )
    return jnp.concatenate([rel_part, lay_part], axis=1).T


def ffn_kernel(first, *refs):
    if first:
        x_ref, g_ref, wg_ref, wu_ref, wd_ref = refs[:5]
        refs = refs[5:]
    else:
        x_ref, g_ref, wg_ref, wu_ref, wd_ref, out_in, grad_in = refs[:7]
        refs = refs[7:]
    out_ref, grad_ref, gate_ref, up_ref, down_ref, gate_acc, up_acc, down_acc = refs
    step = pl.program_id(0)

    @pl.when(step == 0)
    def _():
        for acc in (gate_acc, up_acc, down_acc):
            acc[...] = jnp.zeros(acc.shape, F32)

    rows_in, grad_in_rows = x_ref[...], g_ref[...]
    gate = nn(rows_in, wg_ref[...]).astype(BF16).astype(F32)
    up = nn(rows_in, wu_ref[...]).astype(BF16).astype(F32)
    grad_act = nn(grad_in_rows, wd_ref[...])
    square = gate * gate
    slope = (2 / jnp.pi) ** 0.5
    tanh = jnp.tanh(slope * gate * (1.0 + 0.044715 * square))
    half = 0.5 * (1.0 + tanh)
    value = gate * half
    deriv = half + 0.5 * gate * (1.0 - tanh * tanh) * slope * (1.0 + 3 * 0.044715 * square)
    act = (value * up).astype(BF16)
    grad_gate = (deriv * up * grad_act).astype(BF16)
    grad_up = (value * grad_act).astype(BF16)
    out = nt(act, wd_ref[...])
    grad = nt(grad_gate, wg_ref[...]) + nt(grad_up, wu_ref[...])
    if not first:
        out = out + out_in[...]
        grad = grad + grad_in[...]
    out_ref[...] = out.astype(out_ref.dtype)
    grad_ref[...] = grad.astype(grad_ref.dtype)
    rows_t = rows_in.astype(F32).T.astype(BF16)
    grads_t = grad_in_rows.astype(F32).T.astype(BF16)
    gate_acc[...] += nn(rows_t, grad_gate)
    up_acc[...] += nn(rows_t, grad_up)
    down_acc[...] += nn(grads_t, act)

    @pl.when(step == pl.num_programs(0) - 1)
    def _():
        gate_ref[...] = gate_acc[...].astype(BF16)
        up_ref[...] = up_acc[...].astype(BF16)
        down_ref[...] = down_acc[...].astype(BF16)


def ffn(normed, grad_ffn, w_gate, w_up, w_down, before=None):
    rows, model = normed.shape
    hidden = w_gate.shape[1]
    first = before is None
    row_spec = pl.BlockSpec((BQ, model), lambda r: (r, 0))
    whole = pl.BlockSpec((model, hidden), lambda r: (0, 0))
    kind = F32 if first else BF16
    part = jax.ShapeDtypeStruct((rows, model), kind)
    grad = jax.ShapeDtypeStruct((model, hidden), BF16)
    return pl.pallas_call(
        functools.partial(ffn_kernel, first),
        grid=(rows // BQ,),
        in_specs=[row_spec] * 2 + [whole] * 3 + ([] if first else [row_spec] * 2),
        out_specs=[row_spec] * 2 + [whole] * 3,
        out_shape=[part] * 2 + [grad] * 3,
        scratch_shapes=[pltpu.VMEM((model, hidden), F32)] * 3,
        compiler_params=params(),
        cost_estimate=pl.CostEstimate(
            flops=18 * rows * model * hidden,
            bytes_accessed=12 * model * hidden + 12 * rows * model,
            transcendentals=rows * hidden,
        ),
        name="ffn_first" if first else "ffn_last",
    )(normed, grad_ffn, w_gate, w_up, w_down, *(() if first else before))


def back_kernel(parts, *refs):
    x_ref = refs[0]
    grads = refs[1 : 1 + parts]
    weights = refs[1 + parts : 1 + 2 * parts]
    out_ref = refs[1 + 2 * parts]
    sums = refs[2 + 2 * parts : 2 + 3 * parts]
    accs = refs[2 + 3 * parts :]
    step = pl.program_id(0)

    @pl.when(step == 0)
    def _():
        for acc in accs:
            acc[...] = jnp.zeros(acc.shape, F32)

    rows_t = x_ref[...].astype(F32).T.astype(BF16)
    out = None
    for grad, weight, acc in zip(grads, weights, accs):
        term = nt(grad[...], weight[...])
        out = term if out is None else out + term
        acc[...] += nn(rows_t, grad[...])
    out_ref[...] = out.astype(BF16)

    @pl.when(step == pl.num_programs(0) - 1)
    def _():
        for total, acc in zip(sums, accs):
            total[...] = acc[...].astype(BF16)


def project_back(normed, grads, weights):
    rows, model = normed.shape
    width = weights[0].shape[1]
    parts = len(grads)
    row_spec = pl.BlockSpec((BQ, model), lambda r: (r, 0))
    grad_spec = pl.BlockSpec((BQ, width), lambda r: (r, 0))
    whole = pl.BlockSpec((model, width), lambda r: (0, 0))
    return pl.pallas_call(
        functools.partial(back_kernel, parts),
        grid=(rows // BQ,),
        in_specs=[row_spec] + [grad_spec] * parts + [whole] * parts,
        out_specs=[row_spec] + [whole] * parts,
        out_shape=[jax.ShapeDtypeStruct((rows, model), BF16)]
        + [jax.ShapeDtypeStruct((model, width), BF16)] * parts,
        scratch_shapes=[pltpu.VMEM((model, width), F32)] * parts,
        compiler_params=params(),
        cost_estimate=pl.CostEstimate(
            flops=4 * parts * rows * model * width,
            bytes_accessed=4 * parts * model * width + 4 * rows * model,
            transcendentals=0,
        ),
        name="project_back",
    )(normed, *grads, *weights)


def norm_rows(row_data):
    scale_inv = lax.rsqrt(jnp.mean(row_data * row_data, axis=-1, keepdims=True) + EPS)
    return (row_data * scale_inv, scale_inv)


def norm_back(grad_normed, unit_rows, scale_inv, gain):
    grad_unit = grad_normed * gain
    return scale_inv * (
        grad_unit - unit_rows * jnp.mean(grad_unit * unit_rows, axis=-1, keepdims=True)
    )


def lay_index():
    cell = jnp.arange(CELLS, dtype=jnp.int32)
    row, col = cell // GRID, cell % GRID
    row_gap = jnp.minimum(jnp.abs(row[:, None] - row[None, :]), LQ - 1)
    col_gap = jnp.minimum(jnp.abs(col[:, None] - col[None, :]), LQ - 1)
    real = (cell < PATCHES)[:, None] & (cell < PATCHES)[None, :]
    return jnp.where(real, row_gap * LQ + col_gap, LQ * LQ)


def exact_split(rows):
    high = rows.astype(BF16)
    return high, (rows - high.astype(F32)).astype(BF16)


def body(
    text_in, patch_in, cot_text, cot_patch, text_count, intersection, text_cell,
    wq, wk, wv, wo_t, gain_one, w_gate, w_up, w_down_t, gain_two, bias_table,
):
    chips = Chips()
    me = lax.axis_index("dp")
    text_slots, model = text_in.shape[1:]
    patch_slots = patch_in.shape[1]
    rows_count = text_slots + patch_slots
    width = wq.shape[1]
    hidden = w_gate.shape[1]

    count = lax.dynamic_index_in_dim(text_count, me, 0, keepdims=False)
    place = lax.dynamic_index_in_dim(text_cell, me, 0, keepdims=False)
    slot = jnp.arange(rows_count, dtype=jnp.int32)
    is_text, live = slot < count, slot < count + PATCHES
    pad_text = lambda a: jnp.pad(a, ((0, patch_slots), (0, 0)))
    patch_id = jnp.arange(patch_slots, dtype=jnp.int32)
    covers = jnp.zeros((rows_count, patch_slots), F32)
    for k in range(intersection.shape[1]):
        listed = jnp.pad(intersection[0, k], (0, patch_slots))
        covers = covers + (listed[:, None] == patch_id).astype(F32)
    pick = ((slot - count)[:, None] == patch_id) & (patch_id < PATCHES)
    spread = jnp.where(is_text[:, None] & (patch_id < PATCHES), covers, pick.astype(F32))
    spread = spread.astype(BF16)
    pick = pick.astype(BF16)

    cell = jnp.pad(place[0] * GRID + place[1], (0, patch_slots))
    cell = jnp.where(is_text, cell, slot - count)
    feature = jnp.arange(CELLS, dtype=jnp.int32)
    key_tile = slot // 128 + TILE0
    cells = (live[:, None] & (cell[:, None] == feature) & (feature < PATCHES)).astype(BF16)
    cells = cells + (key_tile[:, None] == feature).astype(BF16)
    cells = cells + (~live[:, None] & (feature == DEAD)).astype(BF16)
    feature = feature[:FEAT_ROWS, None]
    cells_t = (live & (cell == feature) & (feature < PATCHES)) | (slot // BQ + QROW0 == feature)
    cells_t = cells_t.astype(BF16)
    lay = lay_index()
    table = bias_table.astype(F32)

    gather = lambda w: lax.all_gather(w, "dp", axis=0, tiled=True)
    qkv = gather(jnp.concatenate([wq, wk, wv], axis=1))
    wq_all, wk_all, wv_all = qkv[:, :width], qkv[:, width : 2 * width], qkv[:, 2 * width :]
    gains = gather(jnp.stack([gain_one, gain_two], axis=1)).astype(F32)
    gain_first, gain_second = gains[:, 0], gains[:, 1]
    wo_all = gather(wo_t)
    gate_all, up_all, down_all = gather(w_gate), gather(w_up), gather(w_down_t)

    patches = half_way(patch_in[0])
    patch_cot = half_way(cot_patch[0])
    rows = jnp.where(is_text[:, None], pad_text(text_in[0]).astype(F32), 0.0) + nn(spread, patches)
    grad_out = jnp.where(is_text[:, None], pad_text(cot_text[0]).astype(F32), 0.0)
    grad_ffn = (grad_out + nn(pick, patch_cot)).astype(BF16)
    grad_out = grad_ffn.astype(F32)

    unit_one, inv_one = norm_rows(rows)
    normed_one = (unit_one * gain_first).astype(BF16)
    queries = nn(normed_one, wq_all).astype(BF16)
    keys = nn(normed_one, wk_all).astype(BF16)
    values = nn(normed_one, wv_all).astype(BF16)
    mixture, probs = attend(table, queries, keys, values, cells, lay)
    part = nt(mixture, wo_all).astype(BF16)
    hidden_rows = rows + (part.astype(F32) + other_core(part).astype(F32))
    unit_two, inv_two = norm_rows(hidden_rows)
    normed_two = (unit_two * gain_second).astype(BF16)

    cut = (hidden // 256 + 1) // 2 * 256
    ffn_part, grad_part, gate_one, up_one, down_one = ffn(
        normed_two, grad_ffn, gate_all[:, :cut], up_all[:, :cut], down_all[:, :cut]
    )
    ffn_part, grad_part, gate_two, up_two, down_two = ffn(
        normed_two, grad_ffn, gate_all[:, cut:], up_all[:, cut:], down_all[:, cut:],
        (ffn_part, grad_part),
    )
    sum_one = chips.scatter_rows(jnp.concatenate([gate_one, up_one, down_one], axis=1))
    sum_two = chips.scatter_rows(jnp.concatenate([gate_two, up_two, down_two], axis=1))
    one, two = cut, hidden - cut
    join = lambda i: jnp.concatenate(
        [sum_one[:, i * one : (i + 1) * one], sum_two[:, i * two : (i + 1) * two]], axis=1
    )
    gate_sum, up_sum, down_sum = join(0), join(1), join(2)

    normed_grad_two = grad_part.astype(F32) + other_core(grad_part).astype(F32)
    hidden_grad = grad_out + norm_back(normed_grad_two, unit_two, inv_two, gain_second)
    grad_attn = hidden_grad.astype(BF16)
    grad_mix = nn(grad_attn, wo_all).astype(BF16)
    wo_grad = tn(grad_attn, mixture).astype(BF16)
    grad_q, grad_k, grad_v, lay_sums, far_sums, near_sums = attend_back(
        queries, keys, values, grad_mix, mixture, probs, cells, cells_t, lay
    )
    table_sum = lax.psum(table_sums(lay_sums, far_sums, near_sums, rows_count), "dp")
    normed_part, wq_grad, wk_grad, wv_grad = project_back(
        normed_one, (grad_q, grad_k, grad_v), (wq_all, wk_all, wv_all)
    )
    sums = chips.scatter_rows(jnp.concatenate([wq_grad, wk_grad, wv_grad, wo_grad], axis=1))
    wq_sum, wk_sum, wv_sum, wo_sum = (sums[:, i * width : (i + 1) * width] for i in range(4))

    own_first = sum(
        jnp.sum(w.astype(F32) * g, axis=1) for w, g in ((wq, wq_sum), (wk, wk_sum), (wv, wv_sum))
    )
    own_second = sum(jnp.sum(w.astype(F32) * g, axis=1) for w, g in ((w_gate, gate_sum), (w_up, up_sum)))
    own = jnp.stack([own_first, own_second])
    own = (own + other_core(own)) / jnp.stack([gain_one, gain_two]).astype(F32)
    gain_one_sum, gain_two_sum = own[0], own[1]

    normed_grad_one = normed_part.astype(F32) + other_core(normed_part).astype(F32)
    rows_grad = hidden_grad + norm_back(normed_grad_one, unit_one, inv_one, gain_first)
    text_grad = jnp.where(is_text[:, None], rows_grad, 0.0)[:text_slots].astype(BF16)
    high, low = exact_split(rows_grad)
    patch_grad = half_way((tn(spread, high) + tn(spread, low)).astype(BF16))

    ffn_sum = ffn_part.astype(F32) + other_core(ffn_part).astype(F32)
    result = jnp.where(live[:, None], hidden_rows + ffn_sum, 0.0).astype(BF16)
    text_out = jnp.where(is_text[:, None], result, 0)[:text_slots]
    patch_out = half_way(tn(pick, result).astype(BF16))
    return (
        text_out[None], patch_out[None], text_grad[None], patch_grad[None],
        wq_sum, wk_sum, wv_sum, wo_sum, gain_one_sum, gate_sum, up_sum, down_sum, gain_two_sum,
        table_sum,
    )


def solution(mesh):
    page, weight, vector = P("dp", None, None), P("dp", "mp"), P("dp")
    return jax.shard_map(
        body,
        mesh=mesh,
        in_specs=(page,) * 4
        + (P(), page, P())
        + (weight,) * 4
        + (vector,)
        + (weight,) * 3
        + (vector, P(None, "mp")),
        out_specs=(page,) * 4
        + (weight,) * 4
        + (vector,)
        + (weight,) * 3
        + (vector, P(None, "mp")),
        check_vma=False,
    )
```

time: 2070 us -> 774 us (0.37)
  waiting for transfers between devices: 1150 us -> 312 us
  matrix products: 477 us -> 31.3 us
  Pallas kernels: 0 us -> 174 us
  local copies, waits for them, and re-layouts: 155 us -> 54.7 us
  blocking collectives: 136 us -> 77.3 us
  other arithmetic: 110 us -> 51.5 us
  starting transfers between devices: 16 us -> 48.7 us
    reduce_scatter x7 -> x0, waiting for transfers between devices: 559 us -> none  [the longest x1 130 us: body(): lax.psum_scatter(up_grad, 'dp', scatter_dimension=0, tiled=True)]
    dot_general x51 -> x11, matrix products: 477 us -> 31.3 us  [the longest x6 18.1 us: nn(): lax.dot_general(left, right, (((1,), (0,)), ((), ())), preferred_element_...]
    pallas_call x0 -> x5, Pallas kernels: none -> 174 us  [the longest x1 62 us: attend(): pl.pallas_call(attend_kernel, grid=(pairs, blocks), in_specs=[pl.BlockSpe...]
    unnamed x2 -> x0, blocking collectives: 136 us -> none
    ppermute x10 -> x34, waiting for transfers between devices: 256 us -> 146 us  [the longest x21 116 us: send(): return lax.ppermute(block, 'dp', route)]
    all_gather x7 -> x5, waiting for transfers between devices: 263 us -> 164 us  [body(): gather = lambda w: lax.all_gather(w, 'dp', axis=0, tiled=True)]
    psum x4 -> x0, waiting for transfers between devices: 64.9 us -> none  [the longest x1 26.9 us: body(): attention = lax.psum(right_product(mixture_all, wo_full), 'mp')]
    dot_general x3 -> x0, local copies, waits for them, and re-layouts: 59.3 us -> none  [block_scores(): jnp.einsum('qkb,bh->hqk', onehot, table, preferred_element_type=jnp.float32)]
  transfers between devices with their start and end apart: 28 -> 39, of which waited for: 17 -> 18; matrix products, arithmetic and copies ran while one was open for 17% -> 14% of each run, Pallas kernels for 0% -> 8%
where the time goes in v1:
time: 774 us; the launch traced here: 766 us
  waiting for transfers between devices  312 us (40%)
  Pallas kernels  174 us (22%)
  blocking collectives  77.3 us (10%)
  local copies, waits for them, and re-layouts  54.7 us (7%)
  other arithmetic  51.5 us (7%)
  starting transfers between devices  48.7 us (6%)
  matrix products  31.3 us (4%)
  between operations  16.3 us (2%)
    all_gather x5, waiting for transfers between devices, body(): gather = lambda w: lax.all_gather(w, 'dp', axis=0, tiled=True)  164 us
    ppermute x21, waiting for transfers between devices, send(): return lax.ppermute(block, 'dp', route)  116 us
    pallas_call x1, Pallas kernels, attend(): pl.pallas_call(attend_kernel, grid=(pairs, blocks), in_specs=[pl.BlockSpe...  62 us
    pallas_call x2, Pallas kernels, ffn(): pl.pallas_call(functools.partial(ffn_kernel, first), grid=(rows // BQ,),...  53.5 us
    pallas_call x1, Pallas kernels, attend_back(): pl.pallas_call(attend_back_kernel, grid=(pairs, blocks), in_specs=[block_...  43.6 us
    psum x1, blocking collectives, body(): lax.psum(table_sums(lay_sums, far_sums, near_sums, rows_count), 'dp')  38.8 us
    all_gather x1, blocking collectives, body(): gather = lambda w: lax.all_gather(w, 'dp', axis=0, tiled=True)  38.6 us
    ppermute x21, starting transfers between devices, send(): return lax.ppermute(block, 'dp', route)  34.5 us
  transfers between devices with their start and end apart: 39, of which 18 were waited for; matrix products, arithmetic and copies ran while one was open for 14% of the time, Pallas kernels for 8%

profile of v1, /device:TPU:0, one launch (start us, length us, event | category | flops | bytes accessed | tf_op | source)
XLA Modules:
  0.0 765.7 jit_solution(17010377246425614848)
XLA Ops:
  17.9 38.6 %all-gather = bf16[16,64,2]{1,2,0:T(2,128)(2,1)S(1)} all-gather(bf16[1,64,2]{1,2,0:T(2,128)(2,1)S(1)} %maximum_bitcast_fusion.3), channel_id=1, replica_groups=mesh['dp'=16,'mp'=2] {'dp'}, dimensions={0}, use_global_device_ids=true | all-gather | bytes 4352 | tf_op jit(solution)/shard_map/all_gather | solution.py:522
  69.4 14.7 %all-gather.7.cloned.1.call-done = bf16[1024,1536]{1,0:T(8,128)(2,1)} async-done(((bf16[64,1536]{1,0:T(8,128)(2,1)}), bf16[1024,1536]{1,0:T(8,128)(2,1)}) %all-gather.7.cloned.1.call-update) | async-done | bytes 3145744 | tf_op jit(solution)/shard_map/all_gather | solution.py:522
  93.3 62.0 %attend.1 = (bf16[1280,512]{1,0:T(8,128)(2,1)}, bf16[8,1280,1280]{2,1,0:T(8,128)(2,1)}) custom-call(f32[48,8]{1,0:T(8,128)} %copy.71.table, bf16[1280,512]{1,0:T(8,128)(2,1)} %convolution_convert_fusion.4.q_ref, bf16[1280,512]{1,0:T(8,128)(2,1)} %convolution_convert_fusion.3.k_ref, bf16[1280,512]{1,0:T(8,128)(2,1)} %convolution_convert_fusion.2.v_ref, ...), custom_call_target="tpu_custom_call" | custom-call | flops 20132659200 | bytes 26214400 | tf_op jit(solution)/shard_map/attend/pallas_call | solution.py:160
  161.9 17.2 %collective-permute-done.3 = bf16[128,1024]{1,0:T(8,128)(2,1)S(1)} collective-permute-done((bf16[128,1024]{1,0:T(8,128)(2,1)S(1)}, bf16[128,1024]{1,0:T(8,128)(2,1)S(1)}, u32[]{:S(2)}, u32[]{:S(2)}) %collective-permute-start.3) | collective-permute-done | bytes 262176 | tf_op jit(solution)/shard_map/ppermute | solution.py:97
  185.0 24.9 %all-gather.11.cloned.1.call-done = bf16[1024,1408]{1,0:T(8,128)(2,1)} async-done(((bf16[64,1408]{1,0:T(8,128)(2,1)}), bf16[1024,1408]{1,0:T(8,128)(2,1)}) %all-gather.11.cloned.1.call-update) | async-done | bytes 2883600 | tf_op jit(solution)/shard_map/all_gather | solution.py:522
  215.0 62.4 %all-gather.13.cloned.1.call-done = bf16[1024,1408]{1,0:T(8,128)(2,1)} async-done(((bf16[64,1408]{1,0:T(8,128)(2,1)}), bf16[1024,1408]{1,0:T(8,128)(2,1)}) %all-gather.13.cloned.1.call-update) | async-done | bytes 2883600 | tf_op jit(solution)/shard_map/all_gather | solution.py:522
  282.6 62.4 %all-gather.15.cloned.1.call-done = bf16[1024,1408]{1,0:T(8,128)(2,1)} async-done(((bf16[64,1408]{1,0:T(8,128)(2,1)}), bf16[1024,1408]{1,0:T(8,128)(2,1)}) %all-gather.15.cloned.1.call-update) | async-done | bytes 2883600 | tf_op jit(solution)/shard_map/all_gather | solution.py:522
  358.9 26.6 %ffn_first.1 = (f32[1280,1024]{1,0:T(8,128)}, f32[1280,1024]{1,0:T(8,128)}, bf16[1024,768]{1,0:T(8,128)(2,1)}, bf16[1024,768]{1,0:T(8,128)(2,1)}, bf16[1024,768]{1,0:T(8,128)(2,1)}) custom-call(bf16[1280,1024]{1,0:T(8,128)(2,1)} %multiply_convert_fusion.refs_0_, bf16[1280,1024]{1,0:T(8,128)(2,1)} %add_convert_fusion.refs_1_, ...), custom_call_target="tpu_custom_call" | custom-call | flops 18119393280 | bytes 25165824 | tf_op jit(solution)/shard_map/ffn_first/pallas_call | solution.py:386
  385.5 27.0 %ffn_last.1 = (bf16[1280,1024]{1,0:T(8,128)(2,1)}, bf16[1280,1024]{1,0:T(8,128)(2,1)}, bf16[1024,640]{1,0:T(8,128)(2,1)}, bf16[1024,640]{1,0:T(8,128)(2,1)}, bf16[1024,640]{1,0:T(8,128)(2,1)}) custom-call(bf16[1280,1024]{1,0:T(8,128)(2,1)} %multiply_convert_fusion.refs_0_, bf16[1280,1024]{1,0:T(8,128)(2,1)} %add_convert_fusion.refs_1_, ...), custom_call_target="tpu_custom_call" | custom-call | flops 15099494400 | bytes 23592960 | tf_op jit(solution)/shard_map/ffn_last/pallas_call | solution.py:386
  424.2 16.6 %collective-permute-done.26 = bf16[4,2,64,896]{3,2,0,1:T(8,128)(2,1)S(1)} collective-permute-done((bf16[4,2,64,896]{3,2,0,1:T(8,128)(2,1)S(1)}, bf16[4,2,64,896]{3,2,0,1:T(8,128)(2,1)S(1)}, u32[]{:S(2)}, u32[]{:S(2)}) %collective-permute-start.26) | collective-permute-done | bytes 917536 | tf_op jit(solution)/shard_map/ppermute | solution.py:66
  443.7 19.9 %collective-permute-done.19 = bf16[4,2,64,1152]{3,2,0,1:T(8,128)(2,1)S(1)} collective-permute-done((bf16[4,2,64,1152]{3,2,0,1:T(8,128)(2,1)S(1)}, bf16[4,2,64,1152]{3,2,0,1:T(8,128)(2,1)S(1)}, u32[]{:S(2)}, u32[]{:S(2)}) %collective-permute-start.19) | collective-permute-done | bytes 1179680 | tf_op jit(solution)/shard_map/ppermute | solution.py:66
  470.6 8.9 %collective-permute-done.27 = bf16[4,64,896]{2,1,0:T(8,128)(2,1)S(1)} collective-permute-done((bf16[4,64,896]{2,1,0:T(8,128)(2,1)S(1)}, bf16[4,64,896]{2,1,0:T(8,128)(2,1)S(1)}, u32[]{:S(2)}, u32[]{:S(2)}) %collective-permute-start.27) | collective-permute-done | bytes 458784 | tf_op jit(solution)/shard_map/ppermute | solution.py:66
  494.7 12.0 %collective-permute-done.31 = bf16[64,1920]{1,0:T(8,128)(2,1)S(1)} collective-permute-done((bf16[64,1920]{1,0:T(8,128)(2,1)S(1)}, bf16[64,1920]{1,0:T(8,128)(2,1)S(1)}, u32[]{:S(2)}, u32[]{:S(2)}) %collective-permute-start.31) | collective-permute-done | bytes 245792 | tf_op jit(solution)/shard_map/ppermute | solution.py:66
  506.7 11.6 %collective-permute-start.23 = (bf16[64,2304]{1,0:T(8,128)(2,1)S(1)}, bf16[64,2304]{1,0:T(8,128)(2,1)S(1)}, u32[]{:S(2)}, u32[]{:S(2)}) collective-permute-start(bf16[64,2304]{1,0:T(8,128)(2,1)S(1)} %get-tuple-element.95), channel_id=1, source_target_pairs={{0,8},{2,10},{4,12},{6,14},{8,16},{10,18},{12,20},{14,22},{16,24},... | collective-permute-start | bytes 884744 | tf_op jit(solution)/shard_map/ppermute | solution.py:66
  518.6 10.9 %collective-permute-done.24 = bf16[64,2304]{1,0:T(8,128)(2,1)S(1)} collective-permute-done((bf16[64,2304]{1,0:T(8,128)(2,1)S(1)}, bf16[64,2304]{1,0:T(8,128)(2,1)S(1)}, u32[]{:S(2)}, u32[]{:S(2)}) %collective-permute-start.24) | collective-permute-done | bytes 294944 | tf_op jit(solution)/shard_map/ppermute | solution.py:66
  544.8 43.6 %attend_back.1 = (bf16[1280,512]{1,0:T(8,128)(2,1)}, bf16[1280,512]{1,0:T(8,128)(2,1)}, bf16[1280,512]{1,0:T(8,128)(2,1)}, f32[8,16,256]{2,1,0:T(8,128)}, f32[8,...) custom-call(bf16[1280,512]{1,0:T(8,128)(2,1)} %convolution_convert_fusion.4.q_ref, ...), custom_call_target="tpu_custom_call" | custom-call | flops 26843545600 | bytes 26214400 | tf_op jit(solution)/shard_map/attend_back/pallas_call | solution.py:262
  588.4 14.4 %project_back.1 = (bf16[1280,1024]{1,0:T(8,128)(2,1)}, bf16[1024,512]{1,0:T(8,128)(2,1)}, bf16[1024,512]{1,0:T(8,128)(2,1)}, bf16[1024,512]{1,0:T(8,128)(2,1)}) custom-call(bf16[1280,1024]{1,0:T(8,128)(2,1)} %copy-done.15, bf16[1280,512]{1,0:T(8,128)(2,1)} %get-tuple-element.42.refs_1_, bf16[1280,512]{1,0:T(8,128)(2,1)} %get-tuple-element.43.refs_2_, ...), custom_call_target="tpu_custom_call" | custom-call | flops 8053063680 | bytes 11534336 | tf_op jit(solution)/shard_map/project_back/pallas_call | solution.py:438
  615.4 16.6 %collective-permute-done.12 = bf16[4,2,64,1024]{3,2,0,1:T(8,128)(2,1)S(1)} collective-permute-done((bf16[4,2,64,1024]{3,2,0,1:T(8,128)(2,1)S(1)}, bf16[4,2,64,1024]{3,2,0,1:T(8,128)(2,1)S(1)}, u32[]{:S(2)}, u32[]{:S(2)}) %collective-permute-start.12) | collective-permute-done | bytes 1048608 | tf_op jit(solution)/shard_map/ppermute | solution.py:66
  640.8 6.7 copy.103
  651.6 9.2 %reshape.290 = f32[8,256,513]{2,1,0:T(8,128)} reshape(f32[8,131328]{1,0:T(8,128)} %pad.34) | data formatting | bytes 8404992 | tf_op jit(solution)/shard_map/reshape | solution.py:318
  663.0 38.8 %psum.7 = f32[48,8]{0,1:T(8,128)} all-reduce(f32[48,8]{0,1:T(8,128)S(1)} %maximum_bitcast_fusion.2), channel_id=1, replica_groups=mesh['dp'=16,'mp'=2] {'dp'}, use_global_device_ids=true, to_apply=%region_15.16 | all-reduce | flops 384 | bytes 3072 | tf_op jit(solution)/shard_map/psum | solution.py:572
  713.5 11.1 %collective-permute-done.17 = bf16[64,2048]{1,0:T(8,128)(2,1)S(1)} collective-permute-done((bf16[64,2048]{1,0:T(8,128)(2,1)S(1)}, bf16[64,2048]{1,0:T(8,128)(2,1)S(1)}, u32[]{:S(2)}, u32[]{:S(2)}) %collective-permute-start.17) | collective-permute-done | bytes 262176 | tf_op jit(solution)/shard_map/ppermute | solution.py:66
  737.0 5.9 collective-permute-start.10
  743.5 11.6 %collective-permute-done.10 = bf16[128,1024]{1,0:T(8,128)(2,1)S(1)} collective-permute-done((bf16[128,1024]{1,0:T(8,128)(2,1)S(1)}, bf16[128,1024]{1,0:T(8,128)(2,1)S(1)}, u32[]{:S(2)}, u32[]{:S(2)}) %collective-permute-start.10) | collective-permute-done | bytes 262176 | tf_op jit(solution)/shard_map/ppermute | solution.py:97
  (312 shorter events, 175.8 us)
Async XLA Ops:
  7.2 76.9 %all-gather.7.cloned.1.call-start = ((), (), s32[]{:S(2)}) async-start(), calls=%async_computation | async-start | bytes 3342336 | tf_op jit(solution)/shard_map/all_gather | solution.py:522
  9.0 146.3 %all-gather.9.cloned.1.call-start = ((), (), s32[]{:S(2)}) async-start(), calls=%async_computation.1 | async-start | bytes 1114112 | tf_op jit(solution)/shard_map/all_gather | solution.py:522
  9.8 200.0 %all-gather.11.cloned.1.call-start = ((), (), s32[]{:S(2)}) async-start(), calls=%async_computation.2 | async-start | bytes 3063808 | tf_op jit(solution)/shard_map/all_gather | solution.py:522
  10.5 266.9 %all-gather.13.cloned.1.call-start = ((), (), s32[]{:S(2)}) async-start(), calls=%async_computation.3 | async-start | bytes 3063808 | tf_op jit(solution)/shard_map/all_gather | solution.py:522
  11.1 333.9 %all-gather.15.cloned.1.call-start = ((), (), s32[]{:S(2)}) async-start(), calls=%async_computation.4 | async-start | bytes 3063808 | tf_op jit(solution)/shard_map/all_gather | solution.py:522
  11.2 51.5 %collective-permute-start = (bf16[128,1024]{1,0:T(8,128)(2,1)S(1)}, bf16[128,1024]{1,0:T(8,128)(2,1)S(1)}, u32[]{:S(2)}, u32[]{:S(2)}) collective-permute-start(bf16[128,1024]{1,0:T(8,128)(2,1)S(1)} %dynamic-slice_bitcast_fusion.7), channel_id=1, source_target_pairs={{0,16},{2,18},{4,20},{6,22},{8,24},{10,26},{12,28},{14,30},{16,0},... | collective-permute-start | bytes 786440 | tf_op jit(solution)/shard_map/ppermute | solution.py:97
  158.6 191.5 %collective-permute-start.2 = (bf16[1280,1024]{1,0:T(8,128)(2,1)S(1)}, bf16[1280,1024]{1,0:T(8,128)(2,1)}, u32[]{:S(2)}, u32[]{:S(2)}) collective-permute-start(bf16[1280,1024]{1,0:T(8,128)(2,1)S(1)} %convolution_convert_fusion), channel_id=1, source_target_pairs={{0,1},{1,0},{2,3},{3,2},{4,5},{5,4},{6,7},{7,6},{8,9},{9,8},{10,11... | collective-permute-start | bytes 7864328 | tf_op jit(solution)/shard_map/ppermute | solution.py:89
  415.6 26.0 %collective-permute-start.28 = (bf16[4,2,64,1024]{3,2,0,1:T(8,128)(2,1)S(1)}, bf16[4,2,64,1024]{3,2,0,1:T(8,128)(2,1)S(1)}, u32[]{:S(2)}, u32[]{:S(2)}) collective-permute-start(bf16[4,2,64,1024]{3,2,0,1:T(8,128)(2,1)S(1)} %bitcast.183), channel_id=1, source_target_pairs={{0,4},{2,6},{4,0},{6,2},{8,12},{10,14},{12,8},{14,10},{16,20},{18,... | collective-permute-start | bytes 3145736 | tf_op jit(solution)/shard_map/ppermute | solution.py:66
  417.4 23.4 %collective-permute-start.26 = (bf16[4,2,64,896]{3,2,0,1:T(8,128)(2,1)S(1)}, bf16[4,2,64,896]{3,2,0,1:T(8,128)(2,1)S(1)}, u32[]{:S(2)}, u32[]{:S(2)}) collective-permute-start(bf16[4,2,64,896]{3,2,0,1:T(8,128)(2,1)S(1)} %bitcast.186), channel_id=1, source_target_pairs={{0,2},{2,0},{4,6},{6,4},{8,10},{10,8},{12,14},{14,12},{16,18},{18,... | collective-permute-start | bytes 2752520 | tf_op jit(solution)/shard_map/ppermute | solution.py:66
  419.5 44.0 %collective-permute-start.19 = (bf16[4,2,64,1152]{3,2,0,1:T(8,128)(2,1)S(1)}, bf16[4,2,64,1152]{3,2,0,1:T(8,128)(2,1)S(1)}, u32[]{:S(2)}, u32[]{:S(2)}) collective-permute-start(bf16[4,2,64,1152]{3,2,0,1:T(8,128)(2,1)S(1)} %bitcast.181), channel_id=1, source_target_pairs={{0,2},{2,0},{4,6},{6,4},{8,10},{10,8},{12,14},{14,12},{16,18},{18,... | collective-permute-start | bytes 3538952 | tf_op jit(solution)/shard_map/ppermute | solution.py:66
  422.8 109.3 %collective-permute-start.8 = (bf16[1280,1024]{1,0:T(8,128)(2,1)S(1)}, bf16[1280,1024]{1,0:T(8,128)(2,1)S(1)}, u32[]{:S(2)}, u32[]{:S(2)}) collective-permute-start(bf16[1280,1024]{1,0:T(8,128)(2,1)S(1)} %copy-done.6), channel_id=1, source_target_pairs={{0,1},{1,0},{2,3},{3,2},{4,5},{5,4},{6,7},{7,6},{8,9},{9,8},{10,11... | collective-permute-start | bytes 7864328 | tf_op jit(solution)/shard_map/ppermute | solution.py:89
  423.8 109.7 %collective-permute-start.5 = (bf16[1280,1024]{1,0:T(8,128)(2,1)S(1)}, bf16[1280,1024]{1,0:T(8,128)(2,1)S(1)}, u32[]{:S(2)}, u32[]{:S(2)}) collective-permute-start(bf16[1280,1024]{1,0:T(8,128)(2,1)S(1)} %copy-done.14), channel_id=1, source_target_pairs={{0,1},{1,0},{2,3},{3,2},{4,5},{5,4},{6,7},{7,6},{8,9},{9,8},{10,11... | collective-permute-start | bytes 7864328 | tf_op jit(solution)/shard_map/ppermute | solution.py:89
  440.8 28.9 %collective-permute-start.21 = (bf16[4,2,64,1152]{3,2,0,1:T(8,128)(2,1)S(1)}, bf16[4,2,64,1152]{3,2,0,1:T(8,128)(2,1)S(1)}, u32[]{:S(2)}, u32[]{:S(2)}) collective-permute-start(bf16[4,2,64,1152]{3,2,0,1:T(8,128)(2,1)S(1)} %bitcast.182), channel_id=1, source_target_pairs={{0,4},{2,6},{4,0},{6,2},{8,12},{10,14},{12,8},{14,10},{16,20},{18,... | collective-permute-start | bytes 3538952 | tf_op jit(solution)/shard_map/ppermute | solution.py:66
  441.7 37.9 %collective-permute-start.27 = (bf16[4,64,896]{2,1,0:T(8,128)(2,1)S(1)}, bf16[4,64,896]{2,1,0:T(8,128)(2,1)S(1)}, u32[]{:S(2)}, u32[]{:S(2)}) collective-permute-start(bf16[4,64,896]{2,1,0:T(8,128)(2,1)S(1)} %dynamic-slice_bitcast_fusion.5), channel_id=1, source_target_pairs={{0,4},{2,6},{4,0},{6,2},{8,12},{10,14},{12,8},{14,10},{16,20},{18,... | collective-permute-start | bytes 1376264 | tf_op jit(solution)/shard_map/ppermute | solution.py:66
  491.7 26.8 %collective-permute-start.25 = (bf16[64,2304]{1,0:T(8,128)(2,1)S(1)}, bf16[64,2304]{1,0:T(8,128)(2,1)S(1)}, u32[]{:S(2)}, u32[]{:S(2)}) collective-permute-start(bf16[64,2304]{1,0:T(8,128)(2,1)S(1)} %get-tuple-element.97), channel_id=1, source_target_pairs={{0,24},{2,26},{4,28},{6,30},{8,0},{10,2},{12,4},{14,6},{16,8},{18,... | collective-permute-start | bytes 884744 | tf_op jit(solution)/shard_map/ppermute | solution.py:66
  506.7 22.7 %collective-permute-start.24 = (bf16[64,2304]{1,0:T(8,128)(2,1)S(1)}, bf16[64,2304]{1,0:T(8,128)(2,1)S(1)}, u32[]{:S(2)}, u32[]{:S(2)}) collective-permute-start(bf16[64,2304]{1,0:T(8,128)(2,1)S(1)} %get-tuple-element.96), channel_id=1, source_target_pairs={{0,16},{2,18},{4,20},{6,22},{8,24},{10,26},{12,28},{14,30},{16,0},... | collective-permute-start | bytes 884744 | tf_op jit(solution)/shard_map/ppermute | solution.py:66
  506.7 22.7 %collective-permute-start.23 = (bf16[64,2304]{1,0:T(8,128)(2,1)S(1)}, bf16[64,2304]{1,0:T(8,128)(2,1)S(1)}, u32[]{:S(2)}, u32[]{:S(2)}) collective-permute-start(bf16[64,2304]{1,0:T(8,128)(2,1)S(1)} %get-tuple-element.95), channel_id=1, source_target_pairs={{0,8},{2,10},{4,12},{6,14},{8,16},{10,18},{12,20},{14,22},{16,24},... | collective-permute-start | bytes 884744 | tf_op jit(solution)/shard_map/ppermute | solution.py:66
  602.8 123.0 %collective-permute-start.9 = (bf16[1280,1024]{1,0:T(8,128)(2,1)}, bf16[1280,1024]{1,0:T(8,128)(2,1)}, u32[]{:S(2)}, u32[]{:S(2)}) collective-permute-start(bf16[1280,1024]{1,0:T(8,128)(2,1)} %get-tuple-element.45), channel_id=1, source_target_pairs={{0,1},{1,0},{2,3},{3,2},{4,5},{5,4},{6,7},{7,6},{8,9},{9,8},{10,11... | collective-permute-start | bytes 7864328 | tf_op jit(solution)/shard_map/ppermute | solution.py:89
  606.4 25.6 %collective-permute-start.12 = (bf16[4,2,64,1024]{3,2,0,1:T(8,128)(2,1)S(1)}, bf16[4,2,64,1024]{3,2,0,1:T(8,128)(2,1)S(1)}, u32[]{:S(2)}, u32[]{:S(2)}) collective-permute-start(bf16[4,2,64,1024]{3,2,0,1:T(8,128)(2,1)S(1)} %bitcast.184), channel_id=1, source_target_pairs={{0,2},{2,0},{4,6},{6,4},{8,10},{10,8},{12,14},{14,12},{16,18},{18,... | collective-permute-start | bytes 3145736 | tf_op jit(solution)/shard_map/ppermute | solution.py:66
  609.9 91.9 %collective-permute-start.6 = (bf16[128,1024]{1,0:T(8,128)(2,1)}, bf16[128,1024]{1,0:T(8,128)(2,1)}, u32[]{:S(2)}, u32[]{:S(2)}) collective-permute-start(bf16[128,1024]{1,0:T(8,128)(2,1)} %dynamic-slice_convert_fusion), channel_id=1, source_target_pairs={{0,16},{2,18},{4,20},{6,22},{8,24},{10,26},{12,28},{14,30},{16,0},... | collective-permute-start | bytes 786440 | tf_op jit(solution)/shard_map/ppermute | solution.py:97
  611.9 26.1 %collective-permute-start.14 = (bf16[4,2,64,1024]{3,2,0,1:T(8,128)(2,1)S(1)}, bf16[4,2,64,1024]{3,2,0,1:T(8,128)(2,1)S(1)}, u32[]{:S(2)}, u32[]{:S(2)}) collective-permute-start(bf16[4,2,64,1024]{3,2,0,1:T(8,128)(2,1)S(1)} %bitcast.185), channel_id=1, source_target_pairs={{0,4},{2,6},{4,0},{6,2},{8,12},{10,14},{12,8},{14,10},{16,20},{18,... | collective-permute-start | bytes 3145736 | tf_op jit(solution)/shard_map/ppermute | solution.py:66
  632.5 69.3 %collective-permute-start.13 = (bf16[4,64,1024]{2,1,0:T(8,128)(2,1)S(1)}, bf16[4,64,1024]{2,1,0:T(8,128)(2,1)S(1)}, u32[]{:S(2)}, u32[]{:S(2)}) collective-permute-start(bf16[4,64,1024]{2,1,0:T(8,128)(2,1)S(1)} %dynamic-slice_bitcast_fusion.4), channel_id=1, source_target_pairs={{0,4},{2,6},{4,0},{6,2},{8,12},{10,14},{12,8},{14,10},{16,20},{18,... | collective-permute-start | bytes 1572872 | tf_op jit(solution)/shard_map/ppermute | solution.py:66
  640.2 61.8 %collective-permute-start.15 = (bf16[4,64,1024]{2,1,0:T(8,128)(2,1)}, bf16[4,64,1024]{2,1,0:T(8,128)(2,1)}, u32[]{:S(2)}, u32[]{:S(2)}) collective-permute-start(bf16[4,64,1024]{2,1,0:T(8,128)(2,1)} %dynamic-slice_bitcast_fusion.3), channel_id=1, source_target_pairs={{0,2},{2,0},{4,6},{6,4},{8,10},{10,8},{12,14},{14,12},{16,18},{18,... | collective-permute-start | bytes 1572872 | tf_op jit(solution)/shard_map/ppermute | solution.py:66
  703.6 21.0 %collective-permute-start.17 = (bf16[64,2048]{1,0:T(8,128)(2,1)S(1)}, bf16[64,2048]{1,0:T(8,128)(2,1)S(1)}, u32[]{:S(2)}, u32[]{:S(2)}) collective-permute-start(bf16[64,2048]{1,0:T(8,128)(2,1)S(1)} %get-tuple-element.99), channel_id=1, source_target_pairs={{0,16},{2,18},{4,20},{6,22},{8,24},{10,26},{12,28},{14,30},{16,0},... | collective-permute-start | bytes 786440 | tf_op jit(solution)/shard_map/ppermute | solution.py:66
  (68 other events, 989.9 us)
Sparse Core Ops, SparseCore 0:
  11.4 72.6 all-gather.6
  86.9 53.7 all-gather.8
  143.4 66.3 all-gather.10
  212.4 64.9 all-gather.12
  280.0 64.9 all-gather.14

commit v2 on v1

v2 whole, which is shorter than its diff:
```python
import functools

import jax
import jax.numpy as jnp
from jax import lax
from jax.experimental import pallas as pl
from jax.experimental.pallas import tpu as pltpu
from jax.sharding import PartitionSpec as P

DH = 64
RB = 32
LQ = 4
GRID = 14
PATCHES = 196
EPS = 1e-06

BQ = 256
PAD = 128
WIN = BQ + 2 * PAD
CELLS = 256
TILE0 = PATCHES
DEAD = 206
FEAT_ROWS = 208
MASKED = -1e30
VMEM = 60 * 1024 * 1024
ATTEND_WEIGHT = 4
ROW_VMEM = 24 * 1024 * 1024
F32 = jnp.float32
BF16 = jnp.bfloat16


def nt(left, right):
    return lax.dot_general(left, right, (((1,), (1,)), ((), ())), preferred_element_type=F32)


def nn(left, right):
    return lax.dot_general(left, right, (((1,), (0,)), ((), ())), preferred_element_type=F32)


def tn(left, right):
    return lax.dot_general(left, right, (((0,), (0,)), ((), ())), preferred_element_type=F32)


def params(**more):
    return pltpu.CompilerParams(vmem_limit_bytes=VMEM, **more)


def grid_of(devices):
    side = max(1, round((devices / 4) ** 0.5))
    return (devices // (side * side), side, side)


class Chips:
    def __init__(self):
        self.count = lax.axis_size("dp")
        self.sizes = grid_of(self.count)
        self.plane = self.sizes[1] * self.sizes[2]
        self.strides = (self.plane, self.sizes[2], 1)
        self.me = lax.axis_index("dp")
        layers = range(self.sizes[0])
        self.planes = [[z * self.plane + i for i in range(self.plane)] for z in layers]
        self.columns = [[z * self.plane + i for z in layers] for i in range(self.plane)]

    def send(self, block, axis, distance):
        size, stride = self.sizes[axis], self.strides[axis]
        route = []
        for i in range(self.count):
            c = (i // stride) % size
            route.append((i, i + ((c + distance) % size - c) * stride))
        return lax.ppermute(block, "dp", route)

    def gather_rows(self, block, fast, cuts, after=(), plane_after=(), aside=None):
        block = tie(block, *after)
        if self.sizes[1:] != (2, 2):
            whole = lax.all_gather(block, "dp", axis=0, tiled=True)
            ends = [sum(cuts[: i + 1]) for i in range(len(cuts))]
            whole = [whole[:, end - cut : end] for cut, end in zip(cuts, ends)]
            return whole, (block,), (block,), (block,)
        half = block.shape[0] // 2
        size = self.sizes[0]
        if fast:
            layers = tuple(self.send(block, 0, k) for k in range(1, size))
            own = jnp.stack((block,) + layers)
        else:
            copies = jnp.concatenate([block] * size)
            own = lax.all_to_all(copies, "dp", 0, 0, axis_index_groups=self.columns, tiled=True)
            own = own.reshape((size,) + block.shape)
            layers = (own,)
        own = tie(own, *plane_after)
        by_x, by_y = self.send(own, 2, 1), self.send(own, 1, 1)
        waits = () if aside is None else aside(layers)
        far_top = self.send(tie(by_y[:, :half], *waits), 2, 1)
        far_low = self.send(by_x[:, half:], 1, 1)
        whole = assemble(self.me, size, fast, cuts, own, by_x, by_y, far_top, far_low)
        return whole, layers, (by_x, by_y), (far_top, far_low)

    def order(self, rows):
        part = rows // self.count
        return [(z * self.plane + i) * part for i in range(self.plane) for z in range(self.sizes[0])]

    def exchange(self, block, groups):
        heard = lax.all_to_all(block, "dp", 0, 0, axis_index_groups=groups, tiled=True)
        count = len(groups[0])
        heard = heard.reshape(count, block.shape[0] // count, block.shape[1])
        total = heard[0].astype(F32)
        for i in range(1, count):
            total = total + heard[i].astype(F32)
        return total


    def trade(self, block, groups):
        count = block.shape[0]
        at = self.me % self.plane if groups is self.planes else self.me // self.plane
        total = lax.dynamic_index_in_dim(block, at, 0, keepdims=False).astype(F32)
        for k in range(1, count):
            part = lax.dynamic_index_in_dim(block, at ^ k, 0, keepdims=False)
            route = [(g[i], g[i ^ k]) for g in groups for i in range(count)]
            total = total + lax.ppermute(part, "dp", route).astype(F32)
        return total


def tie_kernel(*refs):
    pass


def tie(block, *others):
    if not others:
        return block
    anywhere = pl.BlockSpec(memory_space=pl.ANY)
    return pl.pallas_call(
        tie_kernel,
        in_specs=[anywhere] * (1 + len(others)),
        out_specs=anywhere,
        out_shape=jax.ShapeDtypeStruct(block.shape, block.dtype),
        input_output_aliases={0: 0},
        name="tie",
    )(block, *others)


def assemble_kernel(me, own, by_x, by_y, far_top, far_low, *outs):
    y, x = (me[0] // 2) % 2, me[0] % 2
    half = far_top.shape[1]
    start = 0
    for out in outs:
        cols = slice(start, start + out.shape[3])
        start = start + out.shape[3]
        out[0, 2 * y + x] = own[0, :, cols]
        out[0, 2 * y + 1 - x] = by_x[0, :, cols]
        out[0, 2 * (1 - y) + x] = by_y[0, :, cols]
        out[0, 2 * (1 - y) + 1 - x, :half] = far_top[0, :, cols]
        out[0, 2 * (1 - y) + 1 - x, half:] = far_low[0, :, cols]


def assemble(me, layers, turned, cuts, *parts):
    rows, columns = parts[0].shape[1:]
    whole = pl.BlockSpec((1, rows, columns), lambda k, me: (k, 0, 0))
    half = pl.BlockSpec((1, rows // 2, columns), lambda k, me: (k, 0, 0))
    place = lambda k, me: (lax.rem(me[0] // 4 - k + layers, layers) if turned else k, 0, 0, 0)
    outs = pl.pallas_call(
        assemble_kernel,
        grid_spec=pltpu.PrefetchScalarGridSpec(
            num_scalar_prefetch=1,
            grid=(layers,),
            in_specs=[whole] * 3 + [half] * 2,
            out_specs=[pl.BlockSpec((1, 4, rows, cut), place) for cut in cuts],
        ),
        out_shape=[jax.ShapeDtypeStruct((layers, 4, rows, cut), BF16) for cut in cuts],
        compiler_params=params(),
        name="assemble",
    )(me[None].astype(jnp.int32), *parts)
    return [out.reshape(4 * layers * rows, out.shape[3]) for out in outs]


def other_core(block):
    return lax.ppermute(block, "mp", [(0, 1), (1, 0)])


def send_half(block, after=()):
    count = lax.axis_size("dp")
    route = [(i, (i + count // 2) % count) for i in range(count)]
    rows = block.shape[0] // 2
    core = lax.axis_index("mp")
    mine = tie(lax.dynamic_slice_in_dim(block, core * rows, rows, 0), *after)
    return lax.ppermute(mine, "dp", route)


def join_halves(mine):
    theirs = other_core(mine)
    first = lax.axis_index("mp") == 0
    return jnp.concatenate([jnp.where(first, mine, theirs), jnp.where(first, theirs, mine)], axis=0)


def attend_kernel(first, extra, table, q_ref, k_ref, v_ref, cells_ref, lay_ref, *refs):
    mix_ref, prob_ref, inv_ref, keys, values, layout, near, *score = refs[extra:]
    pair = pl.program_id(0) + first
    length = k_ref.shape[0]
    keys[:, :128] = k_ref[...]
    keys[:, 128:] = cells_ref[...]
    values_t = v_ref[...].astype(F32).T.astype(BF16)
    for h in range(2):
        values[h, :DH] = values_t[h * DH : (h + 1) * DH]
        values[h, DH:] = jnp.ones((16, length), BF16)
    gap = WIN - lax.broadcasted_iota(jnp.int32, (8, BQ + WIN), 1) - PAD
    gap = jnp.clip(gap, -(RB // 2), RB // 2 - 1) + RB // 2
    for h in range(2):
        head = pair * 2 + h
        lay = lay_ref[...]
        grid = jnp.zeros(lay.shape, F32)
        for b in range(LQ * LQ):
            grid = jnp.where(lay == b, table[RB + b, head], grid)
        layout[h] = grid.astype(BF16)
        line = jnp.zeros(gap.shape, F32)
        for b in range(RB):
            line = jnp.where(gap == b, table[b, head], line)
        spread = jnp.broadcast_to(line[:1], (WIN, BQ + WIN))
        near[h] = pltpu.roll(spread, 0, 1, stride=1, stride_axis=0)[:, WIN:]

    lane = lax.broadcasted_iota(jnp.int32, (1, 128), 1)
    feature = lax.broadcasted_iota(jnp.int32, (1, CELLS), 1)
    tile = feature - TILE0
    is_tile = (tile >= 0) & (tile < 10)

    def fill(item, buffer):
        block, h = divmod(item, 2)
        start, head = block * BQ, pair * 2 + h
        rows = slice(start, start + BQ)
        left = is_tile & ((tile + 2) * 128 <= start)
        right = is_tile & (tile * 128 >= start + BQ + PAD)
        far = jnp.where(left, table[0, head], jnp.where(right, table[RB - 1, head], 0.0))
        far = jnp.where(feature == DEAD, MASKED, far)
        bias = (nn(cells_ref[rows], layout[h]) + far).astype(BF16)
        mine = jnp.where((lane // DH) == h, q_ref[rows] * DH ** (-0.5), 0.0).astype(BF16)
        buffer[...] = nt(keys[...], jnp.concatenate([mine, bias], axis=1))
        low, high = max(start - PAD, 0), min(start + BQ + PAD, length)
        shift = low - (start - PAD)
        buffer[low:high] += near[h, shift : shift + high - low]

    def use(item, buffer):
        block, h = divmod(item, 2)
        scores = buffer[...]
        top = jnp.max(scores, axis=0, keepdims=True)
        weight = jnp.exp(scores - top).astype(BF16)
        prob_ref[h, block] = weight
        summed = nn(values[h], weight)
        inverse = 1.0 / summed[DH : DH + 1]
        inv_ref[h, :, block * BQ : (block + 1) * BQ] = inverse
        return summed[:DH] * inverse

    items = 2 * (length // BQ)
    depth = len(score)
    for item in range(min(depth - 1, items)):
        fill(item, score[item % depth])
    mixed = []
    for item in range(items):
        if item + depth - 1 < items:
            fill(item + depth - 1, score[(item + depth - 1) % depth])
        mixed.append(use(item, score[item % depth]))
        if item % 2:
            start = item // 2 * BQ
            mix_ref[start : start + BQ] = jnp.concatenate(mixed[-2:], axis=0).T.astype(BF16)


def attend(table, projected, cells, lay, first, pairs, width, into=(), after=()):
    rows = projected.shape[0]
    blocks, all_pairs = rows // BQ, width // 128
    pair_spec = lambda i: pl.BlockSpec((rows, 128), lambda p: (0, i * all_pairs + first + p))
    anywhere = pl.BlockSpec(memory_space=pl.ANY)
    extra = len(into) + len(after)
    return pl.pallas_call(
        functools.partial(attend_kernel, first, extra),
        grid=(pairs,),
        in_specs=[
            pl.BlockSpec(memory_space=pltpu.SMEM),
            pair_spec(0),
            pair_spec(1),
            pair_spec(2),
            pl.BlockSpec((rows, CELLS), lambda p: (0, 0)),
            pl.BlockSpec((CELLS, CELLS), lambda p: (0, 0)),
        ]
        + [anywhere] * extra,
        out_specs=[
            pair_spec(0),
            pl.BlockSpec((2, blocks, rows, BQ), lambda p: (first + p, 0, 0, 0)),
            pl.BlockSpec((2, 1, rows), lambda p: (first + p, 0, 0)),
        ],
        out_shape=[
            jax.ShapeDtypeStruct((rows, width), BF16),
            jax.ShapeDtypeStruct((2 * all_pairs, blocks, rows, BQ), BF16),
            jax.ShapeDtypeStruct((2 * all_pairs, 1, rows), F32),
        ],
        input_output_aliases={6 + i: i for i in range(len(into))},
        scratch_shapes=[
            pltpu.VMEM((rows, 128 + CELLS), BF16),
            pltpu.VMEM((2, DH + 16, rows), BF16),
            pltpu.VMEM((2, CELLS, CELLS), BF16),
            pltpu.VMEM((2, WIN, BQ), F32),
        ]
        + [pltpu.VMEM((rows, BQ), F32)] * 3,
        compiler_params=params(),
        cost_estimate=pl.CostEstimate(
            flops=2 * 2 * pairs * rows * rows * 512 * 3 * ATTEND_WEIGHT,
            bytes_accessed=2 * 2 * pairs * rows * rows,
            transcendentals=2 * pairs * rows * rows,
        ),
        name="attend",
    )(table, projected, projected, projected, cells, lay, *into, *after)


def attend_back_kernel(
    extra, q_ref, k_ref, v_ref, gm_ref, mix_ref, prob_ref, inv_ref, cells_ref, cells_t_ref, lay_ref, *refs
):
    gq_ref, gk_ref, gv_ref, lay_out, rel_out = refs[extra : extra + 5]
    left, queries, grads, query_acc, key_acc, value_acc, by_cell, near_acc, *buffers = refs[extra + 5 :]
    length = k_ref.shape[0]
    blocks = length // BQ
    keys_t = k_ref[...].astype(F32).T.astype(BF16)
    queries[...] = q_ref[...].astype(F32).T.astype(BF16)
    grad_mix = gm_ref[...].astype(F32)
    grad_mix_t = grad_mix.T
    weighted_t = (grad_mix * mix_ref[...].astype(F32)).T
    inner = []
    for h in range(2):
        own = slice(h * DH, (h + 1) * DH)
        left[h, :DH] = keys_t[own]
        left[h, DH:] = cells_t_ref[...]
        inverse = inv_ref[h]
        grads[h] = jnp.zeros(grads.shape[1:], BF16)
        grads[h, own] = (grad_mix_t[own] * inverse).astype(BF16)
        inner.append(jnp.sum(weighted_t[own], axis=0, keepdims=True) * inverse)

    def fill(item, buffer):
        block, h = divmod(item, 2)
        buffer[...] = nn(v_ref[...], grads[h, :, block * BQ : (block + 1) * BQ])

    far_left, far_right = [[], []], [[], []]

    def use(item, buffer):
        block, h = divmod(item, 2)
        start = block * BQ
        cols = slice(start, start + BQ)
        own = slice(h * DH, (h + 1) * DH)
        prob = prob_ref[h, block]
        grad_score = (prob.astype(F32) * (buffer[...] - inner[h][:, cols])).astype(BF16)
        both = nn(left[h], grad_score)
        query_acc[own, cols] = both[:DH]
        by_cell[h, :, cols] = both[DH:].astype(BF16)
        tiles = both[DH + TILE0 : DH + TILE0 + length // 128]
        for t in range(length // 128):
            if (t + 2) * 128 <= start:
                far_left[h].append(tiles[t : t + 1])
            elif t * 128 >= start + BQ + PAD:
                far_right[h].append(tiles[t : t + 1])
        key_part = nt(queries[own, cols], grad_score)
        value_part = nt(grads[h, own, cols], prob)
        low, high = max(start - PAD, 0), min(start + BQ + PAD, length)
        shift = low - (start - PAD)
        part = grad_score[low:high].astype(F32)
        if block == 0:
            key_acc[own] = key_part
            value_acc[own] = value_part
            near_acc[h, :shift] = jnp.zeros((shift, BQ), F32)
            near_acc[h, shift : shift + high - low] = part
        else:
            key_acc[own] += key_part
            value_acc[own] += value_part
            near_acc[h, shift : shift + high - low] += part

    items = 2 * blocks
    depth = len(buffers)
    for item in range(min(depth - 1, items)):
        fill(item, buffers[item % depth])
    for item in range(items):
        if item + depth - 1 < items:
            fill(item + depth - 1, buffers[(item + depth - 1) % depth])
        use(item, buffers[item % depth])

    gq_ref[...] = (query_acc[...].T * DH ** (-0.5)).astype(BF16)
    gk_ref[...] = (key_acc[...].T * DH ** (-0.5)).astype(BF16)
    gv_ref[...] = value_acc[...].T.astype(BF16)
    turn = lax.broadcasted_iota(jnp.int32, (BQ, BQ), 0) + lax.broadcasted_iota(jnp.int32, (BQ, BQ), 1)
    turn = (turn == BQ - 1).astype(BF16)
    column = lax.broadcasted_iota(jnp.int32, (1, BQ + WIN), 1)
    lay = lay_ref[:FEAT_ROWS]
    for h in range(2):
        pairs = nn(by_cell[h], cells_ref[...])
        sums = [
            jnp.sum(jnp.where(lay == b, pairs, 0.0), axis=0, keepdims=True) for b in range(LQ * LQ)
        ]
        lay_out[h] = jnp.concatenate(sums, axis=0)
        band = near_acc[h]
        high = band.astype(BF16)
        low = (band - high.astype(F32)).astype(BF16)
        band = nn(high, turn) + nn(low, turn)
        band = jnp.concatenate([band, jnp.zeros((WIN, WIN), F32)], axis=1)
        band = pltpu.roll(band, 0, 1, stride=1, stride_axis=0)
        rel = jnp.sum(band, axis=0, keepdims=True)
        rel = rel + jnp.where(column == 0, jnp.sum(sum(far_left[h]), axis=1, keepdims=True), 0.0)
        last = column == BQ + WIN - 1
        rel_out[h] = rel + jnp.where(last, jnp.sum(sum(far_right[h]), axis=1, keepdims=True), 0.0)


def attend_back(projected, grad_mix, mixture, probs, inverse, cells, cells_t, lay, first, pairs, after=()):
    rows, width = grad_mix.shape
    blocks, all_pairs = rows // BQ, width // 128
    pair_spec = lambda i: pl.BlockSpec((rows, 128), lambda p: (0, i * all_pairs + first + p))
    out_spec = pl.BlockSpec((rows, 128), lambda p: (0, p))
    small = lambda *shape: pl.BlockSpec((2,) + shape, lambda p: (p, 0, 0))
    whole = lambda *shape: pl.BlockSpec(shape, lambda p: (0, 0))
    wide = jax.ShapeDtypeStruct((rows, 128 * pairs), BF16)
    return pl.pallas_call(
        functools.partial(attend_back_kernel, len(after)),
        grid=(pairs,),
        in_specs=[pair_spec(0), pair_spec(1), pair_spec(2), pair_spec(0), pair_spec(0)]
        + [
            pl.BlockSpec((2, blocks, rows, BQ), lambda p: (first + p, 0, 0, 0)),
            pl.BlockSpec((2, 1, rows), lambda p: (first + p, 0, 0)),
            whole(rows, CELLS),
            whole(FEAT_ROWS, rows),
            whole(CELLS, CELLS),
        ]
        + [pl.BlockSpec(memory_space=pl.ANY)] * len(after),
        out_specs=[out_spec] * 3 + [small(LQ * LQ, CELLS), small(1, BQ + WIN)],
        out_shape=[
            wide,
            wide,
            wide,
            jax.ShapeDtypeStruct((2 * pairs, LQ * LQ, CELLS), F32),
            jax.ShapeDtypeStruct((2 * pairs, 1, BQ + WIN), F32),
        ],
        scratch_shapes=[
            pltpu.VMEM((2, DH + FEAT_ROWS, rows), BF16),
            pltpu.VMEM((128, rows), BF16),
            pltpu.VMEM((2, 128, rows), BF16),
            pltpu.VMEM((128, rows), F32),
            pltpu.VMEM((128, rows), F32),
            pltpu.VMEM((128, rows), F32),
            pltpu.VMEM((2, FEAT_ROWS, rows), BF16),
            pltpu.VMEM((2, WIN, BQ), F32),
        ]
        + [pltpu.VMEM((rows, BQ), F32)] * 3,
        compiler_params=params(),
        cost_estimate=pl.CostEstimate(
            flops=2 * 2 * pairs * rows * rows * 256 * 4,
            bytes_accessed=2 * 2 * pairs * rows * rows,
            transcendentals=0,
        ),
        name="attend_back",
    )(projected, projected, projected, grad_mix, mixture, probs, inverse, cells, cells_t, lay, *after)


def table_sums(lay_sums, rel_sums):
    gap = jnp.arange(BQ + WIN) - (BQ - 1 + PAD)
    bucket = jnp.clip(gap, -(RB // 2), RB // 2 - 1) + RB // 2
    onehot = (bucket[:, None] == jnp.arange(RB)).astype(F32)
    rel = jnp.einsum("hn,nb->bh", rel_sums[:, 0], onehot, precision=lax.Precision.HIGHEST)
    return jnp.concatenate([rel, jnp.sum(lay_sums, axis=-1).T], axis=0)


def ffn_kernel(first, extra, base, hidden, order, x_in, g_in, w_in, *refs):
    if not first:
        out_in, grad_in = refs[:2]
    refs = refs[extra:]
    out_to, grad_to, sums_to = refs[:3]
    x, g, w, rows_t, grads_t, act_all, gate_all, up_all, out, grad, sums = refs[3:14]
    sems, sum_sems = refs[14:16]
    total, model = x.shape
    weight = lambda i: w_in.at[:, base + i * hidden : base + (i + 1) * hidden]
    copy = pltpu.make_async_copy
    loads = [
        copy(x_in, x, sems.at[0]),
        copy(weight(0), w.at[0], sems.at[1]),
        copy(weight(1), w.at[1], sems.at[2]),
        copy(g_in, g, sems.at[3]),
        copy(weight(2), w.at[2], sems.at[4]),
    ]
    if not first:
        out_old, grad_old = refs[16:18]
        loads += [copy(out_in, out_old, sems.at[5]), copy(grad_in, grad_old, sems.at[6])]
    for load in loads:
        load.start()
    loads[0].wait()
    rows_t[...] = x[...].astype(F32).T.astype(BF16)
    for load in loads[1:4]:
        load.wait()
    grads_t[...] = g[...].astype(F32).T.astype(BF16)
    for load in loads[4:]:
        load.wait()
    slope = (2 / jnp.pi) ** 0.5
    for cut in range(2):
        rows = slice(cut * (total // 2), (cut + 1) * (total // 2))
        gate = nn(x[rows], w[0]).astype(BF16).astype(F32)
        up = nn(x[rows], w[1]).astype(BF16).astype(F32)
        grad_act = nn(g[rows], w[2])
        square = gate * gate
        tanh = jnp.tanh(gate * (slope + slope * 0.044715 * square))
        half = 0.5 + 0.5 * tanh
        value = gate * half
        deriv = half + (0.5 * gate) * (1.0 - tanh * tanh) * (slope + 3 * 0.044715 * slope * square)
        act_all[rows] = (value * up).astype(BF16)
        gate_all[rows] = (deriv * up * grad_act).astype(BF16)
        up_all[rows] = (value * grad_act).astype(BF16)
    for cut in range(2):
        rows = slice(cut * (total // 2), (cut + 1) * (total // 2))
        out_part = nt(act_all[rows], w[2])
        grad_part = nt(gate_all[rows], w[0]) + nt(up_all[rows], w[1])
        if not first:
            out_part = out_part + out_old[rows].astype(F32)
            grad_part = grad_part + grad_old[rows].astype(F32)
        out[rows] = out_part.astype(BF16)
        grad[rows] = grad_part.astype(BF16)
    stores = [copy(grad, grad_to, sems.at[0]), copy(out, out_to, sems.at[1])]
    for store in stores:
        store.start()
    part = model // len(order)
    for i, (left, right) in enumerate(((rows_t, gate_all), (rows_t, up_all), (grads_t, act_all))):
        sums[i] = nn(left[...], right[...]).astype(BF16)
        for k, row in enumerate(order):
            store = copy(
                sums.at[i, row : row + part],
                sums_to.at[k * part : (k + 1) * part, i * hidden : (i + 1) * hidden],
                sum_sems.at[i, k],
            )
            store.start()
            stores.append(store)
    for store in stores:
        store.wait()


def ffn(normed, grad_ffn, weights, base, hidden, order, before=()):
    rows, model = normed.shape
    first = not before
    extra = len(before)
    anywhere = pl.BlockSpec(memory_space=pl.ANY)
    part = jax.ShapeDtypeStruct((rows, model), BF16)
    vmem = lambda *shape: pltpu.VMEM(shape, BF16)
    return pl.pallas_call(
        functools.partial(ffn_kernel, first, extra, base, hidden, order),
        in_specs=[anywhere] * (3 + extra),
        out_specs=[anywhere] * 3,
        out_shape=[part, part, jax.ShapeDtypeStruct((model, 3 * hidden), BF16)],
        scratch_shapes=[vmem(rows, model)] * 2
        + [vmem(3, model, hidden)]
        + [vmem(model, rows)] * 2
        + [vmem(rows, hidden)] * 3
        + [vmem(rows, model)] * 2
        + [vmem(3, model, hidden)]
        + [pltpu.SemaphoreType.DMA((7,)), pltpu.SemaphoreType.DMA((3, len(order)))]
        + ([] if first else [vmem(rows, model)] * 2),
        compiler_params=params(),
        cost_estimate=pl.CostEstimate(
            flops=18 * rows * model * hidden,
            bytes_accessed=12 * model * hidden + 8 * rows * model,
            transcendentals=rows * hidden,
        ),
        name="ffn_first" if first else "ffn_last",
    )(normed, grad_ffn, weights, *before)


def back_kernel(order, kind, rows_t, *refs):
    grads = jnp.concatenate([r[...] for r in refs[:3]], axis=1)
    weights = jnp.concatenate([r[...] for r in refs[3:6]], axis=1)
    if kind == "first":
        carry, (out_ref, sums) = refs[6], refs[-2:]
        out = nt(grads, weights)
    else:
        before, table, (out_ref, sums) = *refs[6:8], refs[-2:]
        out = nt(grads, weights) + before[...].astype(F32)
    out_ref[...] = out.astype(BF16)
    found = nn(rows_t[...], grads).astype(BF16)
    model, width = found.shape
    part = model // len(order)
    chunk = model // sums.shape[0]
    for k, start in enumerate(order):
        place, at = divmod(k * part, chunk)
        sums[place, at : at + part, :width] = found[start : start + part]
        if kind == "first":
            sums[place, at : at + part, width:] = carry[k * part : (k + 1) * part]
    if kind != "first":
        for place in range(sums.shape[0]):
            sums[place, chunk:] = table[...]


def project_back(rows_t, grads, weights, width, first, order, plane, carry=None, before=None, table=None, after=()):
    model, rows = rows_t.shape
    half = grads[0].shape[1]
    whole = lambda *shape: pl.BlockSpec(shape, lambda j: (0,) * len(shape), pipeline_mode=pl.Buffered(1))
    at = lambda i: pl.BlockSpec((model, half), lambda j: (0, (i * width + first) // half))
    kind = "first" if before is None else "last"
    if kind == "first":
        more, shape = (carry,), (plane, model // plane, 3 * half + carry.shape[1])
    else:
        more, shape = (before, table), (plane, model // plane + table.shape[0], 3 * half)
    return pl.pallas_call(
        functools.partial(back_kernel, order, kind),
        grid=(1,),
        in_specs=[whole(model, rows)]
        + [whole(rows, half)] * 3
        + [at(0), at(1), at(2)]
        + [whole(*m.shape) for m in more]
        + [pl.BlockSpec(memory_space=pl.ANY)] * len(after),
        out_specs=[whole(rows, model), whole(*shape)],
        out_shape=[jax.ShapeDtypeStruct((rows, model), BF16), jax.ShapeDtypeStruct(shape, BF16)],
        compiler_params=params(),
        cost_estimate=pl.CostEstimate(
            flops=12 * rows * model * half,
            bytes_accessed=12 * model * half + 4 * rows * model,
            transcendentals=0,
        ),
        name="project_back",
    )(rows_t, *grads, weights, weights, weights, *more, *after)


def rows_spec(columns, limit=None):
    if limit is None:
        return pl.BlockSpec((BQ, columns), lambda r: (r, 0))
    return pl.BlockSpec((BQ, columns), lambda r: (jnp.minimum(r, limit // BQ - 1), 0))


def fixed_spec(*shape):
    return pl.BlockSpec(shape, lambda r: (0,) * len(shape))


SCALAR = pl.BlockSpec(memory_space=pltpu.SMEM)


def is_text(count):
    row = lax.broadcasted_iota(jnp.int32, (BQ, 1), 0) + pl.program_id(0) * BQ
    return row < count[0]


def row_call(kernel, name, rows, in_specs, out, scratch, flops, *operands):
    out_specs, out_shape = zip(*out)
    return pl.pallas_call(
        kernel,
        grid=(rows // BQ,),
        in_specs=in_specs,
        out_specs=out_specs,
        out_shape=[jax.ShapeDtypeStruct(*o) for o in out_shape],
        scratch_shapes=scratch,
        compiler_params=pltpu.CompilerParams(vmem_limit_bytes=ROW_VMEM),
        cost_estimate=pl.CostEstimate(flops=flops, bytes_accessed=20 * rows * 1024, transcendentals=0),
        name=name,
    )(*operands)


def embed_kernel(count, text, spread, patches, rows):
    own = jnp.where(is_text(count), text[...].astype(F32), 0.0)
    rows[...] = (own + nn(spread[...], patches[...])).astype(rows.dtype)


def embed(count, text, spread, patches, kind=F32):
    rows, slots = spread.shape
    texts, model = text.shape
    return row_call(
        embed_kernel, "embed", rows,
        [SCALAR, rows_spec(model, texts), rows_spec(slots), fixed_spec(slots, model)],
        [(rows_spec(model), ((rows, model), kind))],
        [], 2 * rows * slots * model, count, text, spread, patches,
    )[0]


def norm(rows):
    inv = lax.rsqrt(jnp.mean(rows * rows, axis=1, keepdims=True) + EPS)
    return rows * inv, inv


def norm_back(grad_normed, rows, gain):
    unit, inv = norm(rows)
    grad_unit = grad_normed * gain
    return inv * (grad_unit - unit * jnp.mean(grad_unit * unit, axis=1, keepdims=True))


def project_kernel(rows, weights, projected, normed_t, gains):
    width = projected.shape[1]

    @pl.when(pl.program_id(0) == 0)
    def _():
        gains[...] = weights[:, width:].astype(F32).T[:8]

    normed = norm(rows[...])[0] * gains[:1]
    normed_t[...] = normed.T.astype(BF16)
    projected[...] = nn(normed.astype(BF16), weights[:, :width]).astype(BF16)


def project(rows, weights):
    count, model = rows.shape
    width = weights.shape[1] - 128
    return row_call(
        project_kernel, "project", count,
        [rows_spec(model), pl.BlockSpec(weights.shape, lambda r: (0, 0), pipeline_mode=pl.Buffered(1))],
        [
            (rows_spec(width), ((count, width), BF16)),
            (pl.BlockSpec((model, BQ), lambda r: (0, r)), ((model, count), BF16)),
            (fixed_spec(8, model), ((8, model), F32)),
        ],
        [], 2 * count * model * width, rows, weights,
    )


def mix_out_kernel(mixture, weight, out):
    out[...] = nt(mixture[...], weight[...]).astype(BF16)


def mix_out(mixture, weights):
    rows, width = mixture.shape
    model = weights.shape[0]
    return row_call(
        mix_out_kernel, "mix_out", rows,
        [rows_spec(width), fixed_spec(model, width)],
        [(rows_spec(model), ((rows, model), BF16))],
        [], 2 * rows * model * width, mixture, weights,
    )[0]


def middle_kernel(rows, own, other, gains, hidden, normed):
    total = rows[...] + (own[...].astype(F32) + other[...].astype(F32))
    hidden[...] = total
    normed[...] = (norm(total)[0] * gains[1:2]).astype(BF16)


def middle(rows, own, other, gains):
    count, model = rows.shape
    return row_call(
        middle_kernel, "middle", count,
        [rows_spec(model)] * 3 + [fixed_spec(8, model)],
        [(rows_spec(model), ((count, model), F32)), (rows_spec(model), ((count, model), BF16))],
        [], 0, rows, own, other, gains,
    )


def after_kernel(order, hidden, own, other, grad_out, gains, weight, mixture, *refs):
    grad_attn, grad_mix, sums, acc = refs[-4:]
    step = pl.program_id(0)

    @pl.when(step == 0)
    def _():
        acc[...] = jnp.zeros(acc.shape, F32)

    grad = own[...].astype(F32) + other[...].astype(F32)
    grad = grad_out[...].astype(F32) + norm_back(grad, hidden[...], gains[1:2])
    low = grad.astype(BF16)
    grad_attn[...] = low
    grad_mix[...] = nn(low, weight[...]).astype(BF16)
    acc[...] += nn(grad.T.astype(BF16), mixture[...])

    @pl.when(step == pl.num_programs(0) - 1)
    def _():
        part = acc.shape[0] // len(order)
        for k, start in enumerate(order):
            sums[k * part : (k + 1) * part] = acc[start : start + part].astype(BF16)


def after_ffn(hidden, own, other, grad_out, gains, weights, mixture, order, after=()):
    rows, model = hidden.shape
    width = mixture.shape[1]
    return row_call(
        functools.partial(after_kernel, order), "after_ffn", rows,
        [rows_spec(model)] * 4
        + [fixed_spec(8, model), fixed_spec(model, width), rows_spec(width)]
        + [pl.BlockSpec(memory_space=pl.ANY)] * len(after),
        [
            (rows_spec(model), ((rows, model), BF16)),
            (rows_spec(width), ((rows, width), BF16)),
            (fixed_spec(model, width), ((model, width), BF16)),
        ],
        [pltpu.VMEM((model, width), F32)], 4 * rows * model * width,
        hidden, own, other, grad_out, gains, weights, mixture, *after,
    )


def last_kernel(count, rows, own, other, grad, gains, spread, *refs):
    text_grad, patch_grad, acc = refs[-3:]
    step = pl.program_id(0)

    @pl.when(step == 0)
    def _():
        acc[...] = jnp.zeros(acc.shape, F32)

    total = own[...].astype(F32) + other[...].astype(F32)
    total = grad[...].astype(F32) + norm_back(total, rows[...], gains[:1])

    @pl.when(step < pl.num_programs(0) - 1)
    def _():
        text_grad[...] = jnp.where(is_text(count), total, 0.0).astype(BF16)

    high = total.astype(BF16)
    low = (total - high.astype(F32)).astype(BF16)
    places = spread[...].astype(F32).T.astype(BF16)
    acc[...] += nn(places, high) + nn(places, low)

    @pl.when(step == pl.num_programs(0) - 1)
    def _():
        patch_grad[...] = acc[...].astype(BF16)


def last(count, rows, own, other, grad, gains, spread, texts, after=()):
    length, model = rows.shape
    slots = spread.shape[1]
    return row_call(
        last_kernel, "last", length,
        [SCALAR] + [rows_spec(model)] * 4 + [fixed_spec(8, model), rows_spec(slots)]
        + [pl.BlockSpec(memory_space=pl.ANY)] * len(after),
        [(rows_spec(model, texts), ((texts, model), BF16)), (fixed_spec(slots, model), ((slots, model), BF16))],
        [pltpu.VMEM((slots, model), F32)], 4 * length * model * slots,
        count, rows, own, other, grad, gains, spread, *after,
    )


def result_kernel(count, hidden, own, other, pick, *refs):
    text_out, patch_out, acc = refs[-3:]
    step = pl.program_id(0)

    @pl.when(step == 0)
    def _():
        acc[...] = jnp.zeros(acc.shape, F32)

    total = hidden[...] + (own[...].astype(F32) + other[...].astype(F32))

    @pl.when(step < pl.num_programs(0) - 1)
    def _():
        text_out[...] = jnp.where(is_text(count), total, 0.0).astype(BF16)

    acc[...] += nn(pick[...].astype(F32).T.astype(BF16), total.astype(BF16))

    @pl.when(step == pl.num_programs(0) - 1)
    def _():
        patch_out[...] = acc[...].astype(BF16)


def result(count, hidden, own, other, pick, texts, after=()):
    length, model = hidden.shape
    slots = pick.shape[1]
    return row_call(
        result_kernel, "result", length,
        [SCALAR] + [rows_spec(model)] * 3 + [rows_spec(slots)]
        + [pl.BlockSpec(memory_space=pl.ANY)] * len(after),
        [(rows_spec(model, texts), ((texts, model), BF16)), (fixed_spec(slots, model), ((slots, model), BF16))],
        [pltpu.VMEM((slots, model), F32)], 2 * length * model * slots,
        count, hidden, own, other, pick, *after,
    )


def lay_index():
    cell = jnp.arange(CELLS, dtype=jnp.int32)
    row, col = cell // GRID, cell % GRID
    row_gap = jnp.minimum(jnp.abs(row[:, None] - row[None, :]), LQ - 1)
    col_gap = jnp.minimum(jnp.abs(col[:, None] - col[None, :]), LQ - 1)
    real = (cell < PATCHES)[:, None] & (cell < PATCHES)[None, :]
    return jnp.where(real, row_gap * LQ + col_gap, LQ * LQ)


def body(
    text_in, patch_in, cot_text, cot_patch, text_count, intersection, text_cell,
    wq, wk, wv, wo_t, gain_one, w_gate, w_up, w_down_t, gain_two, bias_table,
):
    chips = Chips()
    me = lax.axis_index("dp")
    text_slots, model = text_in.shape[1:]
    patch_slots = patch_in.shape[1]
    rows_count = text_slots + patch_slots
    live_slots = (PATCHES + 15) // 16 * 16
    width = wq.shape[1]
    hidden = w_gate.shape[1]

    count = lax.dynamic_slice_in_dim(text_count, me, 1, 0)
    place = lax.dynamic_index_in_dim(text_cell, me, 0, keepdims=False)
    slot = jnp.arange(rows_count, dtype=jnp.int32)
    is_text, live = slot < count, slot < count + PATCHES
    patch_id = jnp.arange(live_slots, dtype=jnp.int32)
    covers = jnp.zeros((rows_count, live_slots), F32)
    for k in range(intersection.shape[1]):
        listed = jnp.pad(intersection[0, k], (0, patch_slots))
        covers = covers + (listed[:, None] == patch_id).astype(F32)
    pick = ((slot - count)[:, None] == patch_id) & (patch_id < PATCHES)
    spread = jnp.where(is_text[:, None] & (patch_id < PATCHES), covers, pick.astype(F32))
    spread = spread.astype(BF16)
    pick = pick.astype(BF16)

    cell = jnp.pad(place[0] * GRID + place[1], (0, patch_slots))
    cell = jnp.where(is_text, cell, slot - count)
    feature = jnp.arange(CELLS, dtype=jnp.int32)
    key_tile = slot // 128 + TILE0
    cells = (live[:, None] & (cell[:, None] == feature) & (feature < PATCHES)).astype(BF16)
    cells = cells + (key_tile[:, None] == feature).astype(BF16)
    cells = cells + (~live[:, None] & (feature == DEAD)).astype(BF16)
    feature = feature[:FEAT_ROWS, None]
    cells_t = (live & (cell == feature) & (feature < PATCHES)) | (key_tile == feature)
    cells_t = cells_t.astype(BF16)
    lay = lay_index()
    table = bias_table.astype(F32)

    cut = hidden // 3 // 256 * 256 + 256
    gains = jnp.pad(jnp.stack([gain_one, gain_two], axis=1), ((0, 0), (0, 126)))
    sent = []
    (qkv,), layers, planes, corners = chips.gather_rows(
        jnp.concatenate([wq, wk, wv, gains], axis=1), True, (3 * width + 128,),
        aside=lambda layers: (sent.append(send_half(patch_in[0, :live_slots], layers)), sent[0])[1:],
    )
    sent = sent or [send_half(patch_in[0, :live_slots])]
    patches = join_halves(sent[0])
    (wo_all, first_set), layers, planes, _ = chips.gather_rows(
        jnp.concatenate([wo_t, w_gate[:, :cut], w_up[:, :cut], w_down_t[:, :cut]], axis=1),
        True, (width, 3 * cut), planes, corners,
    )
    patch_cot = join_halves(send_half(cot_patch[0, :live_slots], layers))
    last_set = lax.all_gather(
        tie(jnp.concatenate([w_gate[:, cut:], w_up[:, cut:], w_down_t[:, cut:]], axis=1), *corners),
        "dp", axis=0, tiled=True,
    )
    rows = embed(count, text_in[0], spread, patches)
    grad_ffn = embed(count, cot_text[0], pick, patch_cot, BF16)

    projected, normed_t, gains = project(rows, qkv)
    half = width // 256
    seen = attend(table, projected, cells, lay, 0, half, width)
    mixture, probs, inverse = attend(table, projected, cells, lay, half, half, width, seen, (*planes, patch_cot))
    part = mix_out(mixture, wo_all)
    hidden_rows, normed_two = middle(rows, part, other_core(part), gains)

    order = chips.order(model)
    ffn_part, grad_part, grads_one = ffn(normed_two, grad_ffn, first_set, 0, cut, order)
    ffn_part, grad_part, grads_two = ffn(
        normed_two, grad_ffn, last_set, 0, hidden - cut, order, (ffn_part, grad_part)
    )
    scatter = lambda a, groups: lax.psum_scatter(
        a, "dp", scatter_dimension=0, axis_index_groups=groups, tiled=True
    )
    sum_one, sum_two = scatter(grads_one, chips.planes), scatter(grads_two, chips.planes)
    grad_attn, grad_mix, wo_grad = after_ffn(
        hidden_rows, grad_part, other_core(grad_part), grad_ffn, gains, wo_all, mixture, order
    )
    sum_one = chips.exchange(tie(sum_one, grad_mix), chips.columns)
    args = (projected, grad_mix, mixture, probs, inverse, cells, cells_t, lay)
    *grads_a, lay_a, rel_a = attend_back(*args, 0, half)
    normed_a, grads_a = project_back(
        normed_t, grads_a, qkv, width, 0, order, chips.plane, carry=wo_grad, after=(sum_one,)
    )
    sum_a = chips.exchange(grads_a.reshape(model, -1), chips.planes).astype(BF16)
    *grads_b, lay_b, rel_b = attend_back(*args, half, half, (normed_a,))
    table_part = table_sums(jnp.concatenate([lay_a, lay_b]), jnp.concatenate([rel_a, rel_b]))
    normed_part, grads_b = project_back(
        normed_t, grads_b, qkv, width, width // 2, order, chips.plane,
        before=normed_a, table=wide_row(table_part, 3 * width // 2),
    )
    sum_two = scatter(tie(jnp.concatenate([sum_two, sum_a], axis=1), normed_part), chips.columns).astype(F32)
    sum_a = sum_two[:, 3 * (hidden - cut) :]
    ffn_other = other_core(ffn_part)
    text_grad, patch_grad = last(
        count, rows, normed_part, other_core(normed_part), grad_attn, gains, spread, text_slots
    )
    text_out, patch_out = result(
        count, hidden_rows, ffn_part, ffn_other, pick, text_slots, (normed_part,)
    )
    sum_b = chips.trade(grads_b, chips.planes)
    chunk = model // chips.plane
    table_row = wide_row(narrow_row(sum_b[chunk], table.shape), sum_b.shape[1])
    layers = chips.sizes[0]
    sum_b = sum_b[:chunk].astype(BF16).reshape(layers, chunk // layers, -1)
    sum_b = jnp.concatenate([sum_b, jnp.broadcast_to(table_row, (layers,) + table_row.shape)], axis=1)
    sum_b = chips.trade(tie(sum_b, patch_grad, patch_out), chips.columns)
    sum_b, table_sum = sum_b[: chunk // layers], narrow_row(sum_b[chunk // layers], table.shape)
    fill = lambda a: jnp.pad(a, ((0, patch_slots - live_slots), (0, 0)))
    back = fill(join_halves(send_half(jnp.concatenate([patch_out, patch_grad], axis=1))))
    patch_out, patch_grad = back[:, :model], back[:, model:]

    rest = hidden - cut
    join = lambda i: jnp.concatenate(
        [
            sum_one[:, i * cut : (i + 1) * cut], sum_two[:, i * rest : (i + 1) * rest],
        ],
        axis=1,
    )
    gate_sum, up_sum, down_sum = join(0), join(1), join(2)
    cols = width // 2
    wq_sum, wk_sum, wv_sum = (
        jnp.concatenate([a[:, i * cols : (i + 1) * cols] for a in (sum_a, sum_b)], axis=1)
        for i in range(3)
    )
    wo_sum = sum_a[:, 3 * cols :]

    own_first = sum(
        jnp.sum(w.astype(F32) * g, axis=1) for w, g in ((wq, wq_sum), (wk, wk_sum), (wv, wv_sum))
    )
    own_second = sum(jnp.sum(w.astype(F32) * g, axis=1) for w, g in ((w_gate, gate_sum), (w_up, up_sum)))
    own = jnp.stack([own_first, own_second])
    own = (own + other_core(own)) / jnp.stack([gain_one, gain_two]).astype(F32)
    return (
        text_out[None], patch_out[None], text_grad[None], patch_grad[None],
        wq_sum, wk_sum, wv_sum, wo_sum, own[0], gate_sum, up_sum, down_sum, own[1],
        table_sum,
    )


def wide_row(values, columns):
    flat = values.reshape(-1)
    high = flat.astype(BF16)
    low = (flat - high.astype(F32)).astype(BF16)
    both = jnp.concatenate([high, low])
    return jnp.pad(both[None], ((0, 15), (0, columns - both.shape[0])))


def narrow_row(row, shape):
    size = shape[0] * shape[1]
    return (row[:size] + row[size : 2 * size]).reshape(shape)


def solution(mesh):
    page, weight, vector = P("dp", None, None), P("dp", "mp"), P("dp")
    return jax.shard_map(
        body,
        mesh=mesh,
        in_specs=(page,) * 4
        + (P(), page, P())
        + (weight,) * 4
        + (vector,)
        + (weight,) * 3
        + (vector, P(None, "mp")),
        out_specs=(page,) * 4
        + (weight,) * 4
        + (vector,)
        + (weight,) * 3
        + (vector, P(None, "mp")),
        check_vma=False,
    )
```

time: 774 us -> 425 us (0.55)
  waiting for transfers between devices: 312 us -> 58.2 us
  blocking collectives: 77.3 us -> 0 us
  matrix products: 31.3 us -> 0.32 us
  Pallas kernels: 174 us -> 204 us
  other arithmetic: 51.5 us -> 34.1 us
    all_gather x5 -> x1, waiting for transfers between devices: 164 us -> 0.02 us  [body(): lax.all_gather(tie(jnp.concatenate([w_gate[:, cut:], w_up[:, cut:], w_dow...]
    ppermute x21 -> x14, waiting for transfers between devices: 116 us -> 12.3 us  [send(): return lax.ppermute(block, 'dp', route)]
    psum x1 -> x0, blocking collectives: 38.8 us -> none  [body(): lax.psum(table_sums(lay_sums, far_sums, near_sums, rows_count), 'dp')]
    all_gather x1 -> x0, blocking collectives: 38.6 us -> none  [body(): gather = lambda w: lax.all_gather(w, 'dp', axis=0, tiled=True)]
    dot_general x11 -> x1, matrix products: 31.3 us -> 0.32 us  [table_sums(): jnp.einsum('hn,nb->bh', rel_sums[:, 0], onehot, precision=lax.Precision.H...]
    pallas_call x5 -> x27, Pallas kernels: 174 us -> 204 us  [the longest x2 51.7 us: ffn(): pl.pallas_call(functools.partial(ffn_kernel, first, extra, base, hidden,...]
    unnamed x111 -> x146, local copies, waits for them, and re-layouts: 15.6 us -> 40.4 us
    ppermute x21 -> x14, starting transfers between devices: 34.5 us -> 21.7 us  [send(): return lax.ppermute(block, 'dp', route)]
  transfers between devices with their start and end apart: 39 -> 37, of which waited for: 18 -> 9; matrix products, arithmetic and copies ran while one was open for 14% -> 11% of each run, Pallas kernels for 8% -> 49%
where the time goes in v2:
time: 425 us; the launch traced here: 419 us
  Pallas kernels  204 us (48%)
  waiting for transfers between devices  58.2 us (14%)
  local copies, waits for them, and re-layouts  57.8 us (14%)
  starting transfers between devices  47.8 us (11%)
  other arithmetic  34.1 us (8%)
  between operations  17.5 us (4%)
    pallas_call x2, Pallas kernels, ffn(): pl.pallas_call(functools.partial(ffn_kernel, first, extra, base, hidden,...  51.7 us
    pallas_call x2, Pallas kernels, attend_back(): pl.pallas_call(functools.partial(attend_back_kernel, len(after)), grid=(p...  47.3 us
    pallas_call x2, Pallas kernels, attend(): pl.pallas_call(functools.partial(attend_kernel, first, extra), grid=(pair...  41.7 us
    unnamed x146, local copies, waits for them, and re-layouts  40.4 us
    pallas_call x8, Pallas kernels, row_call(): pl.pallas_call(kernel, grid=(rows // BQ,), in_specs=in_specs, out_specs=o...  35.8 us
    ppermute x3, waiting for transfers between devices, send_half(): return lax.ppermute(mine, 'dp', route)  31.3 us
    ppermute x14, starting transfers between devices, send(): return lax.ppermute(block, 'dp', route)  21.7 us
    pallas_call x2, Pallas kernels, project_back(): pl.pallas_call(functools.partial(back_kernel, order, kind), grid=(1,), in...  17.8 us
  transfers between devices with their start and end apart: 37, of which 9 were waited for; matrix products, arithmetic and copies ran while one was open for 11% of the time, Pallas kernels for 49%

profile of v2, /device:TPU:0, one launch (start us, length us, event | category | flops | bytes accessed | tf_op | source)
XLA Modules:
  0.0 419.4 jit_solution(10793865282984984071)
XLA Ops:
  9.9 3.1 collective-permute-start
  37.3 4.1 collective-permute-start.3
  42.3 8.7 %collective-permute-done.3.refs_1_ = bf16[104,1024]{1,0:T(8,128)(2,1)S(1)} collective-permute-done((bf16[104,1024]{1,0:T(8,128)(2,1)}, bf16[104,1024]{1,0:T(8,128)(2,1)S(1)}, u32[]{:S(2)}, u32[]{:S(2)}) %collective-permute-start.3) | collective-permute-done | bytes 213024 | tf_op jit(solution)/shard_map/ppermute | solution.py:184
  53.7 4.0 collective-permute-start.11
  70.6 10.9 %collective-permute-done.10.refs_2_ = bf16[64,2048]{1,0:T(8,128)(2,1)} collective-permute-done((bf16[64,2048]{1,0:T(8,128)(2,1)}, bf16[64,2048]{1,0:T(8,128)(2,1)}, u32[]{:S(2)}, u32[]{:S(2)}) %collective-permute-start.10) | collective-permute-done | bytes 262176 | tf_op jit(solution)/shard_map/ppermute | solution.py:70
  87.7 4.4 %assemble.2 = bf16[4,4,64,1664]{3,2,1,0:T(8,128)(2,1)} custom-call(s32[1]{0:T(128)} %bitcast.9.me, bf16[4,64,1664]{2,1,0:T(8,128)(2,1)} %copy-done.33, bf16[4,64,1664]{2,1,0:T(8,128)(2,1)} %collective-permute-done.5.by_x.refs_1_, bf16[4,64,1664]{2,1,0:T(8,128)(2,1)} %copy-done.30, bf16[4,32,1664]{2,1,0:T(8,128)(2,1)} %copy-done.31, ...), custom_call_target="tpu_custom_call" | custom-call | tf_op jit(solution)/shard_map/assemble/pallas_call | solution.py:159
  96.8 5.7 %project.1 = (bf16[1280,1536]{1,0:T(8,128)(2,1)S(1)}, bf16[1024,1280]{1,0:T(8,128)(2,1)S(1)}, f32[8,1024]{1,0:T(8,128)S(1)}) custom-call(f32[1280,1024]{1,0:T(8,128)S(1)} %copy-done.2, bf16[1024,1664]{1,0:T(8,128)(2,1)S(1)} %bitcast.79), custom_call_target="tpu_custom_call" | custom-call | flops 4026531840 | bytes 26214400 | tf_op jit(solution)/shard_map/project/pallas_call | solution.py:633
  105.8 20.7 %attend.2 = (bf16[1280,512]{1,0:T(8,128)(2,1)}, bf16[8,5,1280,256]{3,2,1,0:T(8,128)(2,1)}, f32[8,1,1280]{2,1,0:T(1,128)}) custom-call(f32[48,8]{1,0:T(8,128)} %convert_element_type.153.table, bf16[1280,1536]{1,0:T(8,128)(2,1)} %copy-done.29, bf16[1280,1536]{1,0:T(8,128)(2,1)} %copy-done.29, bf16[1280,1536]{1,0:T(8,128)(2,1)} %copy-done.29, ...), custom_call_target="tpu_custom_call" | custom-call | flops 80530636800 | bytes 13107200 | tf_op jit(solution)/shard_map/attend/pallas_call | solution.py:269
  132.0 21.0 %attend.3 = (bf16[1280,512]{1,0:T(8,128)(2,1)}, bf16[8,5,1280,256]{3,2,1,0:T(8,128)(2,1)}, f32[8,1,1280]{2,1,0:T(1,128)}) custom-call(f32[48,8]{1,0:T(8,128)} %convert_element_type.153.table, bf16[1280,1536]{1,0:T(8,128)(2,1)} %copy-done.29, bf16[1280,1536]{1,0:T(8,128)(2,1)} %copy-done.29, ...), custom_call_target="tpu_custom_call", output_to_operand_aliasing={{0}: (6, {}), {1}: (7, {}), {2}: (8, {})} | custom-call | flops 80530636800 | bytes 13107200 | tf_op jit(solution)/shard_map/attend/pallas_call | solution.py:269
  153.8 4.8 %assemble.3 = (bf16[4,4,64,512]{3,2,1,0:T(8,128)(2,1)}, bf16[4,4,64,1536]{3,2,1,0:T(8,128)(2,1)}) custom-call(s32[1]{0:T(128)} %bitcast.9.me, bf16[4,64,2048]{2,1,0:T(8,128)(2,1)} %tie.12.own, bf16[4,64,2048]{2,1,0:T(8,128)(2,1)} %copy-done.34, bf16[4,64,2048]{2,1,0:T(8,128)(2,1)} %copy-done.35, bf16[4,32,2048]{2,1,0:T(8,128)(2,1)} %copy-done.52, ...), custom_call_target="tpu_custom_call" | custom-call | tf_op jit(solution)/shard_map/assemble/pallas_call | solution.py:159
  173.7 18.3 %ffn_first.1 = (bf16[1280,1024]{1,0:T(8,128)(2,1)}, bf16[1280,1024]{1,0:T(8,128)(2,1)}, bf16[1024,1536]{1,0:T(8,128)(2,1)}) custom-call(bf16[1280,1024]{1,0:T(8,128)(2,1)} %copy-done.28, bf16[1280,1024]{1,0:T(8,128)(2,1)} %copy-done.9, bf16[1024,1536]{1,0:T(8,128)(2,1)} %bitcast.105), custom_call_target="tpu_custom_call" | custom-call | flops 12079595520 | bytes 16777216 | tf_op jit(solution)/shard_map/ffn_first/pallas_call | solution.py:536
  192.3 33.5 %ffn_last.1 = (bf16[1280,1024]{1,0:T(8,128)(2,1)}, bf16[1280,1024]{1,0:T(8,128)(2,1)}, bf16[1024,2688]{1,0:T(8,128)(2,1)}) custom-call(bf16[1280,1024]{1,0:T(8,128)(2,1)} %copy-done.28, bf16[1280,1024]{1,0:T(8,128)(2,1)} %copy-done.9, bf16[1024,2688]{1,0:T(8,128)(2,1)} %all-gather.2.cloned.1.call-done.w_in, bf16[1280,1024]{1,0:T(8,128)(2,1)} %get-tuple-element.64.refs_0_, ...), custom_call_target="tpu_custom_call" | custom-call | flops 21139292160 | bytes 21495808 | tf_op jit(solution)/shard_map/ffn_last/pallas_call | solution.py:536
  238.0 5.9 %after_ffn.1 = (bf16[1280,1024]{1,0:T(8,128)(2,1)S(1)}, bf16[1280,512]{1,0:T(8,128)(2,1)S(1)}, bf16[1024,512]{1,0:T(8,128)(2,1)S(1)}) custom-call(f32[1280,1024]{1,0:T(8,128)S(1)} %copy-done.6, bf16[1280,1024]{1,0:T(8,128)(2,1)S(1)} %copy-done.20, bf16[1280,1024]{1,0:T(8,128)(2,1)S(1)} %collective-permute-done.20.other, bf16[1280,1024]{1,0:T(8,128)(2,1)S(1)} %copy-done.10, ...), custom_call_target="tpu_custom_call" | custom-call | flops 2684354560 | bytes 26214400 | tf_op jit(solution)/shard_map/after_ffn/pallas_call | solution.py:633
  247.5 3.9 all-to-all-start
  251.4 23.6 %attend_back.2 = (bf16[1280,256]{1,0:T(8,128)(2,1)}, bf16[1280,256]{1,0:T(8,128)(2,1)}, bf16[1280,256]{1,0:T(8,128)(2,1)}, f32[4,16,256]{2,1,0:T(8,128)}, f32[4,1,768]{2,1,0:T(1,128)}) custom-call(bf16[1280,1536]{1,0:T(8,128)(2,1)} %copy-done.29, bf16[1280,1536]{1,0:T(8,128)(2,1)} %copy-done.29, bf16[1280,1536]{1,0:T(8,128)(2,1)} %copy-done.29, ...), custom_call_target="tpu_custom_call" | custom-call | flops 13421772800 | bytes 13107200 | tf_op jit(solution)/shard_map/attend_back/pallas_call | solution.py:410
  275.9 8.9 %project_back.2 = (bf16[1280,1024]{1,0:T(8,128)(2,1)}, bf16[4,256,1280]{2,1,0:T(8,128)(2,1)}) custom-call(bf16[1024,1280]{1,0:T(8,128)(2,1)} %copy-done.8, bf16[1280,256]{1,0:T(8,128)(2,1)} %get-tuple-element.72.refs_0_, bf16[1280,256]{1,0:T(8,128)(2,1)} %get-tuple-element.73.refs_1_, bf16[1280,256]{1,0:T(8,128)(2,1)} %get-tuple-element.74.refs_2_, ...), custom_call_target="tpu_custom_call" | custom-call | flops 4026531840 | bytes 8388608 | tf_op jit(solution)/shard_map/project_back/pallas_call | solution.py:593
  284.8 3.7 all-to-all-start.1
  288.7 23.7 %attend_back.3 = (bf16[1280,256]{1,0:T(8,128)(2,1)}, bf16[1280,256]{1,0:T(8,128)(2,1)}, bf16[1280,256]{1,0:T(8,128)(2,1)}, f32[4,16,256]{2,1,0:T(8,128)}, f32[4,1,768]{2,1,0:T(1,128)}) custom-call(bf16[1280,1536]{1,0:T(8,128)(2,1)} %copy-done.29, bf16[1280,1536]{1,0:T(8,128)(2,1)} %copy-done.29, bf16[1280,1536]{1,0:T(8,128)(2,1)} %copy-done.29, ...), custom_call_target="tpu_custom_call" | custom-call | flops 13421772800 | bytes 13107200 | tf_op jit(solution)/shard_map/attend_back/pallas_call | solution.py:410
  315.3 8.9 %project_back.3 = (bf16[1280,1024]{1,0:T(8,128)(2,1)}, bf16[4,272,768]{2,1,0:T(8,128)(2,1)}) custom-call(bf16[1024,1280]{1,0:T(8,128)(2,1)} %copy-done.8, bf16[1280,256]{1,0:T(8,128)(2,1)} %get-tuple-element.78.refs_0_, bf16[1280,256]{1,0:T(8,128)(2,1)} %get-tuple-element.79.refs_1_, bf16[1280,256]{1,0:T(8,128)(2,1)} %get-tuple-element.80.refs_2_, ...), custom_call_target="tpu_custom_call" | custom-call | flops 4026531840 | bytes 8388608 | tf_op jit(solution)/shard_map/project_back/pallas_call | solution.py:593
  343.4 7.3 %result.1 = (bf16[1024,1024]{1,0:T(8,128)(2,1)}, bf16[208,1024]{1,0:T(8,128)(2,1)S(1)}) custom-call(s32[1]{0:T(128)} %dynamic_slice.46.count, f32[1280,1024]{1,0:T(8,128)S(1)} %copy-done.7, bf16[1280,1024]{1,0:T(8,128)(2,1)S(1)} %copy-done.19, bf16[1280,1024]{1,0:T(8,128)(2,1)} %collective-permute-done.19.other, bf16[1280,208]{1,0:T(8,128)(2,1)S(1)} %fusion.3.spread.pick, ...), custom_call_target="tpu_custom_call" | custom-call | flops 545259520 | bytes 26214400 | tf_op jit(solution)/shard_map/result/pallas_call | solution.py:633
  350.7 4.0 collective-permute-done.25
  356.6 8.2 %last.1 = (bf16[1024,1024]{1,0:T(8,128)(2,1)}, bf16[208,1024]{1,0:T(8,128)(2,1)S(1)}) custom-call(s32[1]{0:T(128)} %dynamic_slice.46.count, f32[1280,1024]{1,0:T(8,128)S(1)} %bitcast.83, bf16[1280,1024]{1,0:T(8,128)(2,1)S(1)} %copy-done.4, bf16[1280,1024]{1,0:T(8,128)(2,1)} %collective-permute-done.21.other, bf16[1280,1024]{1,0:T(8,128)(2,1)S(1)} %copy-done.18, ...), custom_call_target="tpu_custom_call" | custom-call | flops 1090519040 | bytes 26214400 | tf_op jit(solution)/shard_map/last/pallas_call | solution.py:633
  373.6 22.6 %collective-permute-done.22 = bf16[104,2048]{1,0:T(8,128)(2,1)S(1)} collective-permute-done((bf16[104,2048]{1,0:T(8,128)(2,1)S(1)}, bf16[104,2048]{1,0:T(8,128)(2,1)S(1)}, u32[]{:S(2)}, u32[]{:S(2)}) %collective-permute-start.22) | collective-permute-done | bytes 426016 | tf_op jit(solution)/shard_map/ppermute | solution.py:184
  396.2 5.1 %collective-permute-done.28 = bf16[80,768]{1,0:T(8,128)(2,1)S(1)} collective-permute-done((bf16[80,768]{1,0:T(8,128)(2,1)S(1)}, bf16[80,768]{1,0:T(8,128)(2,1)S(1)}, u32[]{:S(2)}, u32[]{:S(2)}) %collective-permute-start.28) | collective-permute-done | bytes 122912 | tf_op jit(solution)/shard_map/ppermute | solution.py:118
  (331 shorter events, 136.9 us)
Async XLA Ops:
  8.0 184.2 %all-gather.2.cloned.1.call-start = ((), (), s32[]{:S(2)}) async-start(), calls=%async_computation.5 | async-start | bytes 5849088 | tf_op jit(solution)/shard_map/all_gather | solution.py:906
  29.7 23.1 %collective-permute-start.5 = (bf16[4,64,1664]{2,1,0:T(8,128)(2,1)S(1)}, bf16[4,64,1664]{2,1,0:T(8,128)(2,1)}, u32[]{:S(2)}, u32[]{:S(2)}) collective-permute-start(bf16[4,64,1664]{2,1,0:T(8,128)(2,1)S(1)} %pad_maximum_fusion.2.own), channel_id=1, source_target_pairs={{0,2},{2,0},{4,6},{6,4},{8,10},{10,8},{12,14},{14,12},{16,18},{18,... | collective-permute-start | bytes 2555912 | tf_op jit(solution)/shard_map/ppermute | solution.py:70
  31.2 21.6 %collective-permute-start.6 = (bf16[4,64,1664]{2,1,0:T(8,128)(2,1)S(1)}, bf16[4,64,1664]{2,1,0:T(8,128)(2,1)S(1)}, u32[]{:S(2)}, u32[]{:S(2)}) collective-permute-start(bf16[4,64,1664]{2,1,0:T(8,128)(2,1)S(1)} %pad_maximum_fusion.2.own), channel_id=1, source_target_pairs={{0,4},{2,6},{4,0},{6,2},{8,12},{10,14},{12,8},{14,10},{16,20},{18,... | collective-permute-start | bytes 2555912 | tf_op jit(solution)/shard_map/ppermute | solution.py:70
  57.7 23.8 %collective-permute-start.10 = (bf16[64,2048]{1,0:T(8,128)(2,1)}, bf16[64,2048]{1,0:T(8,128)(2,1)}, u32[]{:S(2)}, u32[]{:S(2)}) collective-permute-start(bf16[64,2048]{1,0:T(8,128)(2,1)} %tie.11), channel_id=1, source_target_pairs={{0,16},{2,18},{4,20},{6,22},{8,24},{10,26},{12,28},{14,30},{16,0},... | collective-permute-start | bytes 786440 | tf_op jit(solution)/shard_map/ppermute | solution.py:70
  59.2 22.3 %collective-permute-start.9 = (bf16[64,2048]{1,0:T(8,128)(2,1)}, bf16[64,2048]{1,0:T(8,128)(2,1)}, u32[]{:S(2)}, u32[]{:S(2)}) collective-permute-start(bf16[64,2048]{1,0:T(8,128)(2,1)} %tie.11), channel_id=1, source_target_pairs={{0,8},{2,10},{4,12},{6,14},{8,16},{10,18},{12,20},{14,22},{16,24},... | collective-permute-start | bytes 786440 | tf_op jit(solution)/shard_map/ppermute | solution.py:70
  61.0 24.4 %collective-permute-start.7 = (bf16[4,32,1664]{2,1,0:T(8,128)(2,1)}, bf16[4,32,1664]{2,1,0:T(8,128)(2,1)S(1)}, u32[]{:S(2)}, u32[]{:S(2)}) collective-permute-start(bf16[4,32,1664]{2,1,0:T(8,128)(2,1)} %tie.10), channel_id=1, source_target_pairs={{0,2},{2,0},{4,6},{6,4},{8,10},{10,8},{12,14},{14,12},{16,18},{18,... | collective-permute-start | bytes 1277960 | tf_op jit(solution)/shard_map/ppermute | solution.py:70
  63.4 22.0 %collective-permute-start.8 = (bf16[4,32,1664]{2,1,0:T(8,128)(2,1)}, bf16[4,32,1664]{2,1,0:T(8,128)(2,1)}, u32[]{:S(2)}, u32[]{:S(2)}) collective-permute-start(bf16[4,32,1664]{2,1,0:T(8,128)(2,1)} %slice.239), channel_id=1, source_target_pairs={{0,4},{2,6},{4,0},{6,2},{8,12},{10,14},{12,8},{14,10},{16,20},{18,... | collective-permute-start | bytes 1277960 | tf_op jit(solution)/shard_map/ppermute | solution.py:70
  81.5 24.3 %collective-permute-start.14 = (bf16[104,1024]{1,0:T(8,128)(2,1)}, bf16[104,1024]{1,0:T(8,128)(2,1)S(1)}, u32[]{:S(2)}, u32[]{:S(2)}) collective-permute-start(bf16[104,1024]{1,0:T(8,128)(2,1)} %tie.13), channel_id=1, source_target_pairs={{0,16},{2,18},{4,20},{6,22},{8,24},{10,26},{12,28},{14,30},{16,0},... | collective-permute-start | bytes 638984 | tf_op jit(solution)/shard_map/ppermute | solution.py:184
  86.2 43.4 %collective-permute-start.12 = (bf16[4,64,2048]{2,1,0:T(8,128)(2,1)}, bf16[4,64,2048]{2,1,0:T(8,128)(2,1)S(1)}, u32[]{:S(2)}, u32[]{:S(2)}) collective-permute-start(bf16[4,64,2048]{2,1,0:T(8,128)(2,1)} %tie.12.own), channel_id=1, source_target_pairs={{0,2},{2,0},{4,6},{6,4},{8,10},{10,8},{12,14},{14,12},{16,18},{18,... | collective-permute-start | bytes 3145736 | tf_op jit(solution)/shard_map/ppermute | solution.py:70
  86.7 40.6 %collective-permute-start.13 = (bf16[4,64,2048]{2,1,0:T(8,128)(2,1)}, bf16[4,64,2048]{2,1,0:T(8,128)(2,1)S(1)}, u32[]{:S(2)}, u32[]{:S(2)}) collective-permute-start(bf16[4,64,2048]{2,1,0:T(8,128)(2,1)} %tie.12.own), channel_id=1, source_target_pairs={{0,4},{2,6},{4,0},{6,2},{8,12},{10,14},{12,8},{14,10},{16,20},{18,... | collective-permute-start | bytes 3145736 | tf_op jit(solution)/shard_map/ppermute | solution.py:70
  87.4 160.0 %reduce-scatter.4.cloned.1.call-start = ((), (), s32[]{:S(2)}) async-start(), calls=%async_computation.6 | async-start | bytes 3932160 | tf_op jit(solution)/shard_map/reduce_scatter | solution.py:925
  105.8 20.7 %collective-permute-start.15 = (bf16[104,1024]{1,0:T(8,128)(2,1)S(1)}, bf16[104,1024]{1,0:T(8,128)(2,1)S(1)}, u32[]{:S(2)}, u32[]{:S(2)}) collective-permute-start(bf16[104,1024]{1,0:T(8,128)(2,1)S(1)} %collective-permute-done.14), channel_id=1, source_target_pairs={{0,1},{1,0},{2,3},{3,2},{4,5},{5,4},{6,7},{7,6},{8,9},{9,8},{10,11... | collective-permute-start | bytes 638984 | tf_op jit(solution)/shard_map/ppermute | solution.py:175
  128.2 24.7 %collective-permute-start.16 = (bf16[4,32,2048]{2,1,0:T(8,128)(2,1)}, bf16[4,32,2048]{2,1,0:T(8,128)(2,1)S(1)}, u32[]{:S(2)}, u32[]{:S(2)}) collective-permute-start(bf16[4,32,2048]{2,1,0:T(8,128)(2,1)} %slice.240), channel_id=1, source_target_pairs={{0,2},{2,0},{4,6},{6,4},{8,10},{10,8},{12,14},{14,12},{16,18},{18,... | collective-permute-start | bytes 1572872 | tf_op jit(solution)/shard_map/ppermute | solution.py:70
  130.5 23.2 %collective-permute-start.17 = (bf16[4,32,2048]{2,1,0:T(8,128)(2,1)}, bf16[4,32,2048]{2,1,0:T(8,128)(2,1)}, u32[]{:S(2)}, u32[]{:S(2)}) collective-permute-start(bf16[4,32,2048]{2,1,0:T(8,128)(2,1)} %slice.241), channel_id=1, source_target_pairs={{0,4},{2,6},{4,0},{6,2},{8,12},{10,14},{12,8},{14,10},{16,20},{18,... | collective-permute-start | bytes 1572872 | tf_op jit(solution)/shard_map/ppermute | solution.py:70
  192.0 135.9 %reduce-scatter.6.cloned.1.call-start = ((), (), s32[]{:S(2)}) async-start(), calls=%async_computation.7 | async-start | bytes 6881280 | tf_op jit(solution)/shard_map/reduce_scatter | solution.py:925
  227.6 109.0 %collective-permute-start.19 = (bf16[1280,1024]{1,0:T(8,128)(2,1)}, bf16[1280,1024]{1,0:T(8,128)(2,1)}, u32[]{:S(2)}, u32[]{:S(2)}) collective-permute-start(bf16[1280,1024]{1,0:T(8,128)(2,1)} %get-tuple-element.66.own), channel_id=1, source_target_pairs={{0,1},{1,0},{2,3},{3,2},{4,5},{5,4},{6,7},{7,6},{8,9},{9,8},{10,11... | collective-permute-start | bytes 7864328 | tf_op jit(solution)/shard_map/ppermute | solution.py:175
  247.5 27.6 %all-to-all-start = ((bf16[4,64,1536]{2,1,0:T(8,128)(2,1)}), bf16[4,64,1536]{2,1,0:T(8,128)(2,1)S(1)}, u32[]{:S(2)}, u32[]{:S(2)}) async-start(bf16[4,64,1536]{2,1,0:T(8,128)(2,1)} %bitcast.88), calls=%async_computation.1 | async-start | bytes 1572864 | tf_op jit(solution)/shard_map/all_to_all | solution.py:102
  284.8 42.0 %all-to-all-start.1 = ((bf16[4,256,1280]{2,1,0:T(8,128)(2,1)}), bf16[4,256,1280]{2,1,0:T(8,128)(2,1)S(1)}, u32[]{:S(2)}, u32[]{:S(2)}) async-start(bf16[4,256,1280]{2,1,0:T(8,128)(2,1)} %get-tuple-element.92), calls=%async_computation.3 | async-start | bytes 5242880 | tf_op jit(solution)/shard_map/all_to_all | solution.py:102
  288.4 116.0 %reduce-scatter.8.cloned.1.call-start = ((), (), s32[]{:S(2)}) async-start(), calls=%async_computation.8 | async-start | bytes 2539520 | tf_op jit(solution)/shard_map/reduce_scatter | solution.py:925
  324.2 32.3 %collective-permute-start.21 = (bf16[1280,1024]{1,0:T(8,128)(2,1)}, bf16[1280,1024]{1,0:T(8,128)(2,1)}, u32[]{:S(2)}, u32[]{:S(2)}) collective-permute-start(bf16[1280,1024]{1,0:T(8,128)(2,1)} %get-tuple-element.85.refs_0_.own.refs_1_), channel_id=1, source_target_pairs={{0,1},{1,0},{2,3},{3,2},{4,5},{5,4},{6,7},{7,6},{8,9},{9,8},{10,11... | collective-permute-start | bytes 7864328 | tf_op jit(solution)/shard_map/ppermute | solution.py:175
  364.8 31.3 %collective-permute-start.22 = (bf16[104,2048]{1,0:T(8,128)(2,1)S(1)}, bf16[104,2048]{1,0:T(8,128)(2,1)S(1)}, u32[]{:S(2)}, u32[]{:S(2)}) collective-permute-start(bf16[104,2048]{1,0:T(8,128)(2,1)S(1)} %fusion.14), channel_id=1, source_target_pairs={{0,16},{2,18},{4,20},{6,22},{8,24},{10,26},{12,28},{14,30},{16,0},... | collective-permute-start | bytes 1277960 | tf_op jit(solution)/shard_map/ppermute | solution.py:184
  369.1 27.2 %collective-permute-start.29 = (bf16[80,768]{1,0:T(8,128)(2,1)S(1)}, bf16[80,768]{1,0:T(8,128)(2,1)S(1)}, u32[]{:S(2)}, u32[]{:S(2)}) collective-permute-start(bf16[80,768]{1,0:T(8,128)(2,1)S(1)} %get-tuple-element.164), channel_id=1, source_target_pairs={{0,24},{8,16},{16,8},{24,0},{2,26},{10,18},{18,10},{26,2},{4,28},{... | collective-permute-start | bytes 368648 | tf_op jit(solution)/shard_map/ppermute | solution.py:118
  370.6 30.8 %collective-permute-start.28 = (bf16[80,768]{1,0:T(8,128)(2,1)S(1)}, bf16[80,768]{1,0:T(8,128)(2,1)S(1)}, u32[]{:S(2)}, u32[]{:S(2)}) collective-permute-start(bf16[80,768]{1,0:T(8,128)(2,1)S(1)} %get-tuple-element.165), channel_id=1, source_target_pairs={{0,16},{8,24},{16,0},{24,8},{2,18},{10,26},{18,2},{26,10},{4,20},{... | collective-permute-start | bytes 368648 | tf_op jit(solution)/shard_map/ppermute | solution.py:118
  372.1 29.3 %collective-permute-start.27 = (bf16[80,768]{1,0:T(8,128)(2,1)S(1)}, bf16[80,768]{1,0:T(8,128)(2,1)S(1)}, u32[]{:S(2)}, u32[]{:S(2)}) collective-permute-start(bf16[80,768]{1,0:T(8,128)(2,1)S(1)} %get-tuple-element.163), channel_id=1, source_target_pairs={{0,8},{8,0},{16,24},{24,16},{2,10},{10,2},{18,26},{26,18},{4,12},{... | collective-permute-start | bytes 368648 | tf_op jit(solution)/shard_map/ppermute | solution.py:118
  (91 other events, 692.4 us)
Sparse Core Ops, SparseCore 0:
  87.5 89.8 all-gather.1
  331.0 45.2 reduce-scatter.7
Sparse Core Ops, SparseCore 1:
  192.1 41.7 reduce-scatter.3
  236.8 84.6 reduce-scatter.5

commit v3 on v2

--- a/solution.py
+++ b/solution.py
@@ -22,9 +22,8 @@
 DEAD = 206
 FEAT_ROWS = 208
 MASKED = -1e30
-VMEM = 60 * 1024 * 1024
 ATTEND_WEIGHT = 4
-ROW_VMEM = 24 * 1024 * 1024
+STREAMED = ("after_ffn", "result", "last")
 F32 = jnp.float32
 BF16 = jnp.bfloat16
 
@@ -41,8 +40,8 @@
     return lax.dot_general(left, right, (((0,), (0,)), ((), ())), preferred_element_type=F32)
 
 
-def params(**more):
-    return pltpu.CompilerParams(vmem_limit_bytes=VMEM, **more)
+def params(mebibytes):
+    return pltpu.CompilerParams(vmem_limit_bytes=mebibytes * 1024 * 1024)
 
 
 def grid_of(devices):
@@ -69,30 +68,20 @@
             route.append((i, i + ((c + distance) % size - c) * stride))
         return lax.ppermute(block, "dp", route)
 
-    def gather_rows(self, block, fast, cuts, after=(), plane_after=(), aside=None):
+    def gather_rows(self, block, after=(), plane_after=(), aside=None):
         block = tie(block, *after)
         if self.sizes[1:] != (2, 2):
             whole = lax.all_gather(block, "dp", axis=0, tiled=True)
-            ends = [sum(cuts[: i + 1]) for i in range(len(cuts))]
-            whole = [whole[:, end - cut : end] for cut, end in zip(cuts, ends)]
-            return whole, (block,), (block,), (block,)
+            return (whole,), (block,), (block,), (block,)
         half = block.shape[0] // 2
-        size = self.sizes[0]
-        if fast:
-            layers = tuple(self.send(block, 0, k) for k in range(1, size))
-            own = jnp.stack((block,) + layers)
-        else:
-            copies = jnp.concatenate([block] * size)
-            own = lax.all_to_all(copies, "dp", 0, 0, axis_index_groups=self.columns, tiled=True)
-            own = own.reshape((size,) + block.shape)
-            layers = (own,)
+        layers = tuple(self.send(block, 0, k) for k in range(1, self.sizes[0]))
+        own = jnp.stack((block,) + layers)
         own = tie(own, *plane_after)
         by_x, by_y = self.send(own, 2, 1), self.send(own, 1, 1)
         waits = () if aside is None else aside(layers)
         far_top = self.send(tie(by_y[:, :half], *waits), 2, 1)
         far_low = self.send(by_x[:, half:], 1, 1)
-        whole = assemble(self.me, size, fast, cuts, own, by_x, by_y, far_top, far_low)
-        return whole, layers, (by_x, by_y), (far_top, far_low)
+        return (own, by_x, by_y, far_top, far_low), layers, (by_x, by_y), (far_top, far_low)
 
     def order(self, rows):
         part = rows // self.count
@@ -108,10 +97,10 @@
         return total
 
 
-    def trade(self, block, groups):
+    def trade(self, block, groups, after=()):
         count = block.shape[0]
         at = self.me % self.plane if groups is self.planes else self.me // self.plane
-        total = lax.dynamic_index_in_dim(block, at, 0, keepdims=False).astype(F32)
+        total = tie(lax.dynamic_index_in_dim(block, at, 0, keepdims=False), *after).astype(F32)
         for k in range(1, count):
             part = lax.dynamic_index_in_dim(block, at ^ k, 0, keepdims=False)
             route = [(g[i], g[i ^ k]) for g in groups for i in range(count)]
@@ -137,38 +126,24 @@
     )(block, *others)
 
 
-def assemble_kernel(me, own, by_x, by_y, far_top, far_low, *outs):
-    y, x = (me[0] // 2) % 2, me[0] % 2
-    half = far_top.shape[1]
-    start = 0
-    for out in outs:
-        cols = slice(start, start + out.shape[3])
-        start = start + out.shape[3]
-        out[0, 2 * y + x] = own[0, :, cols]
-        out[0, 2 * y + 1 - x] = by_x[0, :, cols]
-        out[0, 2 * (1 - y) + x] = by_y[0, :, cols]
-        out[0, 2 * (1 - y) + 1 - x, :half] = far_top[0, :, cols]
-        out[0, 2 * (1 - y) + 1 - x, half:] = far_low[0, :, cols]
-
-
-def assemble(me, layers, turned, cuts, *parts):
-    rows, columns = parts[0].shape[1:]
-    whole = pl.BlockSpec((1, rows, columns), lambda k, me: (k, 0, 0))
-    half = pl.BlockSpec((1, rows // 2, columns), lambda k, me: (k, 0, 0))
-    place = lambda k, me: (lax.rem(me[0] // 4 - k + layers, layers) if turned else k, 0, 0, 0)
-    outs = pl.pallas_call(
-        assemble_kernel,
-        grid_spec=pltpu.PrefetchScalarGridSpec(
-            num_scalar_prefetch=1,
-            grid=(layers,),
-            in_specs=[whole] * 3 + [half] * 2,
-            out_specs=[pl.BlockSpec((1, 4, rows, cut), place) for cut in cuts],
-        ),
-        out_shape=[jax.ShapeDtypeStruct((layers, 4, rows, cut), BF16) for cut in cuts],
-        compiler_params=params(),
-        name="assemble",
-    )(me[None].astype(jnp.int32), *parts)
-    return [out.reshape(4 * layers * rows, out.shape[3]) for out in outs]
+def load_parts(me, parts, columns, target, sems):
+    copy = pltpu.make_async_copy
+    if len(parts) == 1:
+        return [copy(parts[0].at[:, columns], target, sems.at[0])]
+    z, y, x = me[0] // 4, lax.rem(me[0] // 2, 2), lax.rem(me[0], 2)
+    layers, rows = parts[0].shape[:2]
+    places = (2 * y + x, 2 * y + 1 - x, 2 * (1 - y) + x) + (2 * (1 - y) + 1 - x,) * 2
+    copies = []
+    for k in range(layers):
+        layer = lax.rem(z - k + layers, layers)
+        for i, (part, place) in enumerate(zip(parts, places)):
+            start = (layer * 4 + place) * rows + (rows // 2 if i == 4 else 0)
+            rows_at = pl.ds(pl.multiple_of(start, rows // 2), part.shape[1])
+            copies.append(copy(part.at[k, :, columns], target.at[rows_at], sems.at[len(copies)]))
+    return copies
+
+
+PARTS = 20
 
 
 def other_core(block):
@@ -190,9 +165,13 @@
     return jnp.concatenate([jnp.where(first, mine, theirs), jnp.where(first, theirs, mine)], axis=0)
 
 
+SCALAR = pl.BlockSpec(memory_space=pltpu.SMEM)
+
+
 def attend_kernel(first, extra, table, q_ref, k_ref, v_ref, cells_ref, lay_ref, *refs):
-    mix_ref, prob_ref, inv_ref, keys, values, layout, near, *score = refs[extra:]
-    pair = pl.program_id(0) + first
+    mix_ref, prob_to, inv_ref, keys, values, layout, near, prob_ref, sems, *score = refs[extra:]
+    step = pl.program_id(0)
+    pair = step + first
     length = k_ref.shape[0]
     keys[:, :128] = k_ref[...]
     keys[:, 128:] = cells_ref[...]
@@ -240,11 +219,16 @@
         scores = buffer[...]
         top = jnp.max(scores, axis=0, keepdims=True)
         weight = jnp.exp(scores - top).astype(BF16)
-        prob_ref[h, block] = weight
+        prob_ref[step, h, block] = weight
+        out_copy(step, h, block).start()
         summed = nn(values[h], weight)
         inverse = 1.0 / summed[DH : DH + 1]
         inv_ref[h, :, block * BQ : (block + 1) * BQ] = inverse
         return summed[:DH] * inverse
+
+    def out_copy(at, h, block):
+        place = prob_to.at[2 * (first + at) + h, block]
+        return pltpu.make_async_copy(prob_ref.at[at, h, block], place, sems.at[at, h, block])
 
     items = 2 * (length // BQ)
     depth = len(score)
@@ -258,6 +242,12 @@
         if item % 2:
             start = item // 2 * BQ
             mix_ref[start : start + BQ] = jnp.concatenate(mixed[-2:], axis=0).T.astype(BF16)
+
+    @pl.when(step == pl.num_programs(0) - 1)
+    def _():
+        for at in range(prob_ref.shape[0]):
+            for item in range(items):
+                out_copy(at, item % 2, item // 2).wait()
 
 
 def attend(table, projected, cells, lay, first, pairs, width, into=(), after=()):
@@ -280,7 +270,7 @@
         + [anywhere] * extra,
         out_specs=[
             pair_spec(0),
-            pl.BlockSpec((2, blocks, rows, BQ), lambda p: (first + p, 0, 0, 0)),
+            anywhere,
             pl.BlockSpec((2, 1, rows), lambda p: (first + p, 0, 0)),
         ],
         out_shape=[
@@ -294,9 +284,11 @@
             pltpu.VMEM((2, DH + 16, rows), BF16),
             pltpu.VMEM((2, CELLS, CELLS), BF16),
             pltpu.VMEM((2, WIN, BQ), F32),
+            pltpu.VMEM((pairs, 2, blocks, rows, BQ), BF16),
+            pltpu.SemaphoreType.DMA((pairs, 2, blocks)),
         ]
         + [pltpu.VMEM((rows, BQ), F32)] * 3,
-        compiler_params=params(),
+        compiler_params=params(36),
         cost_estimate=pl.CostEstimate(
             flops=2 * 2 * pairs * rows * rows * 512 * 3 * ATTEND_WEIGHT,
             bytes_accessed=2 * 2 * pairs * rows * rows,
@@ -306,13 +298,38 @@
     )(table, projected, projected, projected, cells, lay, *into, *after)
 
 
-def attend_back_kernel(
-    extra, q_ref, k_ref, v_ref, gm_ref, mix_ref, prob_ref, inv_ref, cells_ref, cells_t_ref, lay_ref, *refs
+def heads_back_kernel(
+    order, first, starts, q_ref, k_ref, v_ref, gm_ref, mix_ref, inv_ref, cells_ref, cells_t_ref, lay_ref,
+    table_in, prob_from, rows_from, weights_from, more_from, *refs
 ):
-    gq_ref, gk_ref, gv_ref, lay_out, rel_out = refs[extra : extra + 5]
-    left, queries, grads, query_acc, key_acc, value_acc, by_cell, near_acc, *buffers = refs[extra + 5 :]
+    out_to, sums_to, table_ref = refs[-23:-20]
+    left, queries, grads, query_acc, key_acc, value_acc, by_cell, near_acc = refs[-20:-12]
+    prob_ref, found, rows_t, weights, more, out, sums, prob_sems, sems = refs[-12:-3]
+    buffers = refs[-3:]
+    step = pl.program_id(0)
+    copy = pltpu.make_async_copy
     length = k_ref.shape[0]
     blocks = length // BQ
+    half = found.shape[2]
+
+    def prob_copy(at, h, block):
+        place = prob_from.at[2 * (first + at) + h, block]
+        return copy(place, prob_ref.at[at, h, block], prob_sems.at[at, h, block])
+
+    loads = [copy(rows_from, rows_t, sems.at[0]), copy(more_from, more, sems.at[1])] + [
+        copy(weights_from.at[:, start : start + half], weights.at[i], sems.at[2 + i])
+        for i, start in enumerate(starts)
+    ]
+
+    @pl.when(step == 0)
+    def _():
+        for at in range(prob_ref.shape[0]):
+            for item in range(2 * blocks):
+                prob_copy(at, item % 2, item // 2).start()
+        for load in loads:
+            load.start()
+        table_ref[...] = table_in[...]
+
     keys_t = k_ref[...].astype(F32).T.astype(BF16)
     queries[...] = q_ref[...].astype(F32).T.astype(BF16)
     grad_mix = gm_ref[...].astype(F32)
@@ -339,7 +356,8 @@
         start = block * BQ
         cols = slice(start, start + BQ)
         own = slice(h * DH, (h + 1) * DH)
-        prob = prob_ref[h, block]
+        prob_copy(step, h, block).wait()
+        prob = prob_ref[step, h, block]
         grad_score = (prob.astype(F32) * (buffer[...] - inner[h][:, cols])).astype(BF16)
         both = nn(left[h], grad_score)
         query_acc[own, cols] = both[:DH]
@@ -374,19 +392,23 @@
             fill(item + depth - 1, buffers[(item + depth - 1) % depth])
         use(item, buffers[item % depth])
 
-    gq_ref[...] = (query_acc[...].T * DH ** (-0.5)).astype(BF16)
-    gk_ref[...] = (key_acc[...].T * DH ** (-0.5)).astype(BF16)
-    gv_ref[...] = value_acc[...].T.astype(BF16)
+    place = pl.ds(pl.multiple_of(step * 128, 128), 128)
+    found[0, :, place] = (query_acc[...].T * DH ** (-0.5)).astype(BF16)
+    found[1, :, place] = (key_acc[...].T * DH ** (-0.5)).astype(BF16)
+    found[2, :, place] = value_acc[...].T.astype(BF16)
     turn = lax.broadcasted_iota(jnp.int32, (BQ, BQ), 0) + lax.broadcasted_iota(jnp.int32, (BQ, BQ), 1)
     turn = (turn == BQ - 1).astype(BF16)
     column = lax.broadcasted_iota(jnp.int32, (1, BQ + WIN), 1)
+    bucket = jnp.clip(column - (BQ - 1 + PAD), -(RB // 2), RB // 2 - 1) + RB // 2
+    lower = lax.broadcasted_iota(jnp.int32, (16, 1), 0)
+    table_lane = lax.broadcasted_iota(jnp.int32, (1, 128), 1)
     lay = lay_ref[:FEAT_ROWS]
     for h in range(2):
         pairs = nn(by_cell[h], cells_ref[...])
-        sums = [
+        bucket_sums = [
             jnp.sum(jnp.where(lay == b, pairs, 0.0), axis=0, keepdims=True) for b in range(LQ * LQ)
         ]
-        lay_out[h] = jnp.concatenate(sums, axis=0)
+        lay_part = jnp.sum(jnp.concatenate(bucket_sums, axis=0), axis=1, keepdims=True)
         band = near_acc[h]
         high = band.astype(BF16)
         low = (band - high.astype(F32)).astype(BF16)
@@ -396,94 +418,143 @@
         rel = jnp.sum(band, axis=0, keepdims=True)
         rel = rel + jnp.where(column == 0, jnp.sum(sum(far_left[h]), axis=1, keepdims=True), 0.0)
         last = column == BQ + WIN - 1
-        rel_out[h] = rel + jnp.where(last, jnp.sum(sum(far_right[h]), axis=1, keepdims=True), 0.0)
-
-
-def attend_back(projected, grad_mix, mixture, probs, inverse, cells, cells_t, lay, first, pairs, after=()):
+        rel = rel + jnp.where(last, jnp.sum(sum(far_right[h]), axis=1, keepdims=True), 0.0)
+        head = 2 * (first + step) + h
+        for t, part in enumerate(
+            (
+                jnp.sum(jnp.where(bucket == lower, rel, 0.0), axis=1, keepdims=True),
+                jnp.sum(jnp.where(bucket == lower + 16, rel, 0.0), axis=1, keepdims=True),
+                lay_part,
+            )
+        ):
+            table_ref[...] += jnp.where(table_lane == t * 16 + head, part, 0.0)
+
+    @pl.when(step == pl.num_programs(0) - 1)
+    def _():
+        for load in loads:
+            load.wait()
+        result = nt(found[0], weights[0]) + nt(found[1], weights[1]) + nt(found[2], weights[2])
+        if first:
+            result = result + more[...].astype(F32)
+        out[...] = result.astype(BF16)
+        store = copy(out, out_to, sems.at[0])
+        store.start()
+        model = rows_t.shape[0]
+        part = model // len(order)
+        places = sums.shape[0]
+        chunk = model // places
+        for i in range(3):
+            grad = nn(rows_t[...], found[i]).astype(BF16)
+            for k, start in enumerate(order):
+                place, at = divmod(k * part, chunk)
+                sums[place, at : at + part, i * half : (i + 1) * half] = grad[start : start + part]
+        if first:
+            high = table_ref[...].astype(BF16)
+            low = (table_ref[...] - high.astype(F32)).astype(BF16)
+            rest = jnp.zeros((16, 3 * half - 256), BF16)
+            for place in range(places):
+                sums[place, chunk:] = jnp.concatenate([high, low, rest], axis=1)
+        else:
+            for place in range(places):
+                sums[place, :, 3 * half :] = more[place * chunk : (place + 1) * chunk]
+        last_store = copy(sums, sums_to, sems.at[1])
+        last_store.start()
+        store.wait()
+        last_store.wait()
+
+
+def heads_back(
+    projected, grad_mix, mixture, probs, inverse, cells, cells_t, lay, rows_t, weights, first, pairs, order, plane,
+    table, more, after=()
+):
     rows, width = grad_mix.shape
-    blocks, all_pairs = rows // BQ, width // 128
+    model = rows_t.shape[0]
+    blocks, all_pairs, half = rows // BQ, width // 128, 128 * pairs
     pair_spec = lambda i: pl.BlockSpec((rows, 128), lambda p: (0, i * all_pairs + first + p))
-    out_spec = pl.BlockSpec((rows, 128), lambda p: (0, p))
-    small = lambda *shape: pl.BlockSpec((2,) + shape, lambda p: (p, 0, 0))
     whole = lambda *shape: pl.BlockSpec(shape, lambda p: (0, 0))
-    wide = jax.ShapeDtypeStruct((rows, 128 * pairs), BF16)
+    anywhere = pl.BlockSpec(memory_space=pl.ANY)
+    if first:
+        shape = (plane, model // plane + 16, 3 * half)
+    else:
+        shape = (plane, model // plane, 3 * half + more.shape[1])
+    vmem = lambda *shape: pltpu.VMEM(shape, BF16)
+    starts = [i * width + 128 * first for i in range(3)]
     return pl.pallas_call(
-        functools.partial(attend_back_kernel, len(after)),
+        functools.partial(heads_back_kernel, order, first, starts),
         grid=(pairs,),
         in_specs=[pair_spec(0), pair_spec(1), pair_spec(2), pair_spec(0), pair_spec(0)]
         + [
-            pl.BlockSpec((2, blocks, rows, BQ), lambda p: (first + p, 0, 0, 0)),
             pl.BlockSpec((2, 1, rows), lambda p: (first + p, 0, 0)),
             whole(rows, CELLS),
             whole(FEAT_ROWS, rows),
             whole(CELLS, CELLS),
+            whole(16, 128),
         ]
-        + [pl.BlockSpec(memory_space=pl.ANY)] * len(after),
-        out_specs=[out_spec] * 3 + [small(LQ * LQ, CELLS), small(1, BQ + WIN)],
+        + [anywhere] * (4 + len(after)),
+        out_specs=[anywhere, anywhere, whole(16, 128)],
         out_shape=[
-            wide,
-            wide,
-            wide,
-            jax.ShapeDtypeStruct((2 * pairs, LQ * LQ, CELLS), F32),
-            jax.ShapeDtypeStruct((2 * pairs, 1, BQ + WIN), F32),
+            jax.ShapeDtypeStruct((rows, model), BF16),
+            jax.ShapeDtypeStruct(shape, BF16),
+            jax.ShapeDtypeStruct((16, 128), F32),
         ],
         scratch_shapes=[
-            pltpu.VMEM((2, DH + FEAT_ROWS, rows), BF16),
-            pltpu.VMEM((128, rows), BF16),
-            pltpu.VMEM((2, 128, rows), BF16),
+            vmem(2, DH + FEAT_ROWS, rows),
+            vmem(128, rows),
+            vmem(2, 128, rows),
             pltpu.VMEM((128, rows), F32),
             pltpu.VMEM((128, rows), F32),
             pltpu.VMEM((128, rows), F32),
-            pltpu.VMEM((2, FEAT_ROWS, rows), BF16),
+            vmem(2, FEAT_ROWS, rows),
             pltpu.VMEM((2, WIN, BQ), F32),
+            vmem(pairs, 2, blocks, rows, BQ),
+            vmem(3, rows, half),
+            vmem(model, rows),
+            vmem(3, model, half),
+            vmem(*more.shape),
+            vmem(rows, model),
+            vmem(*shape),
+            pltpu.SemaphoreType.DMA((pairs, 2, blocks)),
+            pltpu.SemaphoreType.DMA((5,)),
         ]
         + [pltpu.VMEM((rows, BQ), F32)] * 3,
-        compiler_params=params(),
+        compiler_params=params(60),
         cost_estimate=pl.CostEstimate(
-            flops=2 * 2 * pairs * rows * rows * 256 * 4,
-            bytes_accessed=2 * 2 * pairs * rows * rows,
+            flops=2 * pairs * rows * rows * 256 * 2 + 4 * rows * model * half,
+            bytes_accessed=2 * pairs * rows * rows,
             transcendentals=0,
         ),
-        name="attend_back",
-    )(projected, projected, projected, grad_mix, mixture, probs, inverse, cells, cells_t, lay, *after)
-
-
-def table_sums(lay_sums, rel_sums):
-    gap = jnp.arange(BQ + WIN) - (BQ - 1 + PAD)
-    bucket = jnp.clip(gap, -(RB // 2), RB // 2 - 1) + RB // 2
-    onehot = (bucket[:, None] == jnp.arange(RB)).astype(F32)
-    rel = jnp.einsum("hn,nb->bh", rel_sums[:, 0], onehot, precision=lax.Precision.HIGHEST)
-    return jnp.concatenate([rel, jnp.sum(lay_sums, axis=-1).T], axis=0)
-
-
-def ffn_kernel(first, extra, base, hidden, order, x_in, g_in, w_in, *refs):
+        name="heads_back",
+    )(
+        projected, projected, projected, grad_mix, mixture, inverse, cells, cells_t, lay,
+        table, probs, rows_t, weights, more, *after,
+    )
+
+
+def ffn_kernel(first, count, extra, base, hidden, order, me, x_in, g_in, *refs):
+    parts, refs = refs[:count], refs[count:]
     if not first:
         out_in, grad_in = refs[:2]
     refs = refs[extra:]
     out_to, grad_to, sums_to = refs[:3]
     x, g, w, rows_t, grads_t, act_all, gate_all, up_all, out, grad, sums = refs[3:14]
-    sems, sum_sems = refs[14:16]
+    sems, sum_sems, part_sems = refs[14:17]
     total, model = x.shape
-    weight = lambda i: w_in.at[:, base + i * hidden : base + (i + 1) * hidden]
     copy = pltpu.make_async_copy
-    loads = [
-        copy(x_in, x, sems.at[0]),
-        copy(weight(0), w.at[0], sems.at[1]),
-        copy(weight(1), w.at[1], sems.at[2]),
-        copy(g_in, g, sems.at[3]),
-        copy(weight(2), w.at[2], sems.at[4]),
-    ]
+    weight = lambda i: load_parts(
+        me, parts, slice(base + i * hidden, base + (i + 1) * hidden), w.at[i], part_sems.at[i]
+    )
+    loads = [[copy(x_in, x, sems.at[0])], weight(0), weight(1), [copy(g_in, g, sems.at[3])], weight(2)]
     if not first:
-        out_old, grad_old = refs[16:18]
-        loads += [copy(out_in, out_old, sems.at[5]), copy(grad_in, grad_old, sems.at[6])]
-    for load in loads:
+        out_old, grad_old = refs[17:19]
+        loads += [[copy(out_in, out_old, sems.at[5])], [copy(grad_in, grad_old, sems.at[6])]]
+    for load in sum(loads, []):
         load.start()
-    loads[0].wait()
+    loads[0][0].wait()
     rows_t[...] = x[...].astype(F32).T.astype(BF16)
-    for load in loads[1:4]:
+    for load in sum(loads[1:4], []):
         load.wait()
     grads_t[...] = g[...].astype(F32).T.astype(BF16)
-    for load in loads[4:]:
+    for load in sum(loads[4:], []):
         load.wait()
     slope = (2 / jnp.pi) ** 0.5
     for cut in range(2):
@@ -526,7 +597,7 @@
         store.wait()
 
 
-def ffn(normed, grad_ffn, weights, base, hidden, order, before=()):
+def ffn(me, normed, grad_ffn, parts, base, hidden, order, before=()):
     rows, model = normed.shape
     first = not before
     extra = len(before)
@@ -534,8 +605,8 @@
     part = jax.ShapeDtypeStruct((rows, model), BF16)
     vmem = lambda *shape: pltpu.VMEM(shape, BF16)
     return pl.pallas_call(
-        functools.partial(ffn_kernel, first, extra, base, hidden, order),
-        in_specs=[anywhere] * (3 + extra),
+        functools.partial(ffn_kernel, first, len(parts), extra, base, hidden, order),
+        in_specs=[SCALAR] + [anywhere] * (2 + len(parts) + extra),
         out_specs=[anywhere] * 3,
         out_shape=[part, part, jax.ShapeDtypeStruct((model, 3 * hidden), BF16)],
         scratch_shapes=[vmem(rows, model)] * 2
@@ -545,69 +616,16 @@
         + [vmem(rows, model)] * 2
         + [vmem(3, model, hidden)]
         + [pltpu.SemaphoreType.DMA((7,)), pltpu.SemaphoreType.DMA((3, len(order)))]
+        + [pltpu.SemaphoreType.DMA((3, PARTS))]
         + ([] if first else [vmem(rows, model)] * 2),
-        compiler_params=params(),
+        compiler_params=params(60),
         cost_estimate=pl.CostEstimate(
             flops=18 * rows * model * hidden,
             bytes_accessed=12 * model * hidden + 8 * rows * model,
             transcendentals=rows * hidden,
         ),
         name="ffn_first" if first else "ffn_last",
-    )(normed, grad_ffn, weights, *before)
-
-
-def back_kernel(order, kind, rows_t, *refs):
-    grads = jnp.concatenate([r[...] for r in refs[:3]], axis=1)
-    weights = jnp.concatenate([r[...] for r in refs[3:6]], axis=1)
-    if kind == "first":
-        carry, (out_ref, sums) = refs[6], refs[-2:]
-        out = nt(grads, weights)
-    else:
-        before, table, (out_ref, sums) = *refs[6:8], refs[-2:]
-        out = nt(grads, weights) + before[...].astype(F32)
-    out_ref[...] = out.astype(BF16)
-    found = nn(rows_t[...], grads).astype(BF16)
-    model, width = found.shape
-    part = model // len(order)
-    chunk = model // sums.shape[0]
-    for k, start in enumerate(order):
-        place, at = divmod(k * part, chunk)
-        sums[place, at : at + part, :width] = found[start : start + part]
-        if kind == "first":
-            sums[place, at : at + part, width:] = carry[k * part : (k + 1) * part]
-    if kind != "first":
-        for place in range(sums.shape[0]):
-            sums[place, chunk:] = table[...]
-
-
-def project_back(rows_t, grads, weights, width, first, order, plane, carry=None, before=None, table=None, after=()):
-    model, rows = rows_t.shape
-    half = grads[0].shape[1]
-    whole = lambda *shape: pl.BlockSpec(shape, lambda j: (0,) * len(shape), pipeline_mode=pl.Buffered(1))
-    at = lambda i: pl.BlockSpec((model, half), lambda j: (0, (i * width + first) // half))
-    kind = "first" if before is None else "last"
-    if kind == "first":
-        more, shape = (carry,), (plane, model // plane, 3 * half + carry.shape[1])
-    else:
-        more, shape = (before, table), (plane, model // plane + table.shape[0], 3 * half)
-    return pl.pallas_call(
-        functools.partial(back_kernel, order, kind),
-        grid=(1,),
-        in_specs=[whole(model, rows)]
-        + [whole(rows, half)] * 3
-        + [at(0), at(1), at(2)]
-        + [whole(*m.shape) for m in more]
-        + [pl.BlockSpec(memory_space=pl.ANY)] * len(after),
-        out_specs=[whole(rows, model), whole(*shape)],
-        out_shape=[jax.ShapeDtypeStruct((rows, model), BF16), jax.ShapeDtypeStruct(shape, BF16)],
-        compiler_params=params(),
-        cost_estimate=pl.CostEstimate(
-            flops=12 * rows * model * half,
-            bytes_accessed=12 * model * half + 4 * rows * model,
-            transcendentals=0,
-        ),
-        name="project_back",
-    )(rows_t, *grads, weights, weights, weights, *more, *after)
+    )(me, normed, grad_ffn, *parts, *before)
 
 
 def rows_spec(columns, limit=None):
@@ -618,9 +636,6 @@
 
 def fixed_spec(*shape):
     return pl.BlockSpec(shape, lambda r: (0,) * len(shape))
-
-
-SCALAR = pl.BlockSpec(memory_space=pltpu.SMEM)
 
 
 def is_text(count):
@@ -637,7 +652,7 @@
         out_specs=out_specs,
         out_shape=[jax.ShapeDtypeStruct(*o) for o in out_shape],
         scratch_shapes=scratch,
-        compiler_params=pltpu.CompilerParams(vmem_limit_bytes=ROW_VMEM),
+        compiler_params=params(60 if name in STREAMED else 20),
         cost_estimate=pl.CostEstimate(flops=flops, bytes_accessed=20 * rows * 1024, transcendentals=0),
         name=name,
     )(*operands)
@@ -670,46 +685,110 @@
     return inv * (grad_unit - unit * jnp.mean(grad_unit * unit, axis=1, keepdims=True))
 
 
-def project_kernel(rows, weights, projected, normed_t, gains):
-    width = projected.shape[1]
-
-    @pl.when(pl.program_id(0) == 0)
-    def _():
-        gains[...] = weights[:, width:].astype(F32).T[:8]
-
-    normed = norm(rows[...])[0] * gains[:1]
-    normed_t[...] = normed.T.astype(BF16)
-    projected[...] = nn(normed.astype(BF16), weights[:, :width]).astype(BF16)
-
-
-def project(rows, weights):
-    count, model = rows.shape
-    width = weights.shape[1] - 128
-    return row_call(
-        project_kernel, "project", count,
-        [rows_spec(model), pl.BlockSpec(weights.shape, lambda r: (0, 0), pipeline_mode=pl.Buffered(1))],
-        [
-            (rows_spec(width), ((count, width), BF16)),
-            (pl.BlockSpec((model, BQ), lambda r: (0, r)), ((model, count), BF16)),
-            (fixed_spec(8, model), ((8, model), F32)),
+def project_kernel(count, me, rows_from, *refs):
+    parts = refs[:count]
+    projected_to, normed_to, weights_to, gains = refs[count : count + 4]
+    rows, weights, projected, normed_t, sems, part_sems = refs[count + 4 :]
+    copy = pltpu.make_async_copy
+    load = copy(rows_from, rows, sems.at[0])
+    loads = load_parts(me, parts, slice(0, weights.shape[1]), weights, part_sems)
+    load.start()
+    for each in loads:
+        each.start()
+    for each in loads:
+        each.wait()
+    store = copy(weights, weights_to, sems.at[1])
+    store.start()
+    length, width = projected.shape
+    gains[...] = weights[:, width:].astype(F32).T[:8]
+    load.wait()
+    stores = [store]
+    for i in range(2):
+        part = slice(i * length // 2, (i + 1) * length // 2)
+        normed = norm(rows[part])[0] * gains[:1]
+        normed_t[:, part] = normed.T.astype(BF16)
+        projected[part] = nn(normed.astype(BF16), weights[:, :width]).astype(BF16)
+        stores.append(copy(projected.at[part], projected_to.at[part], sems.at[2 + i]))
+        stores[-1].start()
+    stores.append(copy(normed_t, normed_to, sems.at[4]))
+    stores[-1].start()
+    for store in stores:
+        store.wait()
+
+
+def project(me, rows, parts):
+    length, model = rows.shape
+    columns = parts[0].shape[-1]
+    width = columns - 128
+    anywhere = pl.BlockSpec(memory_space=pl.ANY)
+    return pl.pallas_call(
+        functools.partial(project_kernel, len(parts)),
+        in_specs=[SCALAR] + [anywhere] * (1 + len(parts)),
+        out_specs=[anywhere] * 3 + [pl.BlockSpec(memory_space=pltpu.VMEM)],
+        out_shape=[
+            jax.ShapeDtypeStruct((length, width), BF16),
+            jax.ShapeDtypeStruct((model, length), BF16),
+            jax.ShapeDtypeStruct((model, columns), BF16),
+            jax.ShapeDtypeStruct((8, model), F32),
         ],
-        [], 2 * count * model * width, rows, weights,
-    )
-
-
-def mix_out_kernel(mixture, weight, out):
-    out[...] = nt(mixture[...], weight[...]).astype(BF16)
-
-
-def mix_out(mixture, weights):
-    rows, width = mixture.shape
-    model = weights.shape[0]
-    return row_call(
-        mix_out_kernel, "mix_out", rows,
-        [rows_spec(width), fixed_spec(model, width)],
-        [(rows_spec(model), ((rows, model), BF16))],
-        [], 2 * rows * model * width, mixture, weights,
-    )[0]
+        scratch_shapes=[
+            pltpu.VMEM((length, model), F32),
+            pltpu.VMEM((model, columns), BF16),
+            pltpu.VMEM((length, width), BF16),
+            pltpu.VMEM((model, length), BF16),
+            pltpu.SemaphoreType.DMA((5,)),
+            pltpu.SemaphoreType.DMA((PARTS,)),
+        ],
+        compiler_params=params(40),
+        cost_estimate=pl.CostEstimate(
+            flops=2 * length * model * width, bytes_accessed=16 * length * model, transcendentals=0
+        ),
+        name="project",
+    )(me, rows, *parts)
+
+
+def mix_out_kernel(count, me, mixture_from, *refs):
+    parts = refs[:count]
+    out_to, weight_to, mixture, weight, out, sems, part_sems = refs[count:]
+    copy = pltpu.make_async_copy
+    loads = load_parts(me, parts, slice(0, weight.shape[1]), weight, part_sems)
+    loads.append(copy(mixture_from, mixture, sems.at[0]))
+    for each in loads:
+        each.start()
+    for each in loads:
+        each.wait()
+    stores = [copy(weight, weight_to, sems.at[1])]
+    stores[0].start()
+    length = mixture.shape[0]
+    for i in range(2):
+        part = slice(i * length // 2, (i + 1) * length // 2)
+        out[part] = nt(mixture[part], weight[...]).astype(BF16)
+        stores.append(copy(out.at[part], out_to.at[part], sems.at[2 + i]))
+        stores[-1].start()
+    for store in stores:
+        store.wait()
+
+
+def mix_out(me, mixture, parts, model):
+    length, width = mixture.shape
+    anywhere = pl.BlockSpec(memory_space=pl.ANY)
+    vmem = lambda *shape: pltpu.VMEM(shape, BF16)
+    return pl.pallas_call(
+        functools.partial(mix_out_kernel, len(parts)),
+        in_specs=[SCALAR] + [anywhere] * (1 + len(parts)),
+        out_specs=[anywhere] * 2,
+        out_shape=[
+            jax.ShapeDtypeStruct((length, model), BF16),
+            jax.ShapeDtypeStruct((model, width), BF16),
+        ],
+        scratch_shapes=[vmem(length, width), vmem(model, width), vmem(length, model)]
+        + [pltpu.SemaphoreType.DMA((4,)), pltpu.SemaphoreType.DMA((PARTS,))],
+        compiler_params=params(24),
+        cost_estimate=pl.CostEstimate(
+            flops=2 * length * model * width, bytes_accessed=4 * length * model, transcendentals=0
+        ),
+        name="mix_out",
+    )(me, mixture, *parts)
 
 
 def middle_kernel(rows, own, other, gains, hidden, normed):
@@ -840,6 +919,37 @@
     )
 
 
+def finish_kernel(cuts, ffn_one, ffn_two, heads, wq, wk, wv, w_gate, w_up, *outs):
+    part, width = wq.shape
+    half = width // 2
+    start = 0
+    for size, source in zip(cuts, (ffn_one, ffn_two)):
+        for i, out in enumerate(outs[4:7]):
+            out[:, start : start + size] = source[:, i * size : (i + 1) * size].astype(F32)
+        start += size
+    first = 3 * cuts[1]
+    for i, out in enumerate(outs[:3]):
+        out[:, :half] = ffn_two[:, first + i * half : first + (i + 1) * half].astype(F32)
+        out[:, half:] = heads[:, i * half : (i + 1) * half].astype(F32)
+    outs[3][...] = ffn_two[:, first + 3 * half :].astype(F32)
+    total = lambda w, out: jnp.sum(w[...].astype(F32) * out[...], axis=1, keepdims=True)
+    one = total(wq, outs[0]) + total(wk, outs[1]) + total(wv, outs[2])
+    two = total(w_gate, outs[4]) + total(w_up, outs[5])
+    lane = lax.broadcasted_iota(jnp.int32, (part, 128), 1)
+    outs[7][...] = jnp.where(lane == 0, one, jnp.where(lane == 1, two, 0.0))
+
+
+def finish(sums, weights, cuts, width):
+    part, hidden = weights[-1].shape
+    shapes = [(part, width)] * 4 + [(part, hidden)] * 3 + [(part, 128)]
+    return pl.pallas_call(
+        functools.partial(finish_kernel, cuts),
+        out_shape=[jax.ShapeDtypeStruct(shape, F32) for shape in shapes],
+        compiler_params=params(20),
+        name="finish",
+    )(*sums, *weights)
+
+
 def lay_index():
     cell = jnp.arange(CELLS, dtype=jnp.int32)
     row, col = cell // GRID, cell % GRID
@@ -892,15 +1002,15 @@
     cut = hidden // 3 // 256 * 256 + 256
     gains = jnp.pad(jnp.stack([gain_one, gain_two], axis=1), ((0, 0), (0, 126)))
     sent = []
-    (qkv,), layers, planes, corners = chips.gather_rows(
-        jnp.concatenate([wq, wk, wv, gains], axis=1), True, (3 * width + 128,),
+    qkv, layers, planes, corners = chips.gather_rows(
+        jnp.concatenate([wq, wk, wv, gains], axis=1),
         aside=lambda layers: (sent.append(send_half(patch_in[0, :live_slots], layers)), sent[0])[1:],
     )
     sent = sent or [send_half(patch_in[0, :live_slots])]
     patches = join_halves(sent[0])
-    (wo_all, first_set), layers, planes, _ = chips.gather_rows(
+    first_set, layers, planes, _ = chips.gather_rows(
         jnp.concatenate([wo_t, w_gate[:, :cut], w_up[:, :cut], w_down_t[:, :cut]], axis=1),
-        True, (width, 3 * cut), planes, corners,
+        planes, corners,
     )
     patch_cot = join_halves(send_half(cot_patch[0, :live_slots], layers))
     last_set = lax.all_gather(
@@ -910,17 +1020,20 @@
     rows = embed(count, text_in[0], spread, patches)
     grad_ffn = embed(count, cot_text[0], pick, patch_cot, BF16)
 
-    projected, normed_t, gains = project(rows, qkv)
+    place = me[None].astype(jnp.int32)
+    projected, normed_t, qkv, gains = project(place, rows, qkv)
     half = width // 256
     seen = attend(table, projected, cells, lay, 0, half, width)
     mixture, probs, inverse = attend(table, projected, cells, lay, half, half, width, seen, (*planes, patch_cot))
-    part = mix_out(mixture, wo_all)
+    part, wo_all = mix_out(place, mixture, first_set, model)
     hidden_rows, normed_two = middle(rows, part, other_core(part), gains)
 
     order = chips.order(model)
-    ffn_part, grad_part, grads_one = ffn(normed_two, grad_ffn, first_set, 0, cut, order)
+    ffn_part, grad_part, grads_one = ffn(
+        place, normed_two, grad_ffn, first_set, width, cut, order
+    )
     ffn_part, grad_part, grads_two = ffn(
-        normed_two, grad_ffn, last_set, 0, hidden - cut, order, (ffn_part, grad_part)
+        place, normed_two, grad_ffn, (last_set,), 0, hidden - cut, order, (ffn_part, grad_part)
     )
     scatter = lambda a, groups: lax.psum_scatter(
         a, "dp", scatter_dimension=0, axis_index_groups=groups, tiled=True
@@ -930,78 +1043,53 @@
         hidden_rows, grad_part, other_core(grad_part), grad_ffn, gains, wo_all, mixture, order
     )
     sum_one = chips.exchange(tie(sum_one, grad_mix), chips.columns)
-    args = (projected, grad_mix, mixture, probs, inverse, cells, cells_t, lay)
-    *grads_a, lay_a, rel_a = attend_back(*args, 0, half)
-    normed_a, grads_a = project_back(
-        normed_t, grads_a, qkv, width, 0, order, chips.plane, carry=wo_grad, after=(sum_one,)
+    args = (projected, grad_mix, mixture, probs, inverse, cells, cells_t, lay, normed_t, qkv)
+    normed_a, grads_a, table_part = heads_back(
+        *args, 0, half, order, chips.plane, jnp.zeros((16, 128), F32), wo_grad
     )
     sum_a = chips.exchange(grads_a.reshape(model, -1), chips.planes).astype(BF16)
-    *grads_b, lay_b, rel_b = attend_back(*args, half, half, (normed_a,))
-    table_part = table_sums(jnp.concatenate([lay_a, lay_b]), jnp.concatenate([rel_a, rel_b]))
-    normed_part, grads_b = project_back(
-        normed_t, grads_b, qkv, width, width // 2, order, chips.plane,
-        before=normed_a, table=wide_row(table_part, 3 * width // 2),
-    )
-    sum_two = scatter(tie(jnp.concatenate([sum_two, sum_a], axis=1), normed_part), chips.columns).astype(F32)
-    sum_a = sum_two[:, 3 * (hidden - cut) :]
+    normed_part, grads_b, _ = heads_back(
+        *args, half, half, order, chips.plane, table_part, normed_a, (sum_one,)
+    )
+    sum_two = scatter(tie(jnp.concatenate([sum_two, sum_a], axis=1), normed_part), chips.columns)
     ffn_other = other_core(ffn_part)
     text_grad, patch_grad = last(
         count, rows, normed_part, other_core(normed_part), grad_attn, gains, spread, text_slots
     )
+    sum_b = chips.trade(grads_b, chips.planes, (patch_grad,))
+    chunk = model // chips.plane
+    layers = chips.sizes[0]
+    table_rows = split_table(sum_b[chunk:])
+    sum_b = sum_b[:chunk].astype(BF16).reshape(layers, chunk // layers, -1)
+    sum_b = jnp.concatenate([sum_b, jnp.broadcast_to(table_rows, (layers,) + table_rows.shape)], axis=1)
     text_out, patch_out = result(
-        count, hidden_rows, ffn_part, ffn_other, pick, text_slots, (normed_part,)
-    )
-    sum_b = chips.trade(grads_b, chips.planes)
-    chunk = model // chips.plane
-    table_row = wide_row(narrow_row(sum_b[chunk], table.shape), sum_b.shape[1])
-    layers = chips.sizes[0]
-    sum_b = sum_b[:chunk].astype(BF16).reshape(layers, chunk // layers, -1)
-    sum_b = jnp.concatenate([sum_b, jnp.broadcast_to(table_row, (layers,) + table_row.shape)], axis=1)
-    sum_b = chips.trade(tie(sum_b, patch_grad, patch_out), chips.columns)
-    sum_b, table_sum = sum_b[: chunk // layers], narrow_row(sum_b[chunk // layers], table.shape)
+        count, hidden_rows, ffn_part, ffn_other, pick, text_slots, (sum_b,)
+    )
+    sum_b = chips.trade(sum_b, chips.columns, (patch_out,))
+    sum_b, table_sum = sum_b[: chunk // layers], sum_b[chunk // layers :]
+    table_sum = table_sum[:, :48] + table_sum[:, 128 : 128 + 48]
+    table_sum = table_sum.reshape(16, 3, 16)[:, :, : table.shape[1]].transpose(1, 0, 2).reshape(table.shape)
     fill = lambda a: jnp.pad(a, ((0, patch_slots - live_slots), (0, 0)))
-    back = fill(join_halves(send_half(jnp.concatenate([patch_out, patch_grad], axis=1))))
-    patch_out, patch_grad = back[:, :model], back[:, model:]
-
-    rest = hidden - cut
-    join = lambda i: jnp.concatenate(
-        [
-            sum_one[:, i * cut : (i + 1) * cut], sum_two[:, i * rest : (i + 1) * rest],
-        ],
-        axis=1,
-    )
-    gate_sum, up_sum, down_sum = join(0), join(1), join(2)
-    cols = width // 2
-    wq_sum, wk_sum, wv_sum = (
-        jnp.concatenate([a[:, i * cols : (i + 1) * cols] for a in (sum_a, sum_b)], axis=1)
-        for i in range(3)
-    )
-    wo_sum = sum_a[:, 3 * cols :]
-
-    own_first = sum(
-        jnp.sum(w.astype(F32) * g, axis=1) for w, g in ((wq, wq_sum), (wk, wk_sum), (wv, wv_sum))
-    )
-    own_second = sum(jnp.sum(w.astype(F32) * g, axis=1) for w, g in ((w_gate, gate_sum), (w_up, up_sum)))
-    own = jnp.stack([own_first, own_second])
-    own = (own + other_core(own)) / jnp.stack([gain_one, gain_two]).astype(F32)
+    patch_grad = fill(join_halves(send_half(patch_grad)))
+    patch_out = fill(join_halves(send_half(patch_out)))
+
+    *sums, own = finish(
+        (sum_one, sum_two, sum_b), (wq, wk, wv, w_gate, w_up), (cut, hidden - cut), width
+    )
+    wq_sum, wk_sum, wv_sum, wo_sum, gate_sum, up_sum, down_sum = sums
+    own = (own + other_core(own))[:, :2] / jnp.stack([gain_one, gain_two], axis=1).astype(F32)
     return (
         text_out[None], patch_out[None], text_grad[None], patch_grad[None],
-        wq_sum, wk_sum, wv_sum, wo_sum, own[0], gate_sum, up_sum, down_sum, own[1],
+        wq_sum, wk_sum, wv_sum, wo_sum, own[:, 0], gate_sum, up_sum, down_sum, own[:, 1],
         table_sum,
     )
 
 
-def wide_row(values, columns):
-    flat = values.reshape(-1)
-    high = flat.astype(BF16)
-    low = (flat - high.astype(F32)).astype(BF16)
-    both = jnp.concatenate([high, low])
-    return jnp.pad(both[None], ((0, 15), (0, columns - both.shape[0])))
-
-
-def narrow_row(row, shape):
-    size = shape[0] * shape[1]
-    return (row[:size] + row[size : 2 * size]).reshape(shape)
+def split_table(rows):
+    values = rows[:, :128] + rows[:, 128:256]
+    high = values.astype(BF16)
+    low = (values - high.astype(F32)).astype(BF16)
+    return jnp.concatenate([high, low, jnp.zeros((16, rows.shape[1] - 256), BF16)], axis=1)
 
 
 def solution(mesh):

time: 425 us -> 411 us (0.967)
  local copies, waits for them, and re-layouts: 57.8 us -> 32.1 us
  waiting for transfers between devices: 58.2 us -> 72.7 us
  other arithmetic: 34.1 us -> 27.1 us
    unnamed x146 -> x127, local copies, waits for them, and re-layouts: 40.4 us -> 18.9 us
    ppermute x6, waiting for transfers between devices: 9.26 us -> 24.2 us  [trade(): total = total + lax.ppermute(part, 'dp', route).astype(F32)]
    ppermute x3 -> x4, waiting for transfers between devices: 31.3 us -> 16.4 us  [send_half(): return lax.ppermute(mine, 'dp', route)]
    reduce_sum x6 -> x0, other arithmetic: 4.98 us -> none  [the longest x5 4.05 us: body(): jnp.sum(w.astype(F32) * g, axis=1)]
    all_gather x1, waiting for transfers between devices: 0.02 us -> 4.61 us  [body(): lax.all_gather(tie(jnp.concatenate([w_gate[:, cut:], w_up[:, cut:], w_dow...]
    pallas_call x8 -> x7, Pallas kernels: 126 us -> 130 us  [the longest x2 61.2 us: heads_back(): pl.pallas_call(functools.partial(heads_back_kernel, order, first, starts)...]
    pallas_call x8 -> x6, Pallas kernels: 35.8 us -> 37.1 us  [row_call(): pl.pallas_call(kernel, grid=(rows // BQ,), in_specs=in_specs, out_specs=o...]
  transfers between devices with their start and end apart: 37 -> 39, of which waited for: 9 -> 16; matrix products, arithmetic and copies ran while one was open for 11% -> 9% of each run, Pallas kernels for 49% -> 51%
where the time goes in v3:
time: 411 us; the launch traced here: 403 us
  Pallas kernels  206 us (50%)
  waiting for transfers between devices  72.7 us (18%)
  starting transfers between devices  48 us (12%)
  local copies, waits for them, and re-layouts  32.1 us (8%)
  other arithmetic  27.1 us (7%)
  between operations  17.8 us (4%)
    pallas_call x2, Pallas kernels, heads_back(): pl.pallas_call(functools.partial(heads_back_kernel, order, first, starts)...  61.2 us
    pallas_call x2, Pallas kernels, ffn(): pl.pallas_call(functools.partial(ffn_kernel, first, len(parts), extra, ba...  54.1 us
    pallas_call x2, Pallas kernels, attend(): pl.pallas_call(functools.partial(attend_kernel, first, extra), grid=(pair...  38.2 us
    pallas_call x6, Pallas kernels, row_call(): pl.pallas_call(kernel, grid=(rows // BQ,), in_specs=in_specs, out_specs=o...  37.1 us
    ppermute x6, waiting for transfers between devices, trade(): total = total + lax.ppermute(part, 'dp', route).astype(F32)  24.2 us
    ppermute x14, starting transfers between devices, send(): return lax.ppermute(block, 'dp', route)  23.4 us
    unnamed x127, local copies, waits for them, and re-layouts  18.9 us
    ppermute x4, waiting for transfers between devices, send_half(): return lax.ppermute(mine, 'dp', route)  16.4 us
  transfers between devices with their start and end apart: 39, of which 16 were waited for; matrix products, arithmetic and copies ran while one was open for 9% of the time, Pallas kernels for 51%

profile of v3, /device:TPU:0, one launch (start us, length us, event | category | flops | bytes accessed | tf_op | source)
XLA Modules:
  0.0 403.2 jit_solution(11636559844626788347)
XLA Ops:
  36.7 3.9 collective-permute-start.3
  41.6 8.8 %collective-permute-done.3.refs_1_ = bf16[104,1024]{1,0:T(8,128)(2,1)} collective-permute-done((bf16[104,1024]{1,0:T(8,128)(2,1)}, bf16[104,1024]{1,0:T(8,128)(2,1)}, u32[]{:S(2)}, u32[]{:S(2)}) %collective-permute-start.3) | collective-permute-done | bytes 213024 | tf_op jit(solution)/shard_map/ppermute | solution.py:159
  54.4 5.1 %collective-permute-start.11 = (bf16[64,2048]{1,0:T(8,128)(2,1)}, bf16[64,2048]{1,0:T(8,128)(2,1)}, u32[]{:S(2)}, u32[]{:S(2)}) collective-permute-start(bf16[64,2048]{1,0:T(8,128)(2,1)} %tie.12), channel_id=1, source_target_pairs={{0,24},{2,26},{4,28},{6,30},{8,0},{10,2},{12,4},{14,6},{16,8},{18,... | collective-permute-start | bytes 786440 | tf_op jit(solution)/shard_map/ppermute | solution.py:69
  71.8 11.3 %collective-permute-done.10.refs_2_ = bf16[64,2048]{1,0:T(8,128)(2,1)} collective-permute-done((bf16[64,2048]{1,0:T(8,128)(2,1)}, bf16[64,2048]{1,0:T(8,128)(2,1)}, u32[]{:S(2)}, u32[]{:S(2)}) %collective-permute-start.10) | collective-permute-done | bytes 262176 | tf_op jit(solution)/shard_map/ppermute | solution.py:69
  92.5 9.7 %project.1 = (bf16[1280,1536]{1,0:T(8,128)(2,1)S(1)}, bf16[1024,1280]{1,0:T(8,128)(2,1)S(1)}, bf16[1024,1664]{1,0:T(8,128)(2,1)S(1)}, f32[8,1024]{1,0:T(8,128)S(1)}) custom-call(s32[1]{0:T(128)} %bitcast.9.me, f32[1280,1024]{1,0:T(8,128)} %copy-done.1, bf16[4,64,1664]{2,1,0:T(8,128)(2,1)} %pad_maximum_fusion.3.refs_0_, bf16[4,64,1664]{2,1,0:T(8,128)(2,1)S(1)} %copy-done.17, ...), custom_call_target="tpu_custom_call" | custom-call | flops 4026531840 | bytes 20971520 | tf_op jit(solution)/shard_map/project/pallas_call | solution.py:724
  102.4 19.0 %attend.2 = (bf16[1280,512]{1,0:T(8,128)(2,1)S(1)}, bf16[8,5,1280,256]{3,2,1,0:T(8,128)(2,1)}, f32[8,1,1280]{2,1,0:T(1,128)S(1)}) custom-call(f32[48,8]{1,0:T(8,128)S(1)} %convert_element_type.117.table, bf16[1280,1536]{1,0:T(8,128)(2,1)S(1)} %get-tuple-element.54.q_ref.k_ref.v_ref, bf16[1280,1536]{1,0:T(8,128)(2,1)S(1)} %get-tuple-element.54.q_ref.k_ref.v_ref, ...), custom_call_target="tpu_custom_call" | custom-call | flops 80530636800 | bytes 13107200 | tf_op jit(solution)/shard_map/attend/pallas_call | solution.py:259
  125.5 19.2 %attend.3 = (bf16[1280,512]{1,0:T(8,128)(2,1)S(1)}, bf16[8,5,1280,256]{3,2,1,0:T(8,128)(2,1)}, f32[8,1,1280]{2,1,0:T(1,128)S(1)}) custom-call(f32[48,8]{1,0:T(8,128)S(1)} %convert_element_type.117.table, bf16[1280,1536]{1,0:T(8,128)(2,1)S(1)} %get-tuple-element.54.q_ref.k_ref.v_ref, ...), custom_call_target="tpu_custom_call", output_to_operand_aliasing={{0}: (6, {}), {1}: (7, {}), {2}: (8, {})} | custom-call | flops 80530636800 | bytes 13107200 | tf_op jit(solution)/shard_map/attend/pallas_call | solution.py:259
  144.9 3.9 mix_out.1
  159.4 19.9 %ffn_first.1 = (bf16[1280,1024]{1,0:T(8,128)(2,1)}, bf16[1280,1024]{1,0:T(8,128)(2,1)}, bf16[1024,1536]{1,0:T(8,128)(2,1)}) custom-call(s32[1]{0:T(128)} %bitcast.9.me, bf16[1280,1024]{1,0:T(8,128)(2,1)} %copy-done.38, bf16[1280,1024]{1,0:T(8,128)(2,1)} %copy-done.6, bf16[4,64,2048]{2,1,0:T(8,128)(2,1)} %tie.13.refs_0_, bf16[4,64,2048]{2,1,0:T(8,128)(2,1)} %copy-done.13, ...), custom_call_target="tpu_custom_call" | custom-call | flops 12079595520 | bytes 16777216 | tf_op jit(solution)/shard_map/ffn_first/pallas_call | solution.py:607
  179.6 4.6 %all-gather.2.cloned.1.call-done.refs_0_ = bf16[1024,2688]{1,0:T(8,128)(2,1)} async-done(((bf16[64,2688]{1,0:T(8,128)(2,1)}), bf16[1024,2688]{1,0:T(8,128)(2,1)}) %all-gather.2.cloned.1.call-update) | async-done | bytes 5505040 | tf_op jit(solution)/shard_map/all_gather | solution.py:1016
  184.3 34.2 %ffn_last.1 = (bf16[1280,1024]{1,0:T(8,128)(2,1)}, bf16[1280,1024]{1,0:T(8,128)(2,1)}, bf16[1024,2688]{1,0:T(8,128)(2,1)}) custom-call(s32[1]{0:T(128)} %bitcast.9.me, bf16[1280,1024]{1,0:T(8,128)(2,1)} %copy-done.38, bf16[1280,1024]{1,0:T(8,128)(2,1)} %copy-done.6, bf16[1024,2688]{1,0:T(8,128)(2,1)} %all-gather.2.cloned.1.call-done.refs_0_, ...), custom_call_target="tpu_custom_call" | custom-call | flops 21139292160 | bytes 21495808 | tf_op jit(solution)/shard_map/ffn_last/pallas_call | solution.py:607
  220.3 4.9 %collective-permute-done.20.other = bf16[1280,1024]{1,0:T(8,128)(2,1)S(1)} collective-permute-done((bf16[1280,1024]{1,0:T(8,128)(2,1)S(1)}, bf16[1280,1024]{1,0:T(8,128)(2,1)S(1)}, u32[]{:S(2)}, u32[]{:S(2)}) %collective-permute-start.20) | collective-permute-done | bytes 2621472 | tf_op jit(solution)/shard_map/ppermute | solution.py:150
  226.7 11.5 %after_ffn.1 = (bf16[1280,1024]{1,0:T(8,128)(2,1)}, bf16[1280,512]{1,0:T(8,128)(2,1)}, bf16[1024,512]{1,0:T(8,128)(2,1)}) custom-call(f32[1280,1024]{1,0:T(8,128)} %copy-done.3, bf16[1280,1024]{1,0:T(8,128)(2,1)} %get-tuple-element.66.own, bf16[1280,1024]{1,0:T(8,128)(2,1)} %copy-done.40, bf16[1280,1024]{1,0:T(8,128)(2,1)} %copy-done.6, ...), custom_call_target="tpu_custom_call" | custom-call | flops 2684354560 | bytes 26214400 | tf_op jit(solution)/shard_map/after_ffn/pallas_call | solution.py:648
  238.3 3.9 all-to-all-start
  244.0 30.8 %heads_back.2 = (bf16[1280,1024]{1,0:T(8,128)(2,1)}, bf16[4,256,1280]{2,1,0:T(8,128)(2,1)}, f32[16,128]{1,0:T(8,128)}) custom-call(bf16[1280,1536]{1,0:T(8,128)(2,1)} %copy-done, bf16[1280,1536]{1,0:T(8,128)(2,1)} %copy-done, bf16[1280,1536]{1,0:T(8,128)(2,1)} %copy-done, bf16[1280,512]{1,0:T(8,128)(2,1)} %get-tuple-element.68.gm_ref.refs_1_, ...), custom_call_target="tpu_custom_call" | custom-call | flops 4697620480 | bytes 6553600 | tf_op jit(solution)/shard_map/heads_back/pallas_call | solution.py:482
  274.8 3.7 all-to-all-start.1
  279.4 30.4 %heads_back.3 = (bf16[1280,1024]{1,0:T(8,128)(2,1)}, bf16[4,272,768]{2,1,0:T(8,128)(2,1)}, f32[16,128]{1,0:T(8,128)}) custom-call(bf16[1280,1536]{1,0:T(8,128)(2,1)} %copy-done, bf16[1280,1536]{1,0:T(8,128)(2,1)} %copy-done, bf16[1280,1536]{1,0:T(8,128)(2,1)} %copy-done, bf16[1280,512]{1,0:T(8,128)(2,1)} %get-tuple-element.68.gm_ref.refs_1_, ...), custom_call_target="tpu_custom_call" | custom-call | flops 4697620480 | bytes 6553600 | tf_op jit(solution)/shard_map/heads_back/pallas_call | solution.py:482
  310.4 5.5 %all-to-all-done.1 = bf16[4,256,1280]{2,1,0:T(8,128)(2,1)S(1)} async-done(((bf16[4,256,1280]{2,1,0:T(8,128)(2,1)}), bf16[4,256,1280]{2,1,0:T(8,128)(2,1)S(1)}, u32[]{:S(2)}, u32[]{:S(2)}) %all-to-all-start.1) | async-done | bytes 2621472 | tf_op jit(solution)/shard_map/all_to_all | solution.py:91
  325.0 10.5 %last.1 = (bf16[1024,1024]{1,0:T(8,128)(2,1)}, bf16[208,1024]{1,0:T(8,128)(2,1)}) custom-call(s32[1]{0:T(128)} %dynamic_slice.49.count, f32[1280,1024]{1,0:T(8,128)} %copy-done.1, bf16[1280,1024]{1,0:T(8,128)(2,1)} %get-tuple-element.78.own.refs_1_, bf16[1280,1024]{1,0:T(8,128)(2,1)} %collective-permute-done.21.other, ...), custom_call_target="tpu_custom_call" | custom-call | flops 1090519040 | bytes 26214400 | tf_op jit(solution)/shard_map/last/pallas_call | solution.py:648
  335.5 7.1 %collective-permute-done.23 = bf16[272,768]{1,0:T(8,128)(2,1)S(1)} collective-permute-done((bf16[272,768]{1,0:T(8,128)(2,1)S(1)}, bf16[272,768]{1,0:T(8,128)(2,1)S(1)}, u32[]{:S(2)}, u32[]{:S(2)}) %collective-permute-start.23) | collective-permute-done | bytes 417824 | tf_op jit(solution)/shard_map/ppermute | solution.py:107
  349.8 9.0 %result.1 = (bf16[1024,1024]{1,0:T(8,128)(2,1)}, bf16[208,1024]{1,0:T(8,128)(2,1)}) custom-call(s32[1]{0:T(128)} %dynamic_slice.49.count, f32[1280,1024]{1,0:T(8,128)} %copy-done.3, bf16[1280,1024]{1,0:T(8,128)(2,1)} %get-tuple-element.65.own, bf16[1280,1024]{1,0:T(8,128)(2,1)} %collective-permute-done.19.other, bf16[1280,208]{1,0:T(8,128)(2,1)} %copy-done.8, ...), custom_call_target="tpu_custom_call" | custom-call | flops 545259520 | bytes 26214400 | tf_op jit(solution)/shard_map/result/pallas_call | solution.py:648
  362.9 17.1 %collective-permute-done.30 = bf16[80,768]{1,0:T(8,128)(2,1)S(1)} collective-permute-done((bf16[80,768]{1,0:T(8,128)(2,1)S(1)}, bf16[80,768]{1,0:T(8,128)(2,1)S(1)}, u32[]{:S(2)}, u32[]{:S(2)}) %collective-permute-start.30) | collective-permute-done | bytes 122912 | tf_op jit(solution)/shard_map/ppermute | solution.py:107
  381.1 4.0 collective-permute-done.25
  386.0 3.6 collective-permute-done.27
  (296 shorter events, 103.6 us)
Async XLA Ops:
  8.0 176.2 %all-gather.2.cloned.1.call-start = ((), (), s32[]{:S(2)}) async-start(), calls=%async_computation.5 | async-start | bytes 5849088 | tf_op jit(solution)/shard_map/all_gather | solution.py:1016
  31.3 21.0 %collective-permute-start.5 = (bf16[4,64,1664]{2,1,0:T(8,128)(2,1)}, bf16[4,64,1664]{2,1,0:T(8,128)(2,1)S(1)}, u32[]{:S(2)}, u32[]{:S(2)}) collective-permute-start(bf16[4,64,1664]{2,1,0:T(8,128)(2,1)} %pad_maximum_fusion.3.refs_0_), channel_id=1, source_target_pairs={{0,2},{2,0},{4,6},{6,4},{8,10},{10,8},{12,14},{14,12},{16,18},{18,... | collective-permute-start | bytes 2555912 | tf_op jit(solution)/shard_map/ppermute | solution.py:69
  32.8 20.7 %collective-permute-start.6 = (bf16[4,64,1664]{2,1,0:T(8,128)(2,1)}, bf16[4,64,1664]{2,1,0:T(8,128)(2,1)S(1)}, u32[]{:S(2)}, u32[]{:S(2)}) collective-permute-start(bf16[4,64,1664]{2,1,0:T(8,128)(2,1)} %pad_maximum_fusion.3.refs_0_), channel_id=1, source_target_pairs={{0,4},{2,6},{4,0},{6,2},{8,12},{10,14},{12,8},{14,10},{16,20},{18,... | collective-permute-start | bytes 2555912 | tf_op jit(solution)/shard_map/ppermute | solution.py:69
  59.5 23.6 %collective-permute-start.10 = (bf16[64,2048]{1,0:T(8,128)(2,1)}, bf16[64,2048]{1,0:T(8,128)(2,1)}, u32[]{:S(2)}, u32[]{:S(2)}) collective-permute-start(bf16[64,2048]{1,0:T(8,128)(2,1)} %tie.12), channel_id=1, source_target_pairs={{0,16},{2,18},{4,20},{6,22},{8,24},{10,26},{12,28},{14,30},{16,0},... | collective-permute-start | bytes 786440 | tf_op jit(solution)/shard_map/ppermute | solution.py:69
  60.9 22.2 %collective-permute-start.9 = (bf16[64,2048]{1,0:T(8,128)(2,1)}, bf16[64,2048]{1,0:T(8,128)(2,1)}, u32[]{:S(2)}, u32[]{:S(2)}) collective-permute-start(bf16[64,2048]{1,0:T(8,128)(2,1)} %tie.12), channel_id=1, source_target_pairs={{0,8},{2,10},{4,12},{6,14},{8,16},{10,18},{12,20},{14,22},{16,24},... | collective-permute-start | bytes 786440 | tf_op jit(solution)/shard_map/ppermute | solution.py:69
  62.7 23.4 %collective-permute-start.7 = (bf16[4,32,1664]{2,1,0:T(8,128)(2,1)}, bf16[4,32,1664]{2,1,0:T(8,128)(2,1)S(1)}, u32[]{:S(2)}, u32[]{:S(2)}) collective-permute-start(bf16[4,32,1664]{2,1,0:T(8,128)(2,1)} %tie.11), channel_id=1, source_target_pairs={{0,2},{2,0},{4,6},{6,4},{8,10},{10,8},{12,14},{14,12},{16,18},{18,... | collective-permute-start | bytes 1277960 | tf_op jit(solution)/shard_map/ppermute | solution.py:69
  64.7 21.4 %collective-permute-start.8 = (bf16[4,32,1664]{2,1,0:T(8,128)(2,1)}, bf16[4,32,1664]{2,1,0:T(8,128)(2,1)S(1)}, u32[]{:S(2)}, u32[]{:S(2)}) collective-permute-start(bf16[4,32,1664]{2,1,0:T(8,128)(2,1)} %slice.178), channel_id=1, source_target_pairs={{0,4},{2,6},{4,0},{6,2},{8,12},{10,14},{12,8},{14,10},{16,20},{18,... | collective-permute-start | bytes 1277960 | tf_op jit(solution)/shard_map/ppermute | solution.py:69
  83.1 19.2 %collective-permute-start.14 = (bf16[104,1024]{1,0:T(8,128)(2,1)}, bf16[104,1024]{1,0:T(8,128)(2,1)}, u32[]{:S(2)}, u32[]{:S(2)}) collective-permute-start(bf16[104,1024]{1,0:T(8,128)(2,1)} %tie.14), channel_id=1, source_target_pairs={{0,16},{2,18},{4,20},{6,22},{8,24},{10,26},{12,28},{14,30},{16,0},... | collective-permute-start | bytes 638984 | tf_op jit(solution)/shard_map/ppermute | solution.py:159
  87.6 36.9 %collective-permute-start.12 = (bf16[4,64,2048]{2,1,0:T(8,128)(2,1)}, bf16[4,64,2048]{2,1,0:T(8,128)(2,1)S(1)}, u32[]{:S(2)}, u32[]{:S(2)}) collective-permute-start(bf16[4,64,2048]{2,1,0:T(8,128)(2,1)} %tie.13.refs_0_), channel_id=1, source_target_pairs={{0,2},{2,0},{4,6},{6,4},{8,10},{10,8},{12,14},{14,12},{16,18},{18,... | collective-permute-start | bytes 3145736 | tf_op jit(solution)/shard_map/ppermute | solution.py:69
  88.7 33.9 %collective-permute-start.13 = (bf16[4,64,2048]{2,1,0:T(8,128)(2,1)}, bf16[4,64,2048]{2,1,0:T(8,128)(2,1)}, u32[]{:S(2)}, u32[]{:S(2)}) collective-permute-start(bf16[4,64,2048]{2,1,0:T(8,128)(2,1)} %tie.13.refs_0_), channel_id=1, source_target_pairs={{0,4},{2,6},{4,0},{6,2},{8,12},{10,14},{12,8},{14,10},{16,20},{18,... | collective-permute-start | bytes 3145736 | tf_op jit(solution)/shard_map/ppermute | solution.py:69
  90.3 147.9 %reduce-scatter.4.cloned.1.call-start = ((), (), s32[]{:S(2)}) async-start(), calls=%async_computation.6 | async-start | bytes 3932160 | tf_op jit(solution)/shard_map/reduce_scatter | solution.py:1038
  102.3 19.1 %collective-permute-start.15 = (bf16[104,1024]{1,0:T(8,128)(2,1)}, bf16[104,1024]{1,0:T(8,128)(2,1)S(1)}, u32[]{:S(2)}, u32[]{:S(2)}) collective-permute-start(bf16[104,1024]{1,0:T(8,128)(2,1)} %collective-permute-done.14), channel_id=1, source_target_pairs={{0,1},{1,0},{2,3},{3,2},{4,5},{5,4},{6,7},{7,6},{8,9},{9,8},{10,11... | collective-permute-start | bytes 638984 | tf_op jit(solution)/shard_map/ppermute | solution.py:150
  123.9 20.9 %collective-permute-start.16 = (bf16[4,32,2048]{2,1,0:T(8,128)(2,1)S(1)}, bf16[4,32,2048]{2,1,0:T(8,128)(2,1)S(1)}, u32[]{:S(2)}, u32[]{:S(2)}) collective-permute-start(bf16[4,32,2048]{2,1,0:T(8,128)(2,1)S(1)} %slice.179), channel_id=1, source_target_pairs={{0,2},{2,0},{4,6},{6,4},{8,10},{10,8},{12,14},{14,12},{16,18},{18,... | collective-permute-start | bytes 1572872 | tf_op jit(solution)/shard_map/ppermute | solution.py:69
  124.6 20.2 %collective-permute-start.17 = (bf16[4,32,2048]{2,1,0:T(8,128)(2,1)S(1)}, bf16[4,32,2048]{2,1,0:T(8,128)(2,1)S(1)}, u32[]{:S(2)}, u32[]{:S(2)}) collective-permute-start(bf16[4,32,2048]{2,1,0:T(8,128)(2,1)S(1)} %slice.180), channel_id=1, source_target_pairs={{0,4},{2,6},{4,0},{6,2},{8,12},{10,14},{12,8},{14,10},{16,20},{18,... | collective-permute-start | bytes 1572872 | tf_op jit(solution)/shard_map/ppermute | solution.py:69
  179.4 136.9 %reduce-scatter.6.cloned.1.call-start = ((), (), s32[]{:S(2)}) async-start(), calls=%async_computation.7 | async-start | bytes 6881280 | tf_op jit(solution)/shard_map/reduce_scatter | solution.py:1038
  238.3 36.6 %all-to-all-start = ((bf16[4,64,1536]{2,1,0:T(8,128)(2,1)}), bf16[4,64,1536]{2,1,0:T(8,128)(2,1)S(1)}, u32[]{:S(2)}, u32[]{:S(2)}) async-start(bf16[4,64,1536]{2,1,0:T(8,128)(2,1)} %bitcast.64), calls=%async_computation.1 | async-start | bytes 1572864 | tf_op jit(solution)/shard_map/all_to_all | solution.py:91
  274.8 41.1 %all-to-all-start.1 = ((bf16[4,256,1280]{2,1,0:T(8,128)(2,1)}), bf16[4,256,1280]{2,1,0:T(8,128)(2,1)S(1)}, u32[]{:S(2)}, u32[]{:S(2)}) async-start(bf16[4,256,1280]{2,1,0:T(8,128)(2,1)} %get-tuple-element.85), calls=%async_computation.3 | async-start | bytes 5242880 | tf_op jit(solution)/shard_map/all_to_all | solution.py:91
  278.5 112.6 %reduce-scatter.8.cloned.1.call-start = ((), (), s32[]{:S(2)}) async-start(), calls=%async_computation.8 | async-start | bytes 2539520 | tf_op jit(solution)/shard_map/reduce_scatter | solution.py:1038
  309.9 39.9 %collective-permute-start.19 = (bf16[1280,1024]{1,0:T(8,128)(2,1)}, bf16[1280,1024]{1,0:T(8,128)(2,1)}, u32[]{:S(2)}, u32[]{:S(2)}) collective-permute-start(bf16[1280,1024]{1,0:T(8,128)(2,1)} %get-tuple-element.65.own), channel_id=1, source_target_pairs={{0,1},{1,0},{2,3},{3,2},{4,5},{5,4},{6,7},{7,6},{8,9},{9,8},{10,11... | collective-permute-start | bytes 7864328 | tf_op jit(solution)/shard_map/ppermute | solution.py:150
  322.8 19.7 %collective-permute-start.23 = (bf16[272,768]{1,0:T(8,128)(2,1)S(1)}, bf16[272,768]{1,0:T(8,128)(2,1)S(1)}, u32[]{:S(2)}, u32[]{:S(2)}) collective-permute-start(bf16[272,768]{1,0:T(8,128)(2,1)S(1)} %get-tuple-element.100), channel_id=1, source_target_pairs={{0,4},{2,6},{4,0},{6,2},{8,12},{10,14},{12,8},{14,10},{16,20},{18,... | collective-permute-start | bytes 1253384 | tf_op jit(solution)/shard_map/ppermute | solution.py:107
  347.8 32.2 %collective-permute-start.30 = (bf16[80,768]{1,0:T(8,128)(2,1)S(1)}, bf16[80,768]{1,0:T(8,128)(2,1)S(1)}, u32[]{:S(2)}, u32[]{:S(2)}) collective-permute-start(bf16[80,768]{1,0:T(8,128)(2,1)S(1)} %get-tuple-element.104), channel_id=1, source_target_pairs={{0,16},{8,24},{16,0},{24,8},{2,18},{10,26},{18,2},{26,10},{4,20},{... | collective-permute-start | bytes 368648 | tf_op jit(solution)/shard_map/ppermute | solution.py:107
  347.8 32.2 %collective-permute-start.29 = (bf16[80,768]{1,0:T(8,128)(2,1)S(1)}, bf16[80,768]{1,0:T(8,128)(2,1)S(1)}, u32[]{:S(2)}, u32[]{:S(2)}) collective-permute-start(bf16[80,768]{1,0:T(8,128)(2,1)S(1)} %get-tuple-element.103), channel_id=1, source_target_pairs={{0,8},{8,0},{16,24},{24,16},{2,10},{10,2},{18,26},{26,18},{4,12},{... | collective-permute-start | bytes 368648 | tf_op jit(solution)/shard_map/ppermute | solution.py:107
  359.8 25.2 %collective-permute-start.25 = (bf16[104,1024]{1,0:T(8,128)(2,1)S(1)}, bf16[104,1024]{1,0:T(8,128)(2,1)S(1)}, u32[]{:S(2)}, u32[]{:S(2)}) collective-permute-start(bf16[104,1024]{1,0:T(8,128)(2,1)S(1)} %constant_dynamic-slice_fusion.2), channel_id=1, source_target_pairs={{0,16},{2,18},{4,20},{6,22},{8,24},{10,26},{12,28},{14,30},{16,0},... | collective-permute-start | bytes 638984 | tf_op jit(solution)/shard_map/ppermute | solution.py:159
  361.6 28.0 %collective-permute-start.27 = (bf16[104,1024]{1,0:T(8,128)(2,1)S(1)}, bf16[104,1024]{1,0:T(8,128)(2,1)S(1)}, u32[]{:S(2)}, u32[]{:S(2)}) collective-permute-start(bf16[104,1024]{1,0:T(8,128)(2,1)S(1)} %constant_dynamic-slice_fusion.1), channel_id=1, source_target_pairs={{0,16},{2,18},{4,20},{6,22},{8,24},{10,26},{12,28},{14,30},{16,0},... | collective-permute-start | bytes 638984 | tf_op jit(solution)/shard_map/ppermute | solution.py:159
  (85 other events, 903.0 us)
Sparse Core Ops, SparseCore 0:
  90.4 93.8 all-gather.1
  319.2 53.6 reduce-scatter.7
Sparse Core Ops, SparseCore 1:
  179.5 43.6 reduce-scatter.3
  226.1 83.9 reduce-scatter.5

commit v4 on v3

--- a/solution.py
+++ b/solution.py
@@ -919,7 +919,7 @@
     )
 
 
-def finish_kernel(cuts, ffn_one, ffn_two, heads, wq, wk, wv, w_gate, w_up, *outs):
+def finish_kernel(cuts, ffn_one, ffn_two, heads_a, heads, wq, wk, wv, w_gate, w_up, *outs):
     part, width = wq.shape
     half = width // 2
     start = 0
@@ -927,11 +927,10 @@
         for i, out in enumerate(outs[4:7]):
             out[:, start : start + size] = source[:, i * size : (i + 1) * size].astype(F32)
         start += size
-    first = 3 * cuts[1]
     for i, out in enumerate(outs[:3]):
-        out[:, :half] = ffn_two[:, first + i * half : first + (i + 1) * half].astype(F32)
+        out[:, :half] = heads_a[:, i * half : (i + 1) * half].astype(F32)
         out[:, half:] = heads[:, i * half : (i + 1) * half].astype(F32)
-    outs[3][...] = ffn_two[:, first + 3 * half :].astype(F32)
+    outs[3][...] = heads_a[:, 3 * half :].astype(F32)
     total = lambda w, out: jnp.sum(w[...].astype(F32) * out[...], axis=1, keepdims=True)
     one = total(wq, outs[0]) + total(wk, outs[1]) + total(wv, outs[2])
     two = total(w_gate, outs[4]) + total(w_up, outs[5])
@@ -1047,34 +1046,38 @@
     normed_a, grads_a, table_part = heads_back(
         *args, 0, half, order, chips.plane, jnp.zeros((16, 128), F32), wo_grad
     )
-    sum_a = chips.exchange(grads_a.reshape(model, -1), chips.planes).astype(BF16)
+    ffn_part = tie(ffn_part, grad_mix)
+    text_out, patch_out = result(
+        count, hidden_rows, ffn_part, other_core(ffn_part), pick, text_slots, (normed_a,)
+    )
+    patch_sent = send_half(patch_out)
+    sum_two = scatter(tie(sum_two, patch_out), chips.columns)
+    sum_a = chips.exchange(tie(grads_a.reshape(model, -1), patch_out), chips.planes).astype(BF16)
     normed_part, grads_b, _ = heads_back(
-        *args, half, half, order, chips.plane, table_part, normed_a, (sum_one,)
-    )
-    sum_two = scatter(tie(jnp.concatenate([sum_two, sum_a], axis=1), normed_part), chips.columns)
-    ffn_other = other_core(ffn_part)
+        *args, half, half, order, chips.plane, table_part, normed_a, (sum_one, patch_out)
+    )
+    grads_b = tie(grads_b, sum_a)
+    sum_a = scatter(tie(sum_a, normed_part), chips.columns)
     text_grad, patch_grad = last(
         count, rows, normed_part, other_core(normed_part), grad_attn, gains, spread, text_slots
     )
-    sum_b = chips.trade(grads_b, chips.planes, (patch_grad,))
+    patch_grad = send_half(patch_grad)
+    sum_b = chips.trade(grads_b, chips.planes, (text_grad, patch_sent))
     chunk = model // chips.plane
     layers = chips.sizes[0]
     table_rows = split_table(sum_b[chunk:])
     sum_b = sum_b[:chunk].astype(BF16).reshape(layers, chunk // layers, -1)
     sum_b = jnp.concatenate([sum_b, jnp.broadcast_to(table_rows, (layers,) + table_rows.shape)], axis=1)
-    text_out, patch_out = result(
-        count, hidden_rows, ffn_part, ffn_other, pick, text_slots, (sum_b,)
-    )
-    sum_b = chips.trade(sum_b, chips.columns, (patch_out,))
+    sum_b = chips.trade(tie(sum_b, sum_two), chips.columns)
     sum_b, table_sum = sum_b[: chunk // layers], sum_b[chunk // layers :]
     table_sum = table_sum[:, :48] + table_sum[:, 128 : 128 + 48]
     table_sum = table_sum.reshape(16, 3, 16)[:, :, : table.shape[1]].transpose(1, 0, 2).reshape(table.shape)
     fill = lambda a: jnp.pad(a, ((0, patch_slots - live_slots), (0, 0)))
-    patch_grad = fill(join_halves(send_half(patch_grad)))
-    patch_out = fill(join_halves(send_half(patch_out)))
+    patch_grad = fill(join_halves(tie(patch_grad, sum_b)))
+    patch_out = fill(join_halves(tie(patch_sent, sum_b)))
 
     *sums, own = finish(
-        (sum_one, sum_two, sum_b), (wq, wk, wv, w_gate, w_up), (cut, hidden - cut), width
+        (sum_one, sum_two, sum_a, sum_b), (wq, wk, wv, w_gate, w_up), (cut, hidden - cut), width
     )
     wq_sum, wk_sum, wv_sum, wo_sum, gate_sum, up_sum, down_sum = sums
     own = (own + other_core(own))[:, :2] / jnp.stack([gain_one, gain_two], axis=1).astype(F32)

time: 411 us -> 396 us (0.964)
  waiting for transfers between devices: 72.7 us -> 53.4 us
    ppermute x6, waiting for transfers between devices: 24.2 us -> 12.5 us  [trade(): total = total + lax.ppermute(part, 'dp', route).astype(F32)]
    all_to_all x2, waiting for transfers between devices: 5.55 us -> 0.01 us  [exchange(): lax.all_to_all(block, 'dp', 0, 0, axis_index_groups=groups, tiled=True)]
    unnamed x127 -> x141, local copies, waits for them, and re-layouts: 18.9 us -> 20.3 us
  transfers between devices with their start and end apart: 39 -> 40, of which waited for: 16 -> 14; matrix products, arithmetic and copies ran while one was open for 9% -> 9% of each run, Pallas kernels for 51% -> 53%
where the time goes in v4:
time: 396 us; the launch traced here: 389 us
  Pallas kernels  206 us (52%)
  waiting for transfers between devices  53.4 us (13%)
  starting transfers between devices  51.9 us (13%)
  local copies, waits for them, and re-layouts  35.8 us (9%)
  other arithmetic  24.5 us (6%)
  between operations  17.5 us (4%)
    pallas_call x2, Pallas kernels, heads_back(): pl.pallas_call(functools.partial(heads_back_kernel, order, first, starts)...  61.2 us
    pallas_call x2, Pallas kernels, ffn(): pl.pallas_call(functools.partial(ffn_kernel, first, len(parts), extra, ba...  54.1 us
    pallas_call x2, Pallas kernels, attend(): pl.pallas_call(functools.partial(attend_kernel, first, extra), grid=(pair...  38.2 us
    pallas_call x6, Pallas kernels, row_call(): pl.pallas_call(kernel, grid=(rows // BQ,), in_specs=in_specs, out_specs=o...  37.1 us
    ppermute x14, starting transfers between devices, send(): return lax.ppermute(block, 'dp', route)  23.4 us
    unnamed x141, local copies, waits for them, and re-layouts  20.3 us
    ppermute x14, waiting for transfers between devices, send(): return lax.ppermute(block, 'dp', route)  15.2 us
    ppermute x4, waiting for transfers between devices, send_half(): return lax.ppermute(mine, 'dp', route)  14.5 us
  transfers between devices with their start and end apart: 40, of which 14 were waited for; matrix products, arithmetic and copies ran while one was open for 9% of the time, Pallas kernels for 53%

profile of v4, /device:TPU:0, one launch (start us, length us, event | category | flops | bytes accessed | tf_op | source)
XLA Modules:
  0.0 388.7 jit_solution(13783022966217218306)
XLA Ops:
  9.9 3.1 collective-permute-start
  36.7 3.9 %collective-permute-start.3 = (bf16[104,1024]{1,0:T(8,128)(2,1)}, bf16[104,1024]{1,0:T(8,128)(2,1)}, u32[]{:S(2)}, u32[]{:S(2)}) collective-permute-start(bf16[104,1024]{1,0:T(8,128)(2,1)} %tie.16), channel_id=1, source_target_pairs={{0,16},{2,18},{4,20},{6,22},{8,24},{10,26},{12,28},{14,30},{16,0},... | collective-permute-start | bytes 638984 | tf_op jit(solution)/shard_map/ppermute | solution.py:159
  41.6 8.8 %collective-permute-done.3.refs_1_ = bf16[104,1024]{1,0:T(8,128)(2,1)} collective-permute-done((bf16[104,1024]{1,0:T(8,128)(2,1)}, bf16[104,1024]{1,0:T(8,128)(2,1)}, u32[]{:S(2)}, u32[]{:S(2)}) %collective-permute-start.3) | collective-permute-done | bytes 213024 | tf_op jit(solution)/shard_map/ppermute | solution.py:159
  54.4 5.1 %collective-permute-start.11 = (bf16[64,2048]{1,0:T(8,128)(2,1)}, bf16[64,2048]{1,0:T(8,128)(2,1)}, u32[]{:S(2)}, u32[]{:S(2)}) collective-permute-start(bf16[64,2048]{1,0:T(8,128)(2,1)} %tie.18), channel_id=1, source_target_pairs={{0,24},{2,26},{4,28},{6,30},{8,0},{10,2},{12,4},{14,6},{16,8},{18,... | collective-permute-start | bytes 786440 | tf_op jit(solution)/shard_map/ppermute | solution.py:69
  71.8 11.3 %collective-permute-done.10.refs_2_ = bf16[64,2048]{1,0:T(8,128)(2,1)} collective-permute-done((bf16[64,2048]{1,0:T(8,128)(2,1)}, bf16[64,2048]{1,0:T(8,128)(2,1)}, u32[]{:S(2)}, u32[]{:S(2)}) %collective-permute-start.10) | collective-permute-done | bytes 262176 | tf_op jit(solution)/shard_map/ppermute | solution.py:69
  92.5 9.7 %project.1 = (bf16[1280,1536]{1,0:T(8,128)(2,1)S(1)}, bf16[1024,1280]{1,0:T(8,128)(2,1)S(1)}, bf16[1024,1664]{1,0:T(8,128)(2,1)S(1)}, f32[8,1024]{1,0:T(8,128)S(1)}) custom-call(s32[1]{0:T(128)} %bitcast.9.me, f32[1280,1024]{1,0:T(8,128)} %copy-done.1, bf16[4,64,1664]{2,1,0:T(8,128)(2,1)} %pad_maximum_fusion.1.refs_0_, bf16[4,64,1664]{2,1,0:T(8,128)(2,1)S(1)} %copy-done.18, ...), custom_call_target="tpu_custom_call" | custom-call | flops 4026531840 | bytes 20971520 | tf_op jit(solution)/shard_map/project/pallas_call | solution.py:724
  102.4 19.0 %attend.2 = (bf16[1280,512]{1,0:T(8,128)(2,1)S(1)}, bf16[8,5,1280,256]{3,2,1,0:T(8,128)(2,1)}, f32[8,1,1280]{2,1,0:T(1,128)S(1)}) custom-call(f32[48,8]{1,0:T(8,128)S(1)} %convert_element_type.120.table, bf16[1280,1536]{1,0:T(8,128)(2,1)S(1)} %get-tuple-element.54.q_ref.k_ref.v_ref, bf16[1280,1536]{1,0:T(8,128)(2,1)S(1)} %get-tuple-element.54.q_ref.k_ref.v_ref, ...), custom_call_target="tpu_custom_call" | custom-call | flops 80530636800 | bytes 13107200 | tf_op jit(solution)/shard_map/attend/pallas_call | solution.py:259
  125.5 19.2 %attend.3 = (bf16[1280,512]{1,0:T(8,128)(2,1)S(1)}, bf16[8,5,1280,256]{3,2,1,0:T(8,128)(2,1)}, f32[8,1,1280]{2,1,0:T(1,128)S(1)}) custom-call(f32[48,8]{1,0:T(8,128)S(1)} %convert_element_type.120.table, bf16[1280,1536]{1,0:T(8,128)(2,1)S(1)} %get-tuple-element.54.q_ref.k_ref.v_ref, ...), custom_call_target="tpu_custom_call", output_to_operand_aliasing={{0}: (6, {}), {1}: (7, {}), {2}: (8, {})} | custom-call | flops 80530636800 | bytes 13107200 | tf_op jit(solution)/shard_map/attend/pallas_call | solution.py:259
  144.9 3.9 %mix_out.1 = (bf16[1280,1024]{1,0:T(8,128)(2,1)S(1)}, bf16[1024,512]{1,0:T(8,128)(2,1)S(1)}) custom-call(s32[1]{0:T(128)} %bitcast.9.me, bf16[1280,512]{1,0:T(8,128)(2,1)S(1)} %get-tuple-element.58.mixture_from.mixture.mix_ref, bf16[4,64,2048]{2,1,0:T(8,128)(2,1)S(1)} %copy-done.7, bf16[4,64,2048]{2,1,0:T(8,128)(2,1)S(1)} %collective-permute-done.12.refs_3_.refs_1_, ...), custom_call_target="tpu_custom_call" | custom-call | flops 1342177280 | bytes 5242880 | tf_op jit(solution)/shard_map/mix_out/pallas_call | solution.py:776
  159.5 20.0 %ffn_first.1 = (bf16[1280,1024]{1,0:T(8,128)(2,1)}, bf16[1280,1024]{1,0:T(8,128)(2,1)}, bf16[1024,1536]{1,0:T(8,128)(2,1)}) custom-call(s32[1]{0:T(128)} %bitcast.9.me, bf16[1280,1024]{1,0:T(8,128)(2,1)} %copy-done.40, bf16[1280,1024]{1,0:T(8,128)(2,1)} %copy-done.6, bf16[4,64,2048]{2,1,0:T(8,128)(2,1)} %tie.19.refs_0_, bf16[4,64,2048]{2,1,0:T(8,128)(2,1)} %copy-done.14, ...), custom_call_target="tpu_custom_call" | custom-call | flops 12079595520 | bytes 16777216 | tf_op jit(solution)/shard_map/ffn_first/pallas_call | solution.py:607
  179.7 4.6 %all-gather.2.cloned.1.call-done.refs_0_ = bf16[1024,2688]{1,0:T(8,128)(2,1)} async-done(((bf16[64,2688]{1,0:T(8,128)(2,1)}), bf16[1024,2688]{1,0:T(8,128)(2,1)}) %all-gather.2.cloned.1.call-update) | async-done | bytes 5505040 | tf_op jit(solution)/shard_map/all_gather | solution.py:1015
  184.3 34.1 %ffn_last.1 = (bf16[1280,1024]{1,0:T(8,128)(2,1)}, bf16[1280,1024]{1,0:T(8,128)(2,1)}, bf16[1024,2688]{1,0:T(8,128)(2,1)}) custom-call(s32[1]{0:T(128)} %bitcast.9.me, bf16[1280,1024]{1,0:T(8,128)(2,1)} %copy-done.40, bf16[1280,1024]{1,0:T(8,128)(2,1)} %copy-done.6, bf16[1024,2688]{1,0:T(8,128)(2,1)} %all-gather.2.cloned.1.call-done.refs_0_, ...), custom_call_target="tpu_custom_call" | custom-call | flops 21139292160 | bytes 21495808 | tf_op jit(solution)/shard_map/ffn_last/pallas_call | solution.py:607
  220.2 4.9 %collective-permute-done.19.other = bf16[1280,1024]{1,0:T(8,128)(2,1)S(1)} collective-permute-done((bf16[1280,1024]{1,0:T(8,128)(2,1)S(1)}, bf16[1280,1024]{1,0:T(8,128)(2,1)S(1)}, u32[]{:S(2)}, u32[]{:S(2)}) %collective-permute-start.19) | collective-permute-done | bytes 2621472 | tf_op jit(solution)/shard_map/ppermute | solution.py:150
  226.6 11.5 %after_ffn.1 = (bf16[1280,1024]{1,0:T(8,128)(2,1)}, bf16[1280,512]{1,0:T(8,128)(2,1)}, bf16[1024,512]{1,0:T(8,128)(2,1)}) custom-call(f32[1280,1024]{1,0:T(8,128)} %copy-done.3, bf16[1280,1024]{1,0:T(8,128)(2,1)} %get-tuple-element.66.own, bf16[1280,1024]{1,0:T(8,128)(2,1)} %copy-done.44, bf16[1280,1024]{1,0:T(8,128)(2,1)} %copy-done.6, ...), custom_call_target="tpu_custom_call" | custom-call | flops 2684354560 | bytes 26214400 | tf_op jit(solution)/shard_map/after_ffn/pallas_call | solution.py:648
  238.3 4.0 %all-to-all-start = ((bf16[4,64,1536]{2,1,0:T(8,128)(2,1)}), bf16[4,64,1536]{2,1,0:T(8,128)(2,1)S(1)}, u32[]{:S(2)}, u32[]{:S(2)}) async-start(bf16[4,64,1536]{2,1,0:T(8,128)(2,1)} %bitcast.67), calls=%async_computation.1 | async-start | bytes 1572864 | tf_op jit(solution)/shard_map/all_to_all | solution.py:91
  244.2 30.8 %heads_back.2 = (bf16[1280,1024]{1,0:T(8,128)(2,1)}, bf16[4,256,1280]{2,1,0:T(8,128)(2,1)}, f32[16,128]{1,0:T(8,128)}) custom-call(bf16[1280,1536]{1,0:T(8,128)(2,1)} %copy-done, bf16[1280,1536]{1,0:T(8,128)(2,1)} %copy-done, bf16[1280,1536]{1,0:T(8,128)(2,1)} %copy-done, bf16[1280,512]{1,0:T(8,128)(2,1)} %get-tuple-element.68.refs_1_.gm_ref, ...), custom_call_target="tpu_custom_call" | custom-call | flops 4697620480 | bytes 6553600 | tf_op jit(solution)/shard_map/heads_back/pallas_call | solution.py:482
  277.4 9.0 %result.1 = (bf16[1024,1024]{1,0:T(8,128)(2,1)}, bf16[208,1024]{1,0:T(8,128)(2,1)}) custom-call(s32[1]{0:T(128)} %dynamic_slice.49.count, f32[1280,1024]{1,0:T(8,128)} %copy-done.3, bf16[1280,1024]{1,0:T(8,128)(2,1)} %tie.22.own, bf16[1280,1024]{1,0:T(8,128)(2,1)} %copy-done.42, bf16[1280,208]{1,0:T(8,128)(2,1)} %copy-done.9, ...), custom_call_target="tpu_custom_call" | custom-call | flops 545259520 | bytes 26214400 | tf_op jit(solution)/shard_map/result/pallas_call | solution.py:648
  286.5 3.7 all-to-all-start.1
  290.9 30.4 %heads_back.3 = (bf16[1280,1024]{1,0:T(8,128)(2,1)}, bf16[4,272,768]{2,1,0:T(8,128)(2,1)}, f32[16,128]{1,0:T(8,128)}) custom-call(bf16[1280,1536]{1,0:T(8,128)(2,1)} %copy-done, bf16[1280,1536]{1,0:T(8,128)(2,1)} %copy-done, bf16[1280,1536]{1,0:T(8,128)(2,1)} %copy-done, bf16[1280,512]{1,0:T(8,128)(2,1)} %get-tuple-element.68.refs_1_.gm_ref, ...), custom_call_target="tpu_custom_call" | custom-call | flops 4697620480 | bytes 6553600 | tf_op jit(solution)/shard_map/heads_back/pallas_call | solution.py:482
  328.7 2.9 collective-permute-start.21
  331.6 10.5 %last.1 = (bf16[1024,1024]{1,0:T(8,128)(2,1)}, bf16[208,1024]{1,0:T(8,128)(2,1)}) custom-call(s32[1]{0:T(128)} %dynamic_slice.49.count, f32[1280,1024]{1,0:T(8,128)} %copy-done.1, bf16[1280,1024]{1,0:T(8,128)(2,1)} %get-tuple-element.81.own.refs_1_, bf16[1280,1024]{1,0:T(8,128)(2,1)} %collective-permute-done.22.other, ...), custom_call_target="tpu_custom_call" | custom-call | flops 1090519040 | bytes 26214400 | tf_op jit(solution)/shard_map/last/pallas_call | solution.py:648
  342.1 3.4 collective-permute-done.21.refs_2_.refs_0_
  350.6 5.2 %collective-permute-start.28 = (bf16[80,768]{1,0:T(8,128)(2,1)S(1)}, bf16[80,768]{1,0:T(8,128)(2,1)S(1)}, u32[]{:S(2)}, u32[]{:S(2)}) collective-permute-start(bf16[80,768]{1,0:T(8,128)(2,1)S(1)} %get-tuple-element.103), channel_id=1, source_target_pairs={{0,24},{8,16},{16,8},{24,0},{2,26},{10,18},{18,10},{26,2},{4,28},{... | collective-permute-start | bytes 368648 | tf_op jit(solution)/shard_map/ppermute | solution.py:107
  360.1 10.3 %collective-permute-done.27 = bf16[80,768]{1,0:T(8,128)(2,1)S(1)} collective-permute-done((bf16[80,768]{1,0:T(8,128)(2,1)S(1)}, bf16[80,768]{1,0:T(8,128)(2,1)S(1)}, u32[]{:S(2)}, u32[]{:S(2)}) %collective-permute-start.27) | collective-permute-done | bytes 122912 | tf_op jit(solution)/shard_map/ppermute | solution.py:107
  (318 shorter events, 101.7 us)
Async XLA Ops:
  8.0 176.3 %all-gather.2.cloned.1.call-start = ((), (), s32[]{:S(2)}) async-start(), calls=%async_computation.6 | async-start | bytes 5849088 | tf_op jit(solution)/shard_map/all_gather | solution.py:1015
  31.3 21.0 %collective-permute-start.5 = (bf16[4,64,1664]{2,1,0:T(8,128)(2,1)}, bf16[4,64,1664]{2,1,0:T(8,128)(2,1)S(1)}, u32[]{:S(2)}, u32[]{:S(2)}) collective-permute-start(bf16[4,64,1664]{2,1,0:T(8,128)(2,1)} %pad_maximum_fusion.1.refs_0_), channel_id=1, source_target_pairs={{0,2},{2,0},{4,6},{6,4},{8,10},{10,8},{12,14},{14,12},{16,18},{18,... | collective-permute-start | bytes 2555912 | tf_op jit(solution)/shard_map/ppermute | solution.py:69
  32.8 20.7 %collective-permute-start.6 = (bf16[4,64,1664]{2,1,0:T(8,128)(2,1)}, bf16[4,64,1664]{2,1,0:T(8,128)(2,1)S(1)}, u32[]{:S(2)}, u32[]{:S(2)}) collective-permute-start(bf16[4,64,1664]{2,1,0:T(8,128)(2,1)} %pad_maximum_fusion.1.refs_0_), channel_id=1, source_target_pairs={{0,4},{2,6},{4,0},{6,2},{8,12},{10,14},{12,8},{14,10},{16,20},{18,... | collective-permute-start | bytes 2555912 | tf_op jit(solution)/shard_map/ppermute | solution.py:69
  59.5 23.6 %collective-permute-start.10 = (bf16[64,2048]{1,0:T(8,128)(2,1)}, bf16[64,2048]{1,0:T(8,128)(2,1)}, u32[]{:S(2)}, u32[]{:S(2)}) collective-permute-start(bf16[64,2048]{1,0:T(8,128)(2,1)} %tie.18), channel_id=1, source_target_pairs={{0,16},{2,18},{4,20},{6,22},{8,24},{10,26},{12,28},{14,30},{16,0},... | collective-permute-start | bytes 786440 | tf_op jit(solution)/shard_map/ppermute | solution.py:69
  60.9 22.2 %collective-permute-start.9 = (bf16[64,2048]{1,0:T(8,128)(2,1)}, bf16[64,2048]{1,0:T(8,128)(2,1)}, u32[]{:S(2)}, u32[]{:S(2)}) collective-permute-start(bf16[64,2048]{1,0:T(8,128)(2,1)} %tie.18), channel_id=1, source_target_pairs={{0,8},{2,10},{4,12},{6,14},{8,16},{10,18},{12,20},{14,22},{16,24},... | collective-permute-start | bytes 786440 | tf_op jit(solution)/shard_map/ppermute | solution.py:69
  62.7 23.4 %collective-permute-start.7 = (bf16[4,32,1664]{2,1,0:T(8,128)(2,1)}, bf16[4,32,1664]{2,1,0:T(8,128)(2,1)S(1)}, u32[]{:S(2)}, u32[]{:S(2)}) collective-permute-start(bf16[4,32,1664]{2,1,0:T(8,128)(2,1)} %tie.17), channel_id=1, source_target_pairs={{0,2},{2,0},{4,6},{6,4},{8,10},{10,8},{12,14},{14,12},{16,18},{18,... | collective-permute-start | bytes 1277960 | tf_op jit(solution)/shard_map/ppermute | solution.py:69
  64.7 21.4 %collective-permute-start.8 = (bf16[4,32,1664]{2,1,0:T(8,128)(2,1)}, bf16[4,32,1664]{2,1,0:T(8,128)(2,1)S(1)}, u32[]{:S(2)}, u32[]{:S(2)}) collective-permute-start(bf16[4,32,1664]{2,1,0:T(8,128)(2,1)} %slice.178), channel_id=1, source_target_pairs={{0,4},{2,6},{4,0},{6,2},{8,12},{10,14},{12,8},{14,10},{16,20},{18,... | collective-permute-start | bytes 1277960 | tf_op jit(solution)/shard_map/ppermute | solution.py:69
  83.1 19.2 %collective-permute-start.14 = (bf16[104,1024]{1,0:T(8,128)(2,1)}, bf16[104,1024]{1,0:T(8,128)(2,1)}, u32[]{:S(2)}, u32[]{:S(2)}) collective-permute-start(bf16[104,1024]{1,0:T(8,128)(2,1)} %tie.20), channel_id=1, source_target_pairs={{0,16},{2,18},{4,20},{6,22},{8,24},{10,26},{12,28},{14,30},{16,0},... | collective-permute-start | bytes 638984 | tf_op jit(solution)/shard_map/ppermute | solution.py:159
  87.6 36.9 %collective-permute-start.12 = (bf16[4,64,2048]{2,1,0:T(8,128)(2,1)}, bf16[4,64,2048]{2,1,0:T(8,128)(2,1)S(1)}, u32[]{:S(2)}, u32[]{:S(2)}) collective-permute-start(bf16[4,64,2048]{2,1,0:T(8,128)(2,1)} %tie.19.refs_0_), channel_id=1, source_target_pairs={{0,2},{2,0},{4,6},{6,4},{8,10},{10,8},{12,14},{14,12},{16,18},{18,... | collective-permute-start | bytes 3145736 | tf_op jit(solution)/shard_map/ppermute | solution.py:69
  88.7 33.9 %collective-permute-start.13 = (bf16[4,64,2048]{2,1,0:T(8,128)(2,1)}, bf16[4,64,2048]{2,1,0:T(8,128)(2,1)}, u32[]{:S(2)}, u32[]{:S(2)}) collective-permute-start(bf16[4,64,2048]{2,1,0:T(8,128)(2,1)} %tie.19.refs_0_), channel_id=1, source_target_pairs={{0,4},{2,6},{4,0},{6,2},{8,12},{10,14},{12,8},{14,10},{16,20},{18,... | collective-permute-start | bytes 3145736 | tf_op jit(solution)/shard_map/ppermute | solution.py:69
  90.3 148.0 %reduce-scatter.5.cloned.1.call-start = ((), (), s32[]{:S(2)}) async-start(), calls=%async_computation.7 | async-start | bytes 3932160 | tf_op jit(solution)/shard_map/reduce_scatter | solution.py:1037
  102.3 19.1 %collective-permute-start.15 = (bf16[104,1024]{1,0:T(8,128)(2,1)}, bf16[104,1024]{1,0:T(8,128)(2,1)S(1)}, u32[]{:S(2)}, u32[]{:S(2)}) collective-permute-start(bf16[104,1024]{1,0:T(8,128)(2,1)} %collective-permute-done.14), channel_id=1, source_target_pairs={{0,1},{1,0},{2,3},{3,2},{4,5},{5,4},{6,7},{7,6},{8,9},{9,8},{10,11... | collective-permute-start | bytes 638984 | tf_op jit(solution)/shard_map/ppermute | solution.py:150
  123.9 20.9 %collective-permute-start.16 = (bf16[4,32,2048]{2,1,0:T(8,128)(2,1)S(1)}, bf16[4,32,2048]{2,1,0:T(8,128)(2,1)S(1)}, u32[]{:S(2)}, u32[]{:S(2)}) collective-permute-start(bf16[4,32,2048]{2,1,0:T(8,128)(2,1)S(1)} %slice.179), channel_id=1, source_target_pairs={{0,2},{2,0},{4,6},{6,4},{8,10},{10,8},{12,14},{14,12},{16,18},{18,... | collective-permute-start | bytes 1572872 | tf_op jit(solution)/shard_map/ppermute | solution.py:69
  124.6 20.2 %collective-permute-start.17 = (bf16[4,32,2048]{2,1,0:T(8,128)(2,1)S(1)}, bf16[4,32,2048]{2,1,0:T(8,128)(2,1)S(1)}, u32[]{:S(2)}, u32[]{:S(2)}) collective-permute-start(bf16[4,32,2048]{2,1,0:T(8,128)(2,1)S(1)} %slice.180), channel_id=1, source_target_pairs={{0,4},{2,6},{4,0},{6,2},{8,12},{10,14},{12,8},{14,10},{16,20},{18,... | collective-permute-start | bytes 1572872 | tf_op jit(solution)/shard_map/ppermute | solution.py:69
  179.5 110.7 %reduce-scatter.7.cloned.1.call-start = ((), (), s32[]{:S(2)}) async-start(), calls=%async_computation.8 | async-start | bytes 6881280 | tf_op jit(solution)/shard_map/reduce_scatter | solution.py:1037
  238.2 37.8 %collective-permute-start.20 = (bf16[1280,1024]{1,0:T(8,128)(2,1)}, bf16[1280,1024]{1,0:T(8,128)(2,1)S(1)}, u32[]{:S(2)}, u32[]{:S(2)}) collective-permute-start(bf16[1280,1024]{1,0:T(8,128)(2,1)} %tie.22.own), channel_id=1, source_target_pairs={{0,1},{1,0},{2,3},{3,2},{4,5},{5,4},{6,7},{7,6},{8,9},{9,8},{10,11... | collective-permute-start | bytes 7864328 | tf_op jit(solution)/shard_map/ppermute | solution.py:150
  238.3 36.7 %all-to-all-start = ((bf16[4,64,1536]{2,1,0:T(8,128)(2,1)}), bf16[4,64,1536]{2,1,0:T(8,128)(2,1)S(1)}, u32[]{:S(2)}, u32[]{:S(2)}) async-start(bf16[4,64,1536]{2,1,0:T(8,128)(2,1)} %bitcast.67), calls=%async_computation.1 | async-start | bytes 1572864 | tf_op jit(solution)/shard_map/all_to_all | solution.py:91
  286.5 35.1 %all-to-all-start.1 = ((bf16[4,256,1280]{2,1,0:T(8,128)(2,1)}), bf16[4,256,1280]{2,1,0:T(8,128)(2,1)S(1)}, u32[]{:S(2)}, u32[]{:S(2)}) async-start(bf16[4,256,1280]{2,1,0:T(8,128)(2,1)} %bitcast.66), calls=%async_computation.2 | async-start | bytes 5242880 | tf_op jit(solution)/shard_map/all_to_all | solution.py:91
  290.1 59.4 %reduce-scatter.9.cloned.1.call-start = ((), (), s32[]{:S(2)}) async-start(), calls=%async_computation.9 | async-start | bytes 1720320 | tf_op jit(solution)/shard_map/reduce_scatter | solution.py:1037
  290.9 84.1 %reduce-scatter.11.cloned.1.call-start = ((), (), s32[]{:S(2)}) async-start(), calls=%async_computation.10 | async-start | bytes 819200 | tf_op jit(solution)/shard_map/reduce_scatter | solution.py:1037
  325.2 21.1 %collective-permute-start.25 = (bf16[272,768]{1,0:T(8,128)(2,1)S(1)}, bf16[272,768]{1,0:T(8,128)(2,1)S(1)}, u32[]{:S(2)}, u32[]{:S(2)}) collective-permute-start(bf16[272,768]{1,0:T(8,128)(2,1)S(1)} %get-tuple-element.99), channel_id=1, source_target_pairs={{0,6},{2,4},{4,2},{6,0},{8,14},{10,12},{12,10},{14,8},{16,22},{18,... | collective-permute-start | bytes 1253384 | tf_op jit(solution)/shard_map/ppermute | solution.py:107
  327.9 19.2 %collective-permute-start.24 = (bf16[272,768]{1,0:T(8,128)(2,1)S(1)}, bf16[272,768]{1,0:T(8,128)(2,1)S(1)}, u32[]{:S(2)}, u32[]{:S(2)}) collective-permute-start(bf16[272,768]{1,0:T(8,128)(2,1)S(1)} %get-tuple-element.100), channel_id=1, source_target_pairs={{0,4},{2,6},{4,0},{6,2},{8,12},{10,14},{12,8},{14,10},{16,20},{18,... | collective-permute-start | bytes 1253384 | tf_op jit(solution)/shard_map/ppermute | solution.py:107
  328.4 19.0 %collective-permute-start.23 = (bf16[272,768]{1,0:T(8,128)(2,1)S(1)}, bf16[272,768]{1,0:T(8,128)(2,1)S(1)}, u32[]{:S(2)}, u32[]{:S(2)}) collective-permute-start(bf16[272,768]{1,0:T(8,128)(2,1)S(1)} %get-tuple-element.101), channel_id=1, source_target_pairs={{0,2},{2,0},{4,6},{6,4},{8,10},{10,8},{12,14},{14,12},{16,18},{18,... | collective-permute-start | bytes 1253384 | tf_op jit(solution)/shard_map/ppermute | solution.py:107
  356.7 17.6 %collective-permute-start.30 = (bf16[104,1024]{1,0:T(8,128)(2,1)S(1)}, bf16[104,1024]{1,0:T(8,128)(2,1)S(1)}, u32[]{:S(2)}, u32[]{:S(2)}) collective-permute-start(bf16[104,1024]{1,0:T(8,128)(2,1)S(1)} %constant_dynamic-slice_fusion), channel_id=1, source_target_pairs={{0,16},{2,18},{4,20},{6,22},{8,24},{10,26},{12,28},{14,30},{16,0},... | collective-permute-start | bytes 638984 | tf_op jit(solution)/shard_map/ppermute | solution.py:159
  (93 other events, 1021.4 us)
Sparse Core Ops, SparseCore 0:
  90.4 93.8 all-gather.1
  293.3 34.1 reduce-scatter.8
  331.7 23.7 reduce-scatter.10
Sparse Core Ops, SparseCore 1:
  179.6 43.6 reduce-scatter.4
  226.2 63.4 reduce-scatter.6

commit v5 on v4

--- a/solution.py
+++ b/solution.py
@@ -1007,13 +1007,14 @@
     )
     sent = sent or [send_half(patch_in[0, :live_slots])]
     patches = join_halves(sent[0])
+    heard = planes
     first_set, layers, planes, _ = chips.gather_rows(
         jnp.concatenate([wo_t, w_gate[:, :cut], w_up[:, :cut], w_down_t[:, :cut]], axis=1),
         planes, corners,
     )
     patch_cot = join_halves(send_half(cot_patch[0, :live_slots], layers))
     last_set = lax.all_gather(
-        tie(jnp.concatenate([w_gate[:, cut:], w_up[:, cut:], w_down_t[:, cut:]], axis=1), *corners),
+        tie(jnp.concatenate([w_gate[:, cut:], w_up[:, cut:], w_down_t[:, cut:]], axis=1), *heard),
         "dp", axis=0, tiled=True,
     )
     rows = embed(count, text_in[0], spread, patches)

time: 396 us -> 392 us (0.990)
    all_gather x1, waiting for transfers between devices: 4.55 us -> 0.02 us  [body(): lax.all_gather(tie(jnp.concatenate([w_gate[:, cut:], w_up[:, cut:], w_dow...]
    unnamed x141 -> x143, local copies, waits for them, and re-layouts: 20.3 us -> 18.9 us
  transfers between devices with their start and end apart: 40 -> 40, of which waited for: 14 -> 13; matrix products, arithmetic and copies ran while one was open for 9% -> 9% of each run, Pallas kernels for 53% -> 53%
where the time goes in v5:
time: 392 us; the launch traced here: 385 us
  Pallas kernels  205 us (52%)
  starting transfers between devices  52.8 us (13%)
  waiting for transfers between devices  52.1 us (13%)
  local copies, waits for them, and re-layouts  33.1 us (8%)
  other arithmetic  24.5 us (6%)
  between operations  17.6 us (4%)
    pallas_call x2, Pallas kernels, heads_back(): pl.pallas_call(functools.partial(heads_back_kernel, order, first, starts)...  61.4 us
    pallas_call x2, Pallas kernels, ffn(): pl.pallas_call(functools.partial(ffn_kernel, first, len(parts), extra, ba...  54.2 us
    pallas_call x2, Pallas kernels, attend(): pl.pallas_call(functools.partial(attend_kernel, first, extra), grid=(pair...  38.2 us
    pallas_call x6, Pallas kernels, row_call(): pl.pallas_call(kernel, grid=(rows // BQ,), in_specs=in_specs, out_specs=o...  37.2 us
    ppermute x14, starting transfers between devices, send(): return lax.ppermute(block, 'dp', route)  25 us
    unnamed x143, local copies, waits for them, and re-layouts  18.9 us
    ppermute x4, waiting for transfers between devices, send_half(): return lax.ppermute(mine, 'dp', route)  18.2 us
    ppermute x14, waiting for transfers between devices, send(): return lax.ppermute(block, 'dp', route)  15.1 us
  transfers between devices with their start and end apart: 40, of which 13 were waited for; matrix products, arithmetic and copies ran while one was open for 9% of the time, Pallas kernels for 53%

profile of v5, /device:TPU:0, one launch (start us, length us, event | category | flops | bytes accessed | tf_op | source)
XLA Modules:
  0.0 384.8 jit_solution(12603350972147410750)
XLA Ops:
  10.4 3.1 collective-permute-start
  13.5 2.6 collective-permute-start.1
  37.2 3.9 %collective-permute-start.3 = (bf16[104,1024]{1,0:T(8,128)(2,1)}, bf16[104,1024]{1,0:T(8,128)(2,1)}, u32[]{:S(2)}, u32[]{:S(2)}) collective-permute-start(bf16[104,1024]{1,0:T(8,128)(2,1)} %tie.16), channel_id=1, source_target_pairs={{0,16},{2,18},{4,20},{6,22},{8,24},{10,26},{12,28},{14,30},{16,0},... | collective-permute-start | bytes 638984 | tf_op jit(solution)/shard_map/ppermute | solution.py:159
  42.1 8.8 %collective-permute-done.3.refs_1_ = bf16[104,1024]{1,0:T(8,128)(2,1)} collective-permute-done((bf16[104,1024]{1,0:T(8,128)(2,1)}, bf16[104,1024]{1,0:T(8,128)(2,1)}, u32[]{:S(2)}, u32[]{:S(2)}) %collective-permute-start.3) | collective-permute-done | bytes 213024 | tf_op jit(solution)/shard_map/ppermute | solution.py:159
  55.0 5.1 %collective-permute-start.11 = (bf16[64,2048]{1,0:T(8,128)(2,1)}, bf16[64,2048]{1,0:T(8,128)(2,1)}, u32[]{:S(2)}, u32[]{:S(2)}) collective-permute-start(bf16[64,2048]{1,0:T(8,128)(2,1)} %tie.18), channel_id=1, source_target_pairs={{0,24},{2,26},{4,28},{6,30},{8,0},{10,2},{12,4},{14,6},{16,8},{18,... | collective-permute-start | bytes 786440 | tf_op jit(solution)/shard_map/ppermute | solution.py:69
  72.5 11.2 %collective-permute-done.10.refs_2_ = bf16[64,2048]{1,0:T(8,128)(2,1)} collective-permute-done((bf16[64,2048]{1,0:T(8,128)(2,1)}, bf16[64,2048]{1,0:T(8,128)(2,1)}, u32[]{:S(2)}, u32[]{:S(2)}) %collective-permute-start.10) | collective-permute-done | bytes 262176 | tf_op jit(solution)/shard_map/ppermute | solution.py:69
  91.1 10.0 %project.1 = (bf16[1280,1536]{1,0:T(8,128)(2,1)S(1)}, bf16[1024,1280]{1,0:T(8,128)(2,1)S(1)}, bf16[1024,1664]{1,0:T(8,128)(2,1)S(1)}, f32[8,1024]{1,0:T(8,128)S(1)}) custom-call(s32[1]{0:T(128)} %bitcast.9.me, f32[1280,1024]{1,0:T(8,128)} %copy-done.1, bf16[4,64,1664]{2,1,0:T(8,128)(2,1)} %pad_maximum_fusion.1.refs_0_, bf16[4,64,1664]{2,1,0:T(8,128)(2,1)S(1)} %copy-done.13, ...), custom_call_target="tpu_custom_call" | custom-call | flops 4026531840 | bytes 20971520 | tf_op jit(solution)/shard_map/project/pallas_call | solution.py:724
  101.5 19.0 %attend.2 = (bf16[1280,512]{1,0:T(8,128)(2,1)S(1)}, bf16[8,5,1280,256]{3,2,1,0:T(8,128)(2,1)}, f32[8,1,1280]{2,1,0:T(1,128)S(1)}) custom-call(f32[48,8]{1,0:T(8,128)S(1)} %convert_element_type.120.table, bf16[1280,1536]{1,0:T(8,128)(2,1)S(1)} %get-tuple-element.54.q_ref.k_ref.v_ref, bf16[1280,1536]{1,0:T(8,128)(2,1)S(1)} %get-tuple-element.54.q_ref.k_ref.v_ref, ...), custom_call_target="tpu_custom_call" | custom-call | flops 80530636800 | bytes 13107200 | tf_op jit(solution)/shard_map/attend/pallas_call | solution.py:259
  124.9 19.2 %attend.3 = (bf16[1280,512]{1,0:T(8,128)(2,1)S(1)}, bf16[8,5,1280,256]{3,2,1,0:T(8,128)(2,1)}, f32[8,1,1280]{2,1,0:T(1,128)S(1)}) custom-call(f32[48,8]{1,0:T(8,128)S(1)} %convert_element_type.120.table, bf16[1280,1536]{1,0:T(8,128)(2,1)S(1)} %get-tuple-element.54.q_ref.k_ref.v_ref, ...), custom_call_target="tpu_custom_call", output_to_operand_aliasing={{0}: (6, {}), {1}: (7, {}), {2}: (8, {})} | custom-call | flops 80530636800 | bytes 13107200 | tf_op jit(solution)/shard_map/attend/pallas_call | solution.py:259
  144.2 2.7 mix_out.1
  157.5 20.0 %ffn_first.1 = (bf16[1280,1024]{1,0:T(8,128)(2,1)}, bf16[1280,1024]{1,0:T(8,128)(2,1)}, bf16[1024,1536]{1,0:T(8,128)(2,1)}) custom-call(s32[1]{0:T(128)} %bitcast.9.me, bf16[1280,1024]{1,0:T(8,128)(2,1)} %copy-done.40, bf16[1280,1024]{1,0:T(8,128)(2,1)} %copy-done.6, bf16[4,64,2048]{2,1,0:T(8,128)(2,1)} %tie.19.refs_0_, bf16[4,64,2048]{2,1,0:T(8,128)(2,1)} %copy-done.19, ...), custom_call_target="tpu_custom_call" | custom-call | flops 12079595520 | bytes 16777216 | tf_op jit(solution)/shard_map/ffn_first/pallas_call | solution.py:607
  177.9 34.2 %ffn_last.1 = (bf16[1280,1024]{1,0:T(8,128)(2,1)}, bf16[1280,1024]{1,0:T(8,128)(2,1)}, bf16[1024,2688]{1,0:T(8,128)(2,1)}) custom-call(s32[1]{0:T(128)} %bitcast.9.me, bf16[1280,1024]{1,0:T(8,128)(2,1)} %copy-done.40, bf16[1280,1024]{1,0:T(8,128)(2,1)} %copy-done.6, bf16[1024,2688]{1,0:T(8,128)(2,1)} %all-gather.2.cloned.1.call-done.refs_0_, ...), custom_call_target="tpu_custom_call" | custom-call | flops 21139292160 | bytes 21495808 | tf_op jit(solution)/shard_map/ffn_last/pallas_call | solution.py:607
  214.0 4.7 %collective-permute-done.19.other = bf16[1280,1024]{1,0:T(8,128)(2,1)S(1)} collective-permute-done((bf16[1280,1024]{1,0:T(8,128)(2,1)S(1)}, bf16[1280,1024]{1,0:T(8,128)(2,1)S(1)}, u32[]{:S(2)}, u32[]{:S(2)}) %collective-permute-start.19) | collective-permute-done | bytes 2621472 | tf_op jit(solution)/shard_map/ppermute | solution.py:150
  220.2 11.5 %after_ffn.1 = (bf16[1280,1024]{1,0:T(8,128)(2,1)}, bf16[1280,512]{1,0:T(8,128)(2,1)}, bf16[1024,512]{1,0:T(8,128)(2,1)}) custom-call(f32[1280,1024]{1,0:T(8,128)} %copy-done.3, bf16[1280,1024]{1,0:T(8,128)(2,1)} %get-tuple-element.66.own, bf16[1280,1024]{1,0:T(8,128)(2,1)} %copy-done.44, bf16[1280,1024]{1,0:T(8,128)(2,1)} %copy-done.6, ...), custom_call_target="tpu_custom_call" | custom-call | flops 2684354560 | bytes 26214400 | tf_op jit(solution)/shard_map/after_ffn/pallas_call | solution.py:648
  232.0 3.6 all-to-all-start
  237.5 30.9 %heads_back.2 = (bf16[1280,1024]{1,0:T(8,128)(2,1)}, bf16[4,256,1280]{2,1,0:T(8,128)(2,1)}, f32[16,128]{1,0:T(8,128)}) custom-call(bf16[1280,1536]{1,0:T(8,128)(2,1)} %copy-done, bf16[1280,1536]{1,0:T(8,128)(2,1)} %copy-done, bf16[1280,1536]{1,0:T(8,128)(2,1)} %copy-done, bf16[1280,512]{1,0:T(8,128)(2,1)} %get-tuple-element.68.refs_1_.gm_ref, ...), custom_call_target="tpu_custom_call" | custom-call | flops 4697620480 | bytes 6553600 | tf_op jit(solution)/shard_map/heads_back/pallas_call | solution.py:482
  270.8 9.0 %result.1 = (bf16[1024,1024]{1,0:T(8,128)(2,1)}, bf16[208,1024]{1,0:T(8,128)(2,1)}) custom-call(s32[1]{0:T(128)} %dynamic_slice.49.count, f32[1280,1024]{1,0:T(8,128)} %copy-done.3, bf16[1280,1024]{1,0:T(8,128)(2,1)} %tie.22.own, bf16[1280,1024]{1,0:T(8,128)(2,1)} %copy-done.42, bf16[1280,208]{1,0:T(8,128)(2,1)} %copy-done.9, ...), custom_call_target="tpu_custom_call" | custom-call | flops 545259520 | bytes 26214400 | tf_op jit(solution)/shard_map/result/pallas_call | solution.py:648
  279.8 3.7 all-to-all-start.1
  286.1 30.4 %heads_back.3 = (bf16[1280,1024]{1,0:T(8,128)(2,1)}, bf16[4,272,768]{2,1,0:T(8,128)(2,1)}, f32[16,128]{1,0:T(8,128)}) custom-call(bf16[1280,1536]{1,0:T(8,128)(2,1)} %copy-done, bf16[1280,1536]{1,0:T(8,128)(2,1)} %copy-done, bf16[1280,1536]{1,0:T(8,128)(2,1)} %copy-done, bf16[1280,512]{1,0:T(8,128)(2,1)} %get-tuple-element.68.refs_1_.gm_ref, ...), custom_call_target="tpu_custom_call" | custom-call | flops 4697620480 | bytes 6553600 | tf_op jit(solution)/shard_map/heads_back/pallas_call | solution.py:482
  326.2 10.5 %last.1 = (bf16[1024,1024]{1,0:T(8,128)(2,1)}, bf16[208,1024]{1,0:T(8,128)(2,1)}) custom-call(s32[1]{0:T(128)} %dynamic_slice.49.count, f32[1280,1024]{1,0:T(8,128)} %copy-done.1, bf16[1280,1024]{1,0:T(8,128)(2,1)} %get-tuple-element.81.own.refs_1_, bf16[1280,1024]{1,0:T(8,128)(2,1)} %collective-permute-done.22.other, ...), custom_call_target="tpu_custom_call" | custom-call | flops 1090519040 | bytes 26214400 | tf_op jit(solution)/shard_map/last/pallas_call | solution.py:648
  336.7 6.4 %collective-permute-done.21.refs_2_.refs_0_ = bf16[104,1024]{1,0:T(8,128)(2,1)S(1)} collective-permute-done((bf16[104,1024]{1,0:T(8,128)(2,1)S(1)}, bf16[104,1024]{1,0:T(8,128)(2,1)S(1)}, u32[]{:S(2)}, u32[]{:S(2)}) %collective-permute-start.21) | collective-permute-done | bytes 213024 | tf_op jit(solution)/shard_map/ppermute | solution.py:159
  347.0 5.4 %collective-permute-start.28 = (bf16[80,768]{1,0:T(8,128)(2,1)S(1)}, bf16[80,768]{1,0:T(8,128)(2,1)S(1)}, u32[]{:S(2)}, u32[]{:S(2)}) collective-permute-start(bf16[80,768]{1,0:T(8,128)(2,1)S(1)} %get-tuple-element.103), channel_id=1, source_target_pairs={{0,24},{8,16},{16,8},{24,0},{2,26},{10,18},{18,10},{26,2},{4,28},{... | collective-permute-start | bytes 368648 | tf_op jit(solution)/shard_map/ppermute | solution.py:107
  356.7 9.5 %collective-permute-done.27 = bf16[80,768]{1,0:T(8,128)(2,1)S(1)} collective-permute-done((bf16[80,768]{1,0:T(8,128)(2,1)S(1)}, bf16[80,768]{1,0:T(8,128)(2,1)S(1)}, u32[]{:S(2)}, u32[]{:S(2)}) %collective-permute-start.27) | collective-permute-done | bytes 122912 | tf_op jit(solution)/shard_map/ppermute | solution.py:107
  367.8 2.7 collective-permute-done.30.refs_0_
  (320 shorter events, 99.0 us)
Async XLA Ops:
  8.0 169.9 %all-gather.2.cloned.1.call-start = ((), (), s32[]{:S(2)}) async-start(), calls=%async_computation.6 | async-start | bytes 5849088 | tf_op jit(solution)/shard_map/all_gather | solution.py:1016
  31.8 21.0 %collective-permute-start.5 = (bf16[4,64,1664]{2,1,0:T(8,128)(2,1)}, bf16[4,64,1664]{2,1,0:T(8,128)(2,1)S(1)}, u32[]{:S(2)}, u32[]{:S(2)}) collective-permute-start(bf16[4,64,1664]{2,1,0:T(8,128)(2,1)} %pad_maximum_fusion.1.refs_0_), channel_id=1, source_target_pairs={{0,2},{2,0},{4,6},{6,4},{8,10},{10,8},{12,14},{14,12},{16,18},{18,... | collective-permute-start | bytes 2555912 | tf_op jit(solution)/shard_map/ppermute | solution.py:69
  33.3 20.7 %collective-permute-start.6 = (bf16[4,64,1664]{2,1,0:T(8,128)(2,1)}, bf16[4,64,1664]{2,1,0:T(8,128)(2,1)S(1)}, u32[]{:S(2)}, u32[]{:S(2)}) collective-permute-start(bf16[4,64,1664]{2,1,0:T(8,128)(2,1)} %pad_maximum_fusion.1.refs_0_), channel_id=1, source_target_pairs={{0,4},{2,6},{4,0},{6,2},{8,12},{10,14},{12,8},{14,10},{16,20},{18,... | collective-permute-start | bytes 2555912 | tf_op jit(solution)/shard_map/ppermute | solution.py:69
  60.1 23.7 %collective-permute-start.10 = (bf16[64,2048]{1,0:T(8,128)(2,1)}, bf16[64,2048]{1,0:T(8,128)(2,1)}, u32[]{:S(2)}, u32[]{:S(2)}) collective-permute-start(bf16[64,2048]{1,0:T(8,128)(2,1)} %tie.18), channel_id=1, source_target_pairs={{0,16},{2,18},{4,20},{6,22},{8,24},{10,26},{12,28},{14,30},{16,0},... | collective-permute-start | bytes 786440 | tf_op jit(solution)/shard_map/ppermute | solution.py:69
  61.5 22.3 %collective-permute-start.9 = (bf16[64,2048]{1,0:T(8,128)(2,1)}, bf16[64,2048]{1,0:T(8,128)(2,1)}, u32[]{:S(2)}, u32[]{:S(2)}) collective-permute-start(bf16[64,2048]{1,0:T(8,128)(2,1)} %tie.18), channel_id=1, source_target_pairs={{0,8},{2,10},{4,12},{6,14},{8,16},{10,18},{12,20},{14,22},{16,24},... | collective-permute-start | bytes 786440 | tf_op jit(solution)/shard_map/ppermute | solution.py:69
  63.3 23.5 %collective-permute-start.7 = (bf16[4,32,1664]{2,1,0:T(8,128)(2,1)}, bf16[4,32,1664]{2,1,0:T(8,128)(2,1)S(1)}, u32[]{:S(2)}, u32[]{:S(2)}) collective-permute-start(bf16[4,32,1664]{2,1,0:T(8,128)(2,1)} %tie.17), channel_id=1, source_target_pairs={{0,2},{2,0},{4,6},{6,4},{8,10},{10,8},{12,14},{14,12},{16,18},{18,... | collective-permute-start | bytes 1277960 | tf_op jit(solution)/shard_map/ppermute | solution.py:69
  65.3 21.5 %collective-permute-start.8 = (bf16[4,32,1664]{2,1,0:T(8,128)(2,1)}, bf16[4,32,1664]{2,1,0:T(8,128)(2,1)}, u32[]{:S(2)}, u32[]{:S(2)}) collective-permute-start(bf16[4,32,1664]{2,1,0:T(8,128)(2,1)} %slice.178), channel_id=1, source_target_pairs={{0,4},{2,6},{4,0},{6,2},{8,12},{10,14},{12,8},{14,10},{16,20},{18,... | collective-permute-start | bytes 1277960 | tf_op jit(solution)/shard_map/ppermute | solution.py:69
  72.5 159.5 %reduce-scatter.5.cloned.1.call-start = ((), (), s32[]{:S(2)}) async-start(), calls=%async_computation.7 | async-start | bytes 3932160 | tf_op jit(solution)/shard_map/reduce_scatter | solution.py:1038
  83.8 17.7 %collective-permute-start.14 = (bf16[104,1024]{1,0:T(8,128)(2,1)}, bf16[104,1024]{1,0:T(8,128)(2,1)S(1)}, u32[]{:S(2)}, u32[]{:S(2)}) collective-permute-start(bf16[104,1024]{1,0:T(8,128)(2,1)} %tie.20), channel_id=1, source_target_pairs={{0,16},{2,18},{4,20},{6,22},{8,24},{10,26},{12,28},{14,30},{16,0},... | collective-permute-start | bytes 638984 | tf_op jit(solution)/shard_map/ppermute | solution.py:159
  87.5 35.8 %collective-permute-start.12 = (bf16[4,64,2048]{2,1,0:T(8,128)(2,1)}, bf16[4,64,2048]{2,1,0:T(8,128)(2,1)S(1)}, u32[]{:S(2)}, u32[]{:S(2)}) collective-permute-start(bf16[4,64,2048]{2,1,0:T(8,128)(2,1)} %tie.19.refs_0_), channel_id=1, source_target_pairs={{0,2},{2,0},{4,6},{6,4},{8,10},{10,8},{12,14},{14,12},{16,18},{18,... | collective-permute-start | bytes 3145736 | tf_op jit(solution)/shard_map/ppermute | solution.py:69
  88.6 33.1 %collective-permute-start.13 = (bf16[4,64,2048]{2,1,0:T(8,128)(2,1)}, bf16[4,64,2048]{2,1,0:T(8,128)(2,1)S(1)}, u32[]{:S(2)}, u32[]{:S(2)}) collective-permute-start(bf16[4,64,2048]{2,1,0:T(8,128)(2,1)} %tie.19.refs_0_), channel_id=1, source_target_pairs={{0,4},{2,6},{4,0},{6,2},{8,12},{10,14},{12,8},{14,10},{16,20},{18,... | collective-permute-start | bytes 3145736 | tf_op jit(solution)/shard_map/ppermute | solution.py:69
  101.5 19.0 %collective-permute-start.15 = (bf16[104,1024]{1,0:T(8,128)(2,1)S(1)}, bf16[104,1024]{1,0:T(8,128)(2,1)S(1)}, u32[]{:S(2)}, u32[]{:S(2)}) collective-permute-start(bf16[104,1024]{1,0:T(8,128)(2,1)S(1)} %collective-permute-done.14), channel_id=1, source_target_pairs={{0,1},{1,0},{2,3},{3,2},{4,5},{5,4},{6,7},{7,6},{8,9},{9,8},{10,11... | collective-permute-start | bytes 638984 | tf_op jit(solution)/shard_map/ppermute | solution.py:150
  121.8 22.4 %collective-permute-start.16 = (bf16[4,32,2048]{2,1,0:T(8,128)(2,1)S(1)}, bf16[4,32,2048]{2,1,0:T(8,128)(2,1)S(1)}, u32[]{:S(2)}, u32[]{:S(2)}) collective-permute-start(bf16[4,32,2048]{2,1,0:T(8,128)(2,1)S(1)} %slice.179), channel_id=1, source_target_pairs={{0,2},{2,0},{4,6},{6,4},{8,10},{10,8},{12,14},{14,12},{16,18},{18,... | collective-permute-start | bytes 1572872 | tf_op jit(solution)/shard_map/ppermute | solution.py:69
  123.3 20.8 %collective-permute-start.17 = (bf16[4,32,2048]{2,1,0:T(8,128)(2,1)S(1)}, bf16[4,32,2048]{2,1,0:T(8,128)(2,1)S(1)}, u32[]{:S(2)}, u32[]{:S(2)}) collective-permute-start(bf16[4,32,2048]{2,1,0:T(8,128)(2,1)S(1)} %slice.180), channel_id=1, source_target_pairs={{0,4},{2,6},{4,0},{6,2},{8,12},{10,14},{12,8},{14,10},{16,20},{18,... | collective-permute-start | bytes 1572872 | tf_op jit(solution)/shard_map/ppermute | solution.py:69
  177.6 108.4 %reduce-scatter.7.cloned.1.call-start = ((), (), s32[]{:S(2)}) async-start(), calls=%async_computation.8 | async-start | bytes 6881280 | tf_op jit(solution)/shard_map/reduce_scatter | solution.py:1038
  231.8 37.5 %collective-permute-start.20 = (bf16[1280,1024]{1,0:T(8,128)(2,1)}, bf16[1280,1024]{1,0:T(8,128)(2,1)S(1)}, u32[]{:S(2)}, u32[]{:S(2)}) collective-permute-start(bf16[1280,1024]{1,0:T(8,128)(2,1)} %tie.22.own), channel_id=1, source_target_pairs={{0,1},{1,0},{2,3},{3,2},{4,5},{5,4},{6,7},{7,6},{8,9},{9,8},{10,11... | collective-permute-start | bytes 7864328 | tf_op jit(solution)/shard_map/ppermute | solution.py:150
  232.0 36.5 %all-to-all-start = ((bf16[4,64,1536]{2,1,0:T(8,128)(2,1)}), bf16[4,64,1536]{2,1,0:T(8,128)(2,1)S(1)}, u32[]{:S(2)}, u32[]{:S(2)}) async-start(bf16[4,64,1536]{2,1,0:T(8,128)(2,1)} %bitcast.67), calls=%async_computation.1 | async-start | bytes 1572864 | tf_op jit(solution)/shard_map/all_to_all | solution.py:91
  279.8 36.8 %all-to-all-start.1 = ((bf16[4,256,1280]{2,1,0:T(8,128)(2,1)}), bf16[4,256,1280]{2,1,0:T(8,128)(2,1)S(1)}, u32[]{:S(2)}, u32[]{:S(2)}) async-start(bf16[4,256,1280]{2,1,0:T(8,128)(2,1)} %bitcast.66), calls=%async_computation.2 | async-start | bytes 5242880 | tf_op jit(solution)/shard_map/all_to_all | solution.py:91
  283.5 62.4 %reduce-scatter.9.cloned.1.call-start = ((), (), s32[]{:S(2)}) async-start(), calls=%async_computation.9 | async-start | bytes 1720320 | tf_op jit(solution)/shard_map/reduce_scatter | solution.py:1038
  286.1 85.1 %reduce-scatter.11.cloned.1.call-start = ((), (), s32[]{:S(2)}) async-start(), calls=%async_computation.10 | async-start | bytes 819200 | tf_op jit(solution)/shard_map/reduce_scatter | solution.py:1038
  320.1 23.7 %collective-permute-start.25 = (bf16[272,768]{1,0:T(8,128)(2,1)S(1)}, bf16[272,768]{1,0:T(8,128)(2,1)S(1)}, u32[]{:S(2)}, u32[]{:S(2)}) collective-permute-start(bf16[272,768]{1,0:T(8,128)(2,1)S(1)} %get-tuple-element.99), channel_id=1, source_target_pairs={{0,6},{2,4},{4,2},{6,0},{8,14},{10,12},{12,10},{14,8},{16,22},{18,... | collective-permute-start | bytes 1253384 | tf_op jit(solution)/shard_map/ppermute | solution.py:107
  321.6 22.2 %collective-permute-start.24 = (bf16[272,768]{1,0:T(8,128)(2,1)S(1)}, bf16[272,768]{1,0:T(8,128)(2,1)S(1)}, u32[]{:S(2)}, u32[]{:S(2)}) collective-permute-start(bf16[272,768]{1,0:T(8,128)(2,1)S(1)} %get-tuple-element.100), channel_id=1, source_target_pairs={{0,4},{2,6},{4,0},{6,2},{8,12},{10,14},{12,8},{14,10},{16,20},{18,... | collective-permute-start | bytes 1253384 | tf_op jit(solution)/shard_map/ppermute | solution.py:107
  322.9 20.9 %collective-permute-start.23 = (bf16[272,768]{1,0:T(8,128)(2,1)S(1)}, bf16[272,768]{1,0:T(8,128)(2,1)S(1)}, u32[]{:S(2)}, u32[]{:S(2)}) collective-permute-start(bf16[272,768]{1,0:T(8,128)(2,1)S(1)} %get-tuple-element.101), channel_id=1, source_target_pairs={{0,2},{2,0},{4,6},{6,4},{8,10},{10,8},{12,14},{14,12},{16,18},{18,... | collective-permute-start | bytes 1253384 | tf_op jit(solution)/shard_map/ppermute | solution.py:107
  323.7 19.5 %collective-permute-start.21 = (bf16[104,1024]{1,0:T(8,128)(2,1)S(1)}, bf16[104,1024]{1,0:T(8,128)(2,1)S(1)}, u32[]{:S(2)}, u32[]{:S(2)}) collective-permute-start(bf16[104,1024]{1,0:T(8,128)(2,1)S(1)} %constant_dynamic-slice_fusion.1), channel_id=1, source_target_pairs={{0,16},{2,18},{4,20},{6,22},{8,24},{10,26},{12,28},{14,30},{16,0},... | collective-permute-start | bytes 638984 | tf_op jit(solution)/shard_map/ppermute | solution.py:159
  (94 other events, 1035.0 us)
Sparse Core Ops, SparseCore 0:
  72.6 97.3 all-gather.1
  286.7 34.0 reduce-scatter.8
  326.3 22.1 reduce-scatter.10
Sparse Core Ops, SparseCore 1:
  177.7 41.9 reduce-scatter.4
  222.6 63.4 reduce-scatter.6
